TPU v7x, 32 devices: a whole 2x2x4 slice. The times are simulated.
32 devices in a mesh: ctx: 8 (over y, x, core), tp: 4 (over z).
Axes of the slice: x: 2, y: 2, z: 4, core: 2. Of those that a mesh axis runs over, the one named last changes fastest.
Arguments:
- out_grad: bfloat16 [2048, 8192], P(('ctx', 'tp')), may hold values from -6 to 6
- saved_input: bfloat16 [2048, 8192], P(('ctx', 'tp')), may hold values from -6 to 6
- explicit_filter_weights: float32 [128, 8192], P(None, 'tp'), may hold values from -0.5 to 0.5
- gate_taps: float32 [3, 8192], P(None, 'tp'), may hold values from -3.5 to 3.5
- value_featurizer_weights: float32 [3, 8192], P(None, 'tp'), may hold values from -3.5 to 3.5
Outputs:
- input_grad: bfloat16 [2048, 8192], P('ctx', 'tp')
- explicit_filter_gradient: float32 [128, 8192], P(None, 'tp')
- gate_grad: float32 [3, 8192], P(None, 'tp')
- value_grad: float32 [3, 8192], P(None, 'tp')
All inputs are finite; a program needn't handle non-finite values.
Results may differ from a plain program's by a relative error of at most 0.004.
Values may be sent and summed in bfloat16 or wider, within the bound.
No kernel may reach another device: no remote copies, remote signals or barrier semaphores. Data moves between devices by JAX's collectives and lax.ppermute only.
A program may use at most 64 MiB of HBM per device.

v0:
```python
import math

import jax
import jax.numpy as jnp
from jax import lax
from jax.sharding import PartitionSpec as P


def for_sending(x):

    def short(part):
        return part.astype(jnp.bfloat16) if part.dtype == jnp.float32 else part

    return jax.tree.map(short, x)


def from_behind(x, axis, by):
    count = lax.axis_size(axis)
    pairs = [(i, i + by) for i in range(count) if 0 <= i + by < count]
    return lax.ppermute(x, axis, pairs)


def depthwise(signal, kernel):
    channels = signal.shape[1]
    result = lax.conv_general_dilated(
        signal[None],
        kernel[:, None, :],
        (1,),
        "VALID",
        dimension_numbers=("NWC", "WIO", "NWC"),
        feature_group_count=channels,
        precision=lax.Precision.HIGHEST,
    )
    return result[0]


def causal_mixing(padded, taps, count):
    filter_extent = taps.shape[0]
    return depthwise(padded[: count + filter_extent - 1], taps[::-1])


def anticausal(padded, taps, count):
    return depthwise(padded[: count + taps.shape[0] - 1], taps)


def delayed_input(left, right, filter_extent, base):
    count = left.shape[0]
    start = base - filter_extent + 1
    segment = right[start : start + count + filter_extent - 1]
    return depthwise(segment, left)[::-1]


def compose(value_featurizer_weights, explicit_filter_weights):
    short = value_featurizer_weights.shape[0]
    filter_extent = explicit_filter_weights.shape[0]
    total = jnp.zeros((filter_extent + short - 1, explicit_filter_weights.shape[1]), jnp.float32)
    for i in range(short):
        total = total.at[i : i + filter_extent].add(
            value_featurizer_weights[i] * explicit_filter_weights
        )
    return total


def pass_back(head):
    return from_behind(for_sending(head), "ctx", -1).astype(head.dtype)


def shards(out_grad, saved_input, explicit_filter_weights, gate_taps, value_featurizer_weights):
    tp_count = lax.axis_size("tp")
    width = out_grad.shape[1] // tp_count
    token_rows = out_grad.shape[0] * tp_count
    filter_extent = explicit_filter_weights.shape[0]
    short = gate_taps.shape[0]
    reach = filter_extent + short - 2
    stacked = jnp.stack([out_grad, saved_input])
    local = lax.all_to_all(stacked, "tp", split_axis=2, concat_axis=1, tiled=True)
    input_bf = local[1]
    tail = from_behind(input_bf[token_rows - reach :], "ctx", 1)
    grad_f = local[0].astype(jnp.float32)
    extended_input = jnp.concatenate([tail, input_bf]).astype(jnp.float32)
    extended_value = causal_mixing(
        extended_input, value_featurizer_weights, token_rows + filter_extent - 1
    )
    qext = causal_mixing(extended_input, gate_taps, token_rows + filter_extent - 1)
    gate = qext[filter_extent - 1 :]
    pext = causal_mixing(extended_input, explicit_filter_weights, token_rows + short - 1)
    mixed_signal = causal_mixing(extended_value, explicit_filter_weights, token_rows)
    grad_q = grad_f * mixed_signal
    mixed_signal_gradient = grad_f * gate
    combined = compose(value_featurizer_weights, explicit_filter_weights)
    zpad = jnp.concatenate(
        [
            jnp.zeros((reach, width), jnp.float32),
            mixed_signal_gradient,
            jnp.zeros((reach, width), jnp.float32),
        ]
    )
    qpad = jnp.concatenate(
        [jnp.zeros((reach, width), jnp.float32), grad_q, jnp.zeros((short - 1, width), jnp.float32)]
    )
    whole = anticausal(zpad, combined, token_rows + reach) + anticausal(
        qpad, gate_taps, token_rows + reach
    )
    head = whole[:reach]
    own_rows = whole[reach:]
    incoming = pass_back(head)
    input_grad = jnp.concatenate(
        [own_rows[: token_rows - reach], own_rows[token_rows - reach :] + incoming]
    ).astype(jnp.bfloat16)
    gradient_scale = jnp.float32(1.0 / math.sqrt(token_rows * lax.axis_size("ctx")))
    explicit_filter_term = (
        delayed_input(mixed_signal_gradient, extended_value, filter_extent, filter_extent - 1)
        * gradient_scale
    )
    gate_part = delayed_input(grad_q, extended_input, short, reach) * gradient_scale
    value_part = delayed_input(mixed_signal_gradient, pext, short, short - 1) * gradient_scale
    explicit_filter_gradient, gate_grad, value_grad = lax.psum(
        (explicit_filter_term, gate_part, value_part), "ctx"
    )
    return (input_grad, explicit_filter_gradient, gate_grad, value_grad)


def solution(mesh):
    placed = (
        P(("ctx", "tp"), None),
        P(("ctx", "tp"), None),
        P(None, "tp"),
        P(None, "tp"),
        P(None, "tp"),
    )
    return jax.shard_map(
        shards,
        mesh=mesh,
        in_specs=placed,
        out_specs=(P("ctx", "tp"), P(None, "tp"), P(None, "tp"), P(None, "tp")),
        check_vma=False,
    )
```

profile of v0, /device:TPU:0, one launch (start us, length us, event | category | flops | bytes accessed | tf_op | source)
XLA Modules:
  0.0 357.0 jit_solution(666263850278138449)
XLA Ops:
  8.9 6.9 %copy.100 = bf16[2,64,8192]{1,0,2:T(2,128)(2,1)} copy(bf16[2,64,8192]{2,1,0:T(8,128)(2,1)S(1)} %pad_maximum_fusion.1) | data formatting | bytes 4194304 | tf_op jit(solution)/shard_map/stack | solution.py:75
  15.8 5.9 %reshape.165 = bf16[4,2,131072]{2,1,0:T(2,128)(2,1)} reshape(bf16[8192,2,64]{2,1,0:T(2,128)(2,1)} %bitcast.69) | data formatting | bytes 4194304
  21.8 6.4 %all-to-all-start = ((bf16[4,2,131072]{2,1,0:T(2,128)(2,1)}), bf16[4,2,131072]{2,1,0:T(2,128)(2,1)S(1)}, u32[]{:S(2)}, u32[]{:S(2)}) async-start(bf16[4,2,131072]{2,1,0:T(2,128)(2,1)} %reshape.165), calls=%async_computation | async-start | bytes 4194304 | tf_op jit(solution)/shard_map/all_to_all | solution.py:76
  28.7 5.2 %rev.21 = f32[128,2048]{1,0:T(8,128)} reverse(f32[128,2048]{1,0:T(8,128)S(1)} %copy-done), dimensions={0} | reverse | bytes 2097152 | tf_op jit(solution)/shard_map/rev | solution.py:39
  33.9 4.8 %rev.19 = f32[3,2048]{1,0:T(4,128)} reverse(f32[3,2048]{1,0:T(4,128)S(1)} %copy-done.20), dimensions={0} | reverse | bytes 49152 | tf_op jit(solution)/shard_map/rev | solution.py:39
  41.7 34.8 %all-to-all-done = bf16[4,2,131072]{2,1,0:T(2,128)(2,1)S(1)} async-done(((bf16[4,2,131072]{2,1,0:T(2,128)(2,1)}), bf16[4,2,131072]{2,1,0:T(2,128)(2,1)S(1)}, u32[]{:S(2)}, u32[]{:S(2)}) %all-to-all-start) | async-done | bytes 2097184 | tf_op jit(solution)/shard_map/all_to_all | solution.py:76
  76.4 4.0 %reshape.166 = bf16[8192,2,64]{2,1,0:T(2,128)(2,1)} reshape(bf16[4,2,131072]{2,1,0:T(2,128)(2,1)S(1)} %all-to-all-done) | data formatting | bytes 4194304
  80.4 9.1 %copy.101 = bf16[2,64,4,2048]{3,1,2,0:T(8,128)(2,1)S(1)} copy(bf16[2,64,4,2048]{1,0,3,2:T(2,128)(2,1)} %bitcast.70) | data formatting | bytes 4194304 | tf_op jit(solution)/shard_map/all_to_all | solution.py:76
  93.9 4.1 %scatter-add.11 = f32[130,2048]{1,0:T(8,128)} dynamic-update-slice(f32[130,2048]{1,0:T(8,128)} %scatter-add.10, f32[128,2048]{1,0:T(8,128)} %multiply_add_fusion, s32[]{:T(128)} %constant.105.clone.1, s32[]{:T(128)} %constant.106.clone.1) | dynamic-update-slice | bytes 2097156 | tf_op jit(solution)/shard_map/scatter-add | solution.py:58
  98.0 2.5 fusion.38
  100.5 4.1 %scatter-add.14 = f32[130,1,2048]{2,0,1:T(8,128)} dynamic-update-slice(f32[130,1,2048]{2,0,1:T(8,128)} %bitcast.77, f32[128,1,2048]{2,0,1:T(8,128)} %fusion.38, s32[]{:T(128)} %constant.107.clone.1, s32[]{:T(128)} %constant.106.clone.1, s32[]{:T(128)} %constant.106.clone.1) | dynamic-update-slice | bytes 2097156 | tf_op jit(solution)/shard_map/scatter-add | solution.py:58
  112.2 3.7 %copy.110 = f32[8,49,2048]{2,1,0:T(8,128)} copy(f32[8,49,2048]{2,0,1:T(8,128)S(1)} %convolution_select_fusion) | data formatting | bytes 6422528 | tf_op jit(solution)/shard_map/conv_general_dilated | solution.py:25
  115.9 6.4 %reshape.163 = f32[1,392,2048]{2,0,1:T(1,128)} reshape(f32[8,49,2048]{2,1,0:T(8,128)} %copy.110) | data formatting | bytes 6422528 | tf_op jit(solution)/shard_map/conv_general_dilated | solution.py:25
  122.3 22.7 %fusion.6 = f32[1,258,2048]{2,0,1:T(1,128)} fusion(bf16[1,385,2048]{2,1,0:T(8,128)(2,1)S(1)} %fusion.23, f32[128,1,2048]{2,0,1:T(8,128)S(1)} %bitcast.79), kind=kOutput, calls=%fused_computation.11 | convolution fusion | flops 811597824 | bytes 4739072 | tf_op jit(solution)/shard_map/conv_general_dilated | solution.py:25
  145.0 22.1 %fusion.42 = f32[1,256,2048]{2,0,1:T(1,128)} fusion(f32[1,392,2048]{2,0,1:T(1,128)S(1)} %copy-done.13, f32[128,1,2048]{2,0,1:T(8,128)S(1)} %bitcast.80), kind=kOutput, calls=%fused_computation.61 | convolution fusion | flops 805306368 | bytes 6356992 | tf_op jit(solution)/shard_map/conv_general_dilated | solution.py:25
  168.7 2.8 copy.105
  173.5 5.2 %bitcast_multiply_fusion = (f32[256,1,2048]{2,0,1:T(8,128)}, f32[256,1,2048]{2,0,1:T(8,128)}) fusion(f32[1,256,2048]{2,0,1:T(1,128)} %fusion.42, bf16[2,4,64,2048]{3,2,1,0:T(8,128)(2,1)} %bitcast.72, f32[1,264,2048]{2,1,0:T(8,128)S(1)} %reshape.137), kind=kLoop, calls=%fused_computation.21 | loop fusion | flops 1572864 | bytes 9437184 | tf_op jit(solution)/shard_map/mul | solution.py:88
  178.7 2.5 bitcast_multiply_fusion.3
  182.6 5.5 %reshape.145 = f32[1,8,49,2048]{3,0,2,1:T(1,128)} reshape(f32[1,392,2048]{2,1,0:T(8,128)S(1)} %pad.11) | data formatting | bytes 6422528 | tf_op jit(solution)/shard_map/conv_general_dilated | solution.py:25
  188.1 3.8 %copy.114 = f32[1,8,49,2048]{3,1,2,0:T(8,128)S(1)} copy(f32[1,8,49,2048]{3,0,2,1:T(1,128)} %reshape.145) | data formatting | bytes 6422528 | tf_op jit(solution)/shard_map/conv_general_dilated | solution.py:25
  192.7 3.7 %copy.116 = f32[8,49,2048]{2,1,0:T(8,128)} copy(f32[8,49,2048]{2,0,1:T(8,128)S(1)} %fusion.8) | data formatting | bytes 6422528 | tf_op jit(solution)/shard_map/conv_general_dilated | solution.py:25
  196.3 6.4 %reshape.164 = f32[1,392,2048]{2,0,1:T(1,128)} reshape(f32[8,49,2048]{2,1,0:T(8,128)} %copy.116) | data formatting | bytes 6422528 | tf_op jit(solution)/shard_map/conv_general_dilated | solution.py:25
  203.3 3.2 broadcast_in_dim.41
  206.5 33.7 %slice_add_fusion = f32[1,385,2048]{2,0,1:T(1,128)S(1)} fusion(f32[1,392,2048]{2,0,1:T(1,128)S(1)} %copy-done.15, f32[1,514,2048]{2,0,1:T(1,128)S(1)} %broadcast_in_dim.41, f32[130,1,2048]{2,0,1:T(8,128)S(1)} %copy-done.12), kind=kOutput, calls=%fused_computation.10 | convolution fusion | flops 1230817280 | bytes 11583488 | tf_op jit(solution)/shard_map/conv_general_dilated | solution.py:25
  244.1 21.8 %fusion.33 = f32[1,128,2048]{2,0,1:T(1,128)} fusion(f32[1,392,2048]{2,0,1:T(1,128)S(1)} %copy-done.14, f32[256,1,2048]{2,0,1:T(8,128)S(1)} %copy-done.17), kind=kOutput, calls=%fused_computation.47 | convolution fusion | flops 805306368 | bytes 6356992 | tf_op jit(solution)/shard_map/conv_general_dilated | solution.py:25
  265.9 4.8 %fusion.31 = f32[1,3,2048]{2,0,1:T(1,128)S(1)} fusion(f32[1,258,2048]{2,0,1:T(1,128)S(1)} %copy-done.27, f32[256,1,2048]{2,0,1:T(8,128)S(1)} %copy-done.17), kind=kOutput, calls=%fused_computation.45 | convolution fusion | flops 18874368 | bytes 4235264 | tf_op jit(solution)/shard_map/conv_general_dilated | solution.py:25
  272.9 4.7 %fusion.12 = f32[1,3,2048]{2,0,1:T(1,128)S(1)} fusion(bf16[1,258,2048]{2,1,0:T(8,128)(2,1)S(1)} %fusion.36, f32[256,1,2048]{2,0,1:T(8,128)S(1)} %copy-done.16), kind=kOutput, calls=%fused_computation.18 | convolution fusion | flops 18874368 | bytes 3178496 | tf_op jit(solution)/shard_map/conv_general_dilated | solution.py:25
  281.8 5.2 %rev.22 = f32[128,2048]{1,0:T(8,128)} reverse(f32[128,2048]{1,0:T(8,128)S(1)} %bitcast.78), dimensions={0} | reverse | bytes 2097152 | tf_op jit(solution)/shard_map/rev | solution.py:50
  287.0 2.4 broadcast_multiply_fusion
  289.5 26.6 %all-reduce.1 = (f32[3,2048]{1,0:T(4,128)}, f32[3,2048]{1,0:T(4,128)}) all-reduce(f32[3,2048]{1,0:T(4,128)S(1)} %get-tuple-element.50, f32[3,2048]{1,0:T(4,128)S(1)} %get-tuple-element.49), channel_id=1, replica_groups=mesh['ctx'=8,'tp'=4] {'ctx'}, use_global_device_ids=true, to_apply=%region_1.0 | all-reduce | flops 12288 | bytes 98304 | tf_op jit(solution)/shard_map/psum | solution.py:117
  317.8 29.8 %all-reduce.4.cloned.1.call-done = f32[128,2048]{1,0:T(8,128)} async-done(((f32[128,2048]{1,0:T(8,128)}), f32[128,2048]{1,0:T(8,128)}) %all-reduce.4.cloned.1.call-update) | async-done | bytes 1048592 | tf_op jit(solution)/shard_map/psum | solution.py:117
  347.7 2.3 copy.168
  (104 shorter events, 35.4 us)
Async XLA Ops:
  21.8 6.5 %copy-start.19 = (f32[3,2048]{1,0:T(4,128)S(1)}, f32[3,2048]{1,0:T(4,128)}, u32[]{:S(2)}) copy-start(f32[3,2048]{1,0:T(4,128)} %param.15) | copy-start | bytes 73732
  21.8 6.9 %copy-start = (f32[128,2048]{1,0:T(8,128)S(1)}, f32[128,2048]{1,0:T(8,128)}, u32[]{:S(2)}) copy-start(f32[128,2048]{1,0:T(8,128)} %param.13) | copy-start | bytes 3145732
  21.8 54.6 %all-to-all-start = ((bf16[4,2,131072]{2,1,0:T(2,128)(2,1)}), bf16[4,2,131072]{2,1,0:T(2,128)(2,1)S(1)}, u32[]{:S(2)}, u32[]{:S(2)}) async-start(bf16[4,2,131072]{2,1,0:T(2,128)(2,1)} %reshape.165), calls=%async_computation | async-start | bytes 4194304 | tf_op jit(solution)/shard_map/all_to_all | solution.py:76
  28.2 5.6 %copy-start.20 = (f32[3,2048]{1,0:T(4,128)S(1)}, f32[3,2048]{1,0:T(4,128)}, u32[]{:S(2)}) copy-start(f32[3,2048]{1,0:T(4,128)} %param.14) | copy-start | bytes 73732
  28.2 319.4 %all-reduce.4.cloned.1.call-start = ((), (), s32[]{:S(2)}) async-start(), calls=%async_computation.1 | async-start | bytes 2097152 | tf_op jit(solution)/shard_map/psum | solution.py:117
  89.5 8.5 %copy-start.1 = (bf16[2,64,4,2048]{3,1,2,0:T(8,128)(2,1)}, bf16[2,64,4,2048]{3,1,2,0:T(8,128)(2,1)S(1)}, u32[]{:S(2)}) copy-start(bf16[2,64,4,2048]{3,1,2,0:T(8,128)(2,1)S(1)} %copy.101) | copy-start | bytes 6291460
  89.6 1.1 copy-start.3
  91.6 12.9 %collective-permute-start = (bf16[129,2048]{1,0:T(8,128)(2,1)}, bf16[129,2048]{1,0:T(8,128)(2,1)}, u32[]{:S(2)}, u32[]{:S(2)}) collective-permute-start(bf16[129,2048]{1,0:T(8,128)(2,1)} %slice.135), channel_id=1, source_target_pairs={{0,4},{4,8},{8,12},{12,16},{16,20},{20,24},{24,28},{1,5},{5,9},{9,... | collective-permute-start | bytes 1585160 | tf_op jit(solution)/shard_map/ppermute | solution.py:20
  98.0 6.6 %copy-start.4 = (bf16[1,4,64,2048]{3,2,1,0:T(8,128)(2,1)S(1)}, bf16[1,4,64,2048]{3,2,1,0:T(8,128)(2,1)}, u32[]{:S(2)}) copy-start(bf16[1,4,64,2048]{3,2,1,0:T(8,128)(2,1)} %copy-done.3) | copy-start | bytes 3145732
  115.9 6.4 %copy-start.18 = (f32[128,2048]{1,0:T(8,128)S(1)}, f32[128,2048]{1,0:T(8,128)}, u32[]{:S(2)}) copy-start(f32[128,2048]{1,0:T(8,128)} %rev.21) | copy-start | bytes 3145732
  122.3 22.7 %copy-start.13 = (f32[1,392,2048]{2,0,1:T(1,128)S(1)}, f32[1,392,2048]{2,0,1:T(1,128)}, u32[]{:S(2)}) copy-start(f32[1,392,2048]{2,0,1:T(1,128)} %reshape.163) | copy-start | bytes 9633796
  145.0 22.1 %copy-start.11 = (bf16[1,264,2048]{2,1,0:T(8,128)(2,1)S(1)}, bf16[1,264,2048]{2,1,0:T(8,128)(2,1)}, u32[]{:S(2)}) copy-start(bf16[1,264,2048]{2,1,0:T(8,128)(2,1)} %pad_slice_fusion.2) | copy-start | bytes 3244036
  167.1 1.0 copy-start.22
  167.1 1.0 copy-start.26
  173.5 5.2 %copy-start.2 = (bf16[2,64,4,2048]{3,1,2,0:T(8,128)(2,1)S(1)}, bf16[2,64,4,2048]{3,1,2,0:T(8,128)(2,1)}, u32[]{:S(2)}) copy-start(bf16[2,64,4,2048]{3,1,2,0:T(8,128)(2,1)} %copy-done.1) | copy-start | bytes 6291460
  173.5 5.2 %copy-start.9 = (f32[1,256,2048]{2,0,1:T(1,128)S(1)}, f32[1,256,2048]{2,0,1:T(1,128)}, u32[]{:S(2)}) copy-start(f32[1,256,2048]{2,0,1:T(1,128)} %fusion.42) | copy-start | bytes 6291460
  178.7 2.6 copy-start.23
  181.3 1.0 copy-start.6
  188.1 3.8 %copy-start.21 = (f32[3,2048]{1,0:T(4,128)S(1)}, f32[3,2048]{1,0:T(4,128)}, u32[]{:S(2)}) copy-start(f32[3,2048]{1,0:T(4,128)} %param.14) | copy-start | bytes 73732
  188.1 3.8 %copy-start.24 = (pred[8,49]{0,1:T(8,128)(4,1)S(1)}, pred[8,49]{0,1:T(8,128)(4,1)}, u32[]{:S(2)}) copy-start(pred[8,49]{0,1:T(8,128)(4,1)} %constant.124) | copy-start | bytes 1180
  196.3 6.4 %copy-start.7 = (f32[129,2048]{1,0:T(8,128)S(1)}, f32[129,2048]{1,0:T(8,128)}, u32[]{:S(2)}) copy-start(f32[129,2048]{1,0:T(8,128)} %copy-done.6) | copy-start | bytes 3170308
  196.3 6.4 %copy-start.8 = (f32[256,2048]{1,0:T(8,128)S(1)}, f32[256,2048]{1,0:T(8,128)}, u32[]{:S(2)}) copy-start(f32[256,2048]{1,0:T(8,128)} %get-tuple-element.44) | copy-start | bytes 6291460
  203.3 3.2 copy-start.12
  203.3 3.2 copy-start.15
  240.2 1.7 copy-start.10
  240.3 3.0 copy-start.14
  242.0 2.1 copy-start.17
  244.1 21.8 %copy-start.27 = (f32[1,258,2048]{2,0,1:T(1,128)S(1)}, f32[1,258,2048]{2,0,1:T(1,128)}, u32[]{:S(2)}) copy-start(f32[1,258,2048]{2,0,1:T(1,128)} %fusion.6) | copy-start | bytes 6340612
  265.9 5.4 %copy-start.5 = (bf16[1,4,64,2048]{3,2,1,0:T(8,128)(2,1)S(1)}, bf16[1,4,64,2048]{3,2,1,0:T(8,128)(2,1)}, u32[]{:S(2)}) copy-start(bf16[1,4,64,2048]{3,2,1,0:T(8,128)(2,1)} %copy-done.3) | copy-start | bytes 3145732
  271.3 1.6 copy-start.16
  279.0 37.2 %collective-permute-start.1 = (bf16[129,2048]{1,0:T(8,128)(2,1)}, bf16[129,2048]{1,0:T(8,128)(2,1)S(1)}, u32[]{:S(2)}, u32[]{:S(2)}) collective-permute-start(bf16[129,2048]{1,0:T(8,128)(2,1)} %slice_bitcast_fusion), channel_id=1, source_target_pairs={{4,0},{8,4},{12,8},{16,12},{20,16},{24,20},{28,24},{5,1},{9,5},{13... | collective-permute-start | bytes 1585160 | tf_op jit(solution)/shard_map/ppermute | solution.py:20
  287.0 29.2 %slice-start = ((f32[1,385,2048]{2,0,1:T(1,128)}), f32[1,129,2048]{2,0,1:T(1,128)S(1)}, s32[]{:S(2)}) async-start(f32[1,385,2048]{2,0,1:T(1,128)} %copy-done.10), calls=%async_computation.2 | async-start | bytes 2113536 | tf_op jit(solution)/shard_map/slice | solution.py:108
  (1 other events, 0.9 us)
Sparse Core Ops, SparseCore 0:
  289.5 58.0 all-reduce.3
where the time goes:
time: 361 us; the launch traced here: 357 us
  matrix products  112 us (31%)
  local copies, waits for them, and re-layouts  108 us (30%)
  waiting for transfers between devices  64.6 us (18%)
  blocking collectives  26.6 us (7%)
  other arithmetic  20.7 us (6%)
  between operations  14.7 us (4%)
  starting transfers between devices  9.98 us (3%)
    conv_general_dilated x8, matrix products, depthwise(): lax.conv_general_dilated(signal[None], kernel[:, None, :], (1,), 'VALID',...  111 us
    all_to_all x1, waiting for transfers between devices, shards(): lax.all_to_all(stacked, 'tp', split_axis=2, concat_axis=1, tiled=True)  34.8 us
    conv_general_dilated x10, local copies, waits for them, and re-layouts, depthwise(): lax.conv_general_dilated(signal[None], kernel[:, None, :], (1,), 'VALID',...  32.3 us
    psum x1, waiting for transfers between devices, shards(): lax.psum((explicit_filter_term, gate_part, value_part), 'ctx')  29.8 us
    psum x1, blocking collectives, shards(): lax.psum((explicit_filter_term, gate_part, value_part), 'ctx')  26.6 us
    unnamed x62, local copies, waits for them, and re-layouts  18.9 us
    rev x3, local copies, waits for them, and re-layouts, causal_mixing(): return depthwise(padded[:count + filter_extent - 1], taps[::-1])  10.4 us
    scatter-add x3, local copies, waits for them, and re-layouts, compose(): total.at[i:i + filter_extent]  9.31 us
  transfers between devices with their start and end apart: 4, of which 2 were waited for; matrix products, arithmetic and copies ran while one was open for 10% of the time, Pallas kernels for 0%

commit v1 on v0

v1 whole, which is shorter than its diff:
```python
import math

import jax
import jax.numpy as jnp
import numpy as np
from jax import lax
from jax.experimental import pallas as pl
from jax.experimental.pallas import tpu as pltpu
from jax.sharding import PartitionSpec as P

F32 = jnp.float32
BF16 = jnp.bfloat16


def halves(x):
    high = x.astype(BF16)
    return high, (x - high.astype(F32)).astype(BF16)


def stacked_rows(x):
    high, low = halves(x)
    return jnp.concatenate([high, high, low], axis=0)


def product(matrix, x):
    return jnp.dot(matrix, x, preferred_element_type=F32)


def transforms(extent):
    points = 2 * extent
    angle = np.pi * np.outer(2 * np.arange(extent) + 1, np.arange(points)) / points
    whole = np.concatenate([np.cos(angle), -np.sin(angle)])
    back = whole.T / extent
    back = np.concatenate([-back[extent:], back[:extent]])

    def split(matrix):
        high = matrix.astype(jnp.bfloat16)
        low = (matrix - high.astype(np.float64)).astype(jnp.bfloat16)
        return np.concatenate([high, low, high], axis=1)

    return split(whole), split(whole[:, :extent]), split(back)


def parts(x):
    half = x.shape[0] // 2
    return x[:half], x[half:]


def times(a, b):
    ar, ai = parts(a)
    br, bi = parts(b)
    return ar * br - ai * bi, ar * bi + ai * br


def times_conjugate(a, b):
    ar, ai = parts(a)
    br, bi = parts(b)
    return ar * br + ai * bi, ai * br - ar * bi


def joined(pair):
    return jnp.concatenate(pair, axis=0)


def delayed(x, by):
    return pltpu.roll(x, by, 0)


def advanced(x, by):
    return pltpu.roll(x, x.shape[0] - by, 0)


def signal_kernel(
    u_ref, halo_ref, h_ref, w_ref, forward_ref, short_ref, inverse_ref, v_ref, hs_ref, z_ref
):
    extent = h_ref.shape[0]
    rows = u_ref.shape[0]
    u = jnp.concatenate([halo_ref[...].astype(F32), u_ref[...].astype(F32)], axis=0)
    value = w_ref[0:1] * u
    for i in range(1, w_ref.shape[0]):
        value = value + w_ref[i : i + 1] * delayed(u, i)
    value = value[halo_ref.shape[0] - extent :]
    high, low = halves(value)
    spectrum_h = product(short_ref[...], stacked_rows(h_ref[...]))
    hs_ref[...] = spectrum_h
    for b in range(rows // extent):
        window = slice(b * extent, (b + 2) * extent)
        spectrum = product(
            forward_ref[...], jnp.concatenate([high[window], high[window], low[window]], axis=0)
        )
        v_ref[b] = spectrum
        z = product(inverse_ref[:extent], stacked_rows(joined(times(spectrum, spectrum_h))))
        z_ref[b * extent : (b + 1) * extent] = -z


def gradient_kernel(
    scale,
    pieces,
    me_ref,
    *refs,
):
    g_refs = refs[:pieces]
    (
        u_ref,
        halo_ref,
        v_ref,
        hs_ref,
        z_ref,
        gate_ref,
        w_ref,
        short_ref,
        inverse_ref,
        grad_ref,
        head_ref,
        sums_ref,
        g_all,
    ) = refs[pieces:]
    extent = hs_ref.shape[0] // 2
    rows, width = u_ref.shape
    lead = halo_ref.shape[0]
    taps = gate_ref.shape[0]
    piece = g_refs[0].shape[0]
    for k in range(pieces):
        source = lax.rem(me_ref[0] + (pieces - k), pieces)
        start = pl.multiple_of(source * piece, piece)
        g_all[pl.ds(start, piece), :] = g_refs[k][...].astype(F32)
    g = g_all[...]
    u = jnp.concatenate([halo_ref[...].astype(F32), u_ref[...].astype(F32)], axis=0)
    late = [u] + [delayed(u, i) for i in range(1, taps)]
    q = gate_ref[0:1] * late[0][lead:]
    for i in range(1, taps):
        q = q + gate_ref[i : i + 1] * late[i][lead:]
    dz = g * q
    dq = g * z_ref[...]
    spectrum_h = hs_ref[...]
    correlation = None
    blocks = rows // extent
    back = [jnp.zeros((lead - extent, width), F32)]
    carried = None
    for b in range(blocks):
        spectrum = product(short_ref[...], stacked_rows(dz[b * extent : (b + 1) * extent]))
        term = times_conjugate(spectrum, v_ref[b])
        correlation = (
            term if correlation is None else tuple(x + y for x, y in zip(correlation, term))
        )
        both = product(
            inverse_ref[...], stacked_rows(joined(times_conjugate(spectrum, spectrum_h)))
        )
        back.append(both[:extent] if carried is None else both[:extent] + carried)
        carried = both[extent:]
    back.append(carried)
    r = jnp.concatenate(back, axis=0)
    lags = product(inverse_ref[:extent], stacked_rows(joined(correlation)))
    sums_ref[0:extent] = lags * scale
    rest = [jnp.sum(dq * late[i][lead:], axis=0, keepdims=True) for i in range(taps)]
    rest += [jnp.sum(r * late[i], axis=0, keepdims=True) for i in range(taps)]
    spare = sums_ref.shape[0] - extent - 2 * taps
    rest.append(jnp.zeros((spare, width), F32))
    sums_ref[extent:] = jnp.concatenate(rest, axis=0) * scale
    padded = jnp.concatenate([jnp.zeros((lead, width), F32), dq], axis=0)
    total = w_ref[0:1] * r + gate_ref[0:1] * padded
    for i in range(1, taps):
        total = total + advanced(w_ref[i : i + 1] * r + gate_ref[i : i + 1] * padded, i)
    head_ref[...] = total[:lead].astype(BF16)
    grad_ref[...] = total[lead:].astype(BF16)


def whole_block(shape):
    return pl.BlockSpec(shape, lambda j, *_: (0,) * len(shape))


def columns(shape):
    return pl.BlockSpec(shape, lambda j, *_: (0,) * (len(shape) - 1) + (j,))


VMEM_LIMIT = 48 * 1024 * 1024


def signal_step(u, halo, h, w, matrices, block):
    rows, width = u.shape
    extent = h.shape[0]
    forward, short, inverse = matrices
    blocks = rows // extent
    return pl.pallas_call(
        signal_kernel,
        grid=(width // block,),
        in_specs=[
            columns((rows, block)),
            columns((halo.shape[0], block)),
            columns((extent, block)),
            columns((w.shape[0], block)),
            whole_block(forward.shape),
            whole_block(short.shape),
            whole_block(inverse.shape),
        ],
        out_specs=[
            columns((blocks, 2 * extent, block)),
            columns((2 * extent, block)),
            columns((rows, block)),
        ],
        out_shape=[
            jax.ShapeDtypeStruct((blocks, 2 * extent, width), F32),
            jax.ShapeDtypeStruct((2 * extent, width), F32),
            jax.ShapeDtypeStruct((rows, width), F32),
        ],
        compiler_params=pltpu.CompilerParams(vmem_limit_bytes=VMEM_LIMIT),
        name="signal_step",
    )(u, halo, h, w, forward, short, inverse)


def gradient_step(g_pieces, me, u, halo, v, hs, z, gate, w, matrices, scale, block):
    rows, width = u.shape
    extent = hs.shape[0] // 2
    taps = gate.shape[0]
    lead = halo.shape[0]
    _, short, inverse = matrices
    blocks = rows // extent
    count = extent + -(-2 * taps // 8) * 8

    def kernel(*refs):
        gradient_kernel(scale, len(g_pieces), *refs)

    return pl.pallas_call(
        kernel,
        grid_spec=pltpu.PrefetchScalarGridSpec(
            num_scalar_prefetch=1,
            grid=(width // block,),
            in_specs=[columns((g.shape[0], block)) for g in g_pieces]
            + [
                columns((rows, block)),
                columns((lead, block)),
                columns((blocks, 2 * extent, block)),
                columns((2 * extent, block)),
                columns((rows, block)),
                columns((taps, block)),
                columns((taps, block)),
                whole_block(short.shape),
                whole_block(inverse.shape),
            ],
            out_specs=[
                columns((rows, block)),
                columns((lead, block)),
                columns((count, block)),
            ],
            scratch_shapes=[pltpu.VMEM((rows, block), F32)],
        ),
        out_shape=[
            jax.ShapeDtypeStruct((rows, width), BF16),
            jax.ShapeDtypeStruct((lead, width), BF16),
            jax.ShapeDtypeStruct((count, width), F32),
        ],
        compiler_params=pltpu.CompilerParams(vmem_limit_bytes=VMEM_LIMIT),
        name="gradient_step",
    )(me, *g_pieces, u, halo, v, hs, z, gate, w, short, inverse)


def order_kernel(pieces, me_ref, *refs):
    out_ref, tail_ref = refs[pieces:]
    piece = refs[0].shape[0]
    for k in range(pieces):
        source = lax.rem(me_ref[0] + (pieces - k), pieces)
        start = pl.multiple_of(source * piece, piece)
        out_ref[pl.ds(start, piece), :] = refs[k][...]
    tail_ref[...] = out_ref[out_ref.shape[0] - tail_ref.shape[0] :]


def in_order(pieces, me, lead, block):
    piece, width = pieces[0].shape
    rows = piece * len(pieces)

    def kernel(*refs):
        order_kernel(len(pieces), *refs)

    return pl.pallas_call(
        kernel,
        grid_spec=pltpu.PrefetchScalarGridSpec(
            num_scalar_prefetch=1,
            grid=(width // block,),
            in_specs=[columns((piece, block)) for _ in pieces],
            out_specs=[columns((rows, block)), columns((lead, block))],
        ),
        out_shape=[
            jax.ShapeDtypeStruct((rows, width), BF16),
            jax.ShapeDtypeStruct((lead, width), BF16),
        ],
        name="token_order",
    )(me, *pieces)


def exchange(x, axis):
    count = lax.axis_size(axis)
    me = lax.axis_index(axis)
    width = x.shape[1] // count
    pieces = []
    for k in range(count):
        to = lax.rem(me + k, count)
        pieces.append(lax.dynamic_slice_in_dim(x, to * width, width, axis=1))
    got = [None] * count
    got[0] = pieces[0]
    for k in sorted(range(1, count), key=lambda k: abs(2 * k - count)):
        got[k] = lax.ppermute(pieces[k], axis, [(i, (i + k) % count) for i in range(count)])
    return got


def shifted(x, axis, by):
    count = lax.axis_size(axis)
    pairs = [(i, i + by) for i in range(count) if 0 <= i + by < count]
    return lax.ppermute(x, axis, pairs)


def partner(x, axis, bit):
    count = lax.axis_size(axis)
    return lax.ppermute(x, axis, [(i, i ^ bit) for i in range(count)])


def summed(x, axis):
    count = lax.axis_size(axis)
    me = lax.axis_index(axis)
    width = x.shape[1] // 2
    side = lax.rem(me, 2)
    own = lax.dynamic_slice_in_dim(x, side * width, width, axis=1)
    other = lax.dynamic_slice_in_dim(x, (1 - side) * width, width, axis=1)
    own = own + partner(other, axis, 1)
    bit = 2
    while bit < count:
        short = own.astype(BF16)
        own = short.astype(F32) + partner(short, axis, bit).astype(F32)
        bit *= 2
    other = partner(own, axis, 1)
    first = jnp.where(side == 0, own, other)
    second = jnp.where(side == 0, other, own)
    return jnp.concatenate([first, second], axis=1)


def shards(out_grad, saved_input, explicit_filter_weights, gate_taps, value_featurizer_weights):
    h, gate, w = explicit_filter_weights, gate_taps, value_featurizer_weights
    extent, taps = h.shape[0], gate.shape[0]
    me = lax.axis_index("tp").astype(jnp.int32).reshape(1)
    rows = out_grad.shape[0] * lax.axis_size("tp")
    lead = -(-(extent + taps - 2) // 16) * 16
    block = 256
    matrices = tuple(jnp.asarray(m) for m in transforms(extent))
    u_pieces = exchange(saved_input, "tp")
    g_pieces = exchange(out_grad, "tp")
    u, tail = in_order(u_pieces, me, lead, min(1024, h.shape[1]))
    halo = shifted(tail, "ctx", 1)
    v, hs, z = signal_step(u, halo, h, w, matrices, block)
    scale = 1.0 / math.sqrt(rows * lax.axis_size("ctx"))
    grad, head, sums = gradient_step(
        g_pieces, me, u, halo, v, hs, z, gate, w, matrices, scale, block
    )
    incoming = shifted(head, "ctx", -1)
    end = (grad[rows - lead :].astype(F32) + incoming.astype(F32)).astype(BF16)
    input_grad = jnp.concatenate([grad[: rows - lead], end])
    sums = summed(sums, "ctx")
    return (
        input_grad,
        sums[:extent],
        sums[extent : extent + taps],
        sums[extent + taps : extent + 2 * taps],
    )


def solution(mesh):
    placed = (
        P(("ctx", "tp"), None),
        P(("ctx", "tp"), None),
        P(None, "tp"),
        P(None, "tp"),
        P(None, "tp"),
    )
    return jax.shard_map(
        shards,
        mesh=mesh,
        in_specs=placed,
        out_specs=(P("ctx", "tp"), P(None, "tp"), P(None, "tp"), P(None, "tp")),
        check_vma=False,
    )
```

time: 361 us -> 104 us (0.29)
  the two profiles are of different devices: /device:TPU:0 before, /device:TPU:11 now
where the time goes in v1:
time: 104 us; the launch traced here: 103 us
  waiting for transfers between devices  52.4 us (50%)
  Pallas kernels  21.6 us (21%)
  starting transfers between devices  14.1 us (14%)
  local copies, waits for them, and re-layouts  10.1 us (10%)
  other arithmetic  4.28 us (4%)
    ppermute x6, waiting for transfers between devices, exchange(): lax.ppermute(pieces[k], axis, [(i, (i + k) % count) for i in range(count)])  30.4 us
    ppermute x4, waiting for transfers between devices, partner(): return lax.ppermute(x, axis, [(i, i ^ bit) for i in range(count)])  19.9 us
    pallas_call x1, Pallas kernels, gradient_step(): pl.pallas_call(kernel, grid_spec=pltpu.PrefetchScalarGridSpec(num_scalar_...  11.2 us
    pallas_call x1, Pallas kernels, signal_step(): pl.pallas_call(signal_kernel, grid=(width // block,), in_specs=[columns((...  8.04 us
    ppermute x6, starting transfers between devices, exchange(): lax.ppermute(pieces[k], axis, [(i, (i + k) % count) for i in range(count)])  6.64 us
    ppermute x2, starting transfers between devices, shifted(): return lax.ppermute(x, axis, pairs)  5.91 us
    unnamed x32, local copies, waits for them, and re-layouts  5.83 us
    dynamic_slice x2, local copies, waits for them, and re-layouts, exchange(): pieces.append(lax.dynamic_slice_in_dim(x, to * width, width, axis=1))  4.14 us
  transfers between devices with their start and end apart: 12, of which 10 were waited for; matrix products, arithmetic and copies ran while one was open for 3% of the time, Pallas kernels for 8%

profile of v1, /device:TPU:11, one launch (start us, length us, event | category | flops | bytes accessed | tf_op | source)
XLA Modules:
  0.0 103.2 jit_solution(4317568693594528252)
XLA Ops:
  0.7 2.0 %constant_dynamic-slice_fusion.1 = (bf16[64,2048]{1,0:T(8,128)(2,1)S(1)}, bf16[64,2048]{1,0:T(8,128)(2,1)S(1)}, bf16[64,2048]{1,0:T(8,128)(2,1)}, bf16[64,2048]{1,0:T(8,128)(2,1)S(1)}) fusion(bf16[64,8192]{1,0:T(8,128)(2,1)} %param.9, s32[]{:T(128)S(6)} %select_n.37, s32[]{:T(128)S(6)} %select_n.35, s32[]{:T(128)S(6)} %select_n.34, s32[]{:T(128)S(6)} %select_n.36), kind=kLoop, calls=%fused_computation.15 | loop fusion | bytes 2097168 | tf_op jit(solution)/shard_map/dynamic_slice | solution.py:297
  2.7 1.3 %collective-permute-start.3 = (bf16[64,2048]{1,0:T(8,128)(2,1)S(1)}, bf16[64,2048]{1,0:T(8,128)(2,1)S(1)}, u32[]{:S(2)}, u32[]{:S(2)}) collective-permute-start(bf16[64,2048]{1,0:T(8,128)(2,1)S(1)} %get-tuple-element.25), channel_id=1, source_target_pairs={{0,1},{1,2},{2,3},{3,0},{4,5},{5,6},{6,7},{7,4},{8,9},{9,10},{10,1... | collective-permute-start | bytes 786440 | tf_op jit(solution)/shard_map/ppermute | solution.py:301
  4.0 1.0 collective-permute-start.4
  5.0 1.5 %collective-permute-start.5 = (bf16[64,2048]{1,0:T(8,128)(2,1)S(1)}, bf16[64,2048]{1,0:T(8,128)(2,1)S(1)}, u32[]{:S(2)}, u32[]{:S(2)}) collective-permute-start(bf16[64,2048]{1,0:T(8,128)(2,1)S(1)} %get-tuple-element.24), channel_id=1, source_target_pairs={{0,3},{1,0},{2,1},{3,2},{4,7},{5,4},{6,5},{7,6},{8,11},{9,8},{10,9... | collective-permute-start | bytes 786440 | tf_op jit(solution)/shard_map/ppermute | solution.py:301
  6.4 3.4 %collective-permute-done.3.refs_2_ = bf16[64,2048]{1,0:T(8,128)(2,1)S(1)} collective-permute-done((bf16[64,2048]{1,0:T(8,128)(2,1)S(1)}, bf16[64,2048]{1,0:T(8,128)(2,1)S(1)}, u32[]{:S(2)}, u32[]{:S(2)}) %collective-permute-start.3) | collective-permute-done | bytes 262176 | tf_op jit(solution)/shard_map/ppermute | solution.py:301
  9.8 15.9 %collective-permute-done.4.refs_3_ = bf16[64,2048]{1,0:T(8,128)(2,1)S(1)} collective-permute-done((bf16[64,2048]{1,0:T(8,128)(2,1)S(1)}, bf16[64,2048]{1,0:T(8,128)(2,1)S(1)}, u32[]{:S(2)}, u32[]{:S(2)}) %collective-permute-start.4) | collective-permute-done | bytes 262176 | tf_op jit(solution)/shard_map/ppermute | solution.py:301
  25.8 2.8 %collective-permute-done.5.refs_4_ = bf16[64,2048]{1,0:T(8,128)(2,1)S(1)} collective-permute-done((bf16[64,2048]{1,0:T(8,128)(2,1)S(1)}, bf16[64,2048]{1,0:T(8,128)(2,1)S(1)}, u32[]{:S(2)}, u32[]{:S(2)}) %collective-permute-start.5) | collective-permute-done | bytes 262176 | tf_op jit(solution)/shard_map/ppermute | solution.py:301
  28.6 0.7 copy-done.15
  29.3 2.4 %token_order.1 = (bf16[256,2048]{1,0:T(8,128)(2,1)}, bf16[144,2048]{1,0:T(8,128)(2,1)}) custom-call(s32[1]{0:T(128)} %bitcast.refs_0_, bf16[64,2048]{1,0:T(8,128)(2,1)} %get-tuple-element.26.refs_1_, bf16[64,2048]{1,0:T(8,128)(2,1)} %copy-done.13, bf16[64,2048]{1,0:T(8,128)(2,1)} %copy-done.14, bf16[64,2048]{1,0:T(8,128)(2,1)} %copy-done.15), custom_call_target="tpu_custom_call" | custom-call | tf_op jit(solution)/shard_map/token_order/pallas_call | solution.py:274
  31.7 3.6 %collective-permute-start.6 = (bf16[144,2048]{1,0:T(8,128)(2,1)}, bf16[144,2048]{1,0:T(8,128)(2,1)S(1)}, u32[]{:S(2)}, u32[]{:S(2)}) collective-permute-start(bf16[144,2048]{1,0:T(8,128)(2,1)} %get-tuple-element.13), channel_id=1, source_target_pairs={{0,4},{4,8},{8,12},{12,16},{16,20},{20,24},{24,28},{1,5},{5,9},{9,... | collective-permute-start | bytes 1769480 | tf_op jit(solution)/shard_map/ppermute | solution.py:308
  35.4 2.1 %constant_dynamic-slice_fusion.5 = (bf16[64,2048]{1,0:T(8,128)(2,1)}, bf16[64,2048]{1,0:T(8,128)(2,1)}, bf16[64,2048]{1,0:T(8,128)(2,1)S(1)}, bf16[64,2048]{1,0:T(8,128)(2,1)}) fusion(bf16[64,8192]{1,0:T(8,128)(2,1)} %param.8, s32[]{:T(128)S(6)} %select_n.37, s32[]{:T(128)S(6)} %select_n.35, s32[]{:T(128)S(6)} %select_n.34, s32[]{:T(128)S(6)} %select_n.36), kind=kLoop, calls=%fused_computation.19 | loop fusion | bytes 2097168 | tf_op jit(solution)/shard_map/dynamic_slice | solution.py:297
  37.5 1.4 %collective-permute-start.1 = (bf16[64,2048]{1,0:T(8,128)(2,1)}, bf16[64,2048]{1,0:T(8,128)(2,1)}, u32[]{:S(2)}, u32[]{:S(2)}) collective-permute-start(bf16[64,2048]{1,0:T(8,128)(2,1)} %get-tuple-element.31), channel_id=1, source_target_pairs={{0,2},{1,3},{2,0},{3,1},{4,6},{5,7},{6,4},{7,5},{8,10},{9,11},{10,... | collective-permute-start | bytes 786440 | tf_op jit(solution)/shard_map/ppermute | solution.py:301
  38.9 1.5 %collective-permute-start.2 = (bf16[64,2048]{1,0:T(8,128)(2,1)}, bf16[64,2048]{1,0:T(8,128)(2,1)}, u32[]{:S(2)}, u32[]{:S(2)}) collective-permute-start(bf16[64,2048]{1,0:T(8,128)(2,1)} %get-tuple-element.28), channel_id=1, source_target_pairs={{0,3},{1,0},{2,1},{3,2},{4,7},{5,4},{6,5},{7,6},{8,11},{9,8},{10,9... | collective-permute-start | bytes 786440 | tf_op jit(solution)/shard_map/ppermute | solution.py:301
  40.4 2.1 %collective-permute-done.6.halo_ref.refs_6_ = bf16[144,2048]{1,0:T(8,128)(2,1)S(1)} collective-permute-done((bf16[144,2048]{1,0:T(8,128)(2,1)}, bf16[144,2048]{1,0:T(8,128)(2,1)S(1)}, u32[]{:S(2)}, u32[]{:S(2)}) %collective-permute-start.6) | collective-permute-done | bytes 589856 | tf_op jit(solution)/shard_map/ppermute | solution.py:308
  42.5 0.9 copy-done.6
  43.5 1.0 copy-done.8
  44.5 8.0 %signal_step.1 = (f32[2,256,2048]{2,1,0:T(8,128)}, f32[256,2048]{1,0:T(8,128)S(1)}, f32[256,2048]{1,0:T(8,128)}) custom-call(bf16[256,2048]{1,0:T(8,128)(2,1)S(1)} %copy-done, bf16[144,2048]{1,0:T(8,128)(2,1)S(1)} %collective-permute-done.6.halo_ref.refs_6_, f32[128,2048]{1,0:T(8,128)S(1)} %copy-done.3, f32[3,2048]{1,0:T(4,128)S(1)} %copy-done.9, ...), custom_call_target="tpu_custom_call" | custom-call | tf_op jit(solution)/shard_map/signal_step/pallas_call | solution.py:184
  52.5 1.4 %copy-done.1 = f32[256,2048]{1,0:T(8,128)} copy-done((f32[256,2048]{1,0:T(8,128)}, f32[256,2048]{1,0:T(8,128)S(1)}, u32[]{:S(2)}) %copy-start.1) | copy-done | bytes 2097176
  53.9 6.0 %collective-permute-done.1.refs_3_ = bf16[64,2048]{1,0:T(8,128)(2,1)} collective-permute-done((bf16[64,2048]{1,0:T(8,128)(2,1)}, bf16[64,2048]{1,0:T(8,128)(2,1)}, u32[]{:S(2)}, u32[]{:S(2)}) %collective-permute-start.1) | collective-permute-done | bytes 262176 | tf_op jit(solution)/shard_map/ppermute | solution.py:301
  59.9 2.1 %collective-permute-done.2.refs_4_ = bf16[64,2048]{1,0:T(8,128)(2,1)} collective-permute-done((bf16[64,2048]{1,0:T(8,128)(2,1)}, bf16[64,2048]{1,0:T(8,128)(2,1)}, u32[]{:S(2)}, u32[]{:S(2)}) %collective-permute-start.2) | collective-permute-done | bytes 262176 | tf_op jit(solution)/shard_map/ppermute | solution.py:301
  62.1 11.2 %gradient_step.1 = (bf16[256,2048]{1,0:T(8,128)(2,1)S(1)}, bf16[144,2048]{1,0:T(8,128)(2,1)S(1)}, f32[136,2048]{1,0:T(8,128)S(1)}) custom-call(s32[1]{0:T(128)} %bitcast.refs_0_, bf16[64,2048]{1,0:T(8,128)(2,1)S(1)} %get-tuple-element.30.refs_1_, bf16[64,2048]{1,0:T(8,128)(2,1)} %collective-permute-done.refs_2_, ...), custom_call_target="tpu_custom_call" | custom-call | tf_op jit(solution)/shard_map/gradient_step/pallas_call | solution.py:223
  73.3 1.0 copy-done.4
  74.2 0.8 copy-done.11
  75.6 1.7 %collective-permute-done.8 = f32[136,1024]{1,0:T(8,128)} collective-permute-done((f32[136,1024]{1,0:T(8,128)S(1)}, f32[136,1024]{1,0:T(8,128)}, u32[]{:S(2)}, u32[]{:S(2)}) %collective-permute-start.8) | collective-permute-done | bytes 557088 | tf_op jit(solution)/shard_map/ppermute | solution.py:313
  77.3 1.1 %add_convert_fusion.2 = bf16[136,1024]{1,0:T(8,128)(2,1)S(1)} fusion(f32[136,1024]{1,0:T(8,128)} %collective-permute-done.8, f32[136,2048]{1,0:T(8,128)S(1)} %get-tuple-element.19, s32[]{:T(128)S(6)} %select_n.39), kind=kLoop, calls=%fused_computation.9 | loop fusion | flops 278528 | bytes 1392644 | tf_op jit(solution)/shard_map/convert_element_type | solution.py:326
  78.5 2.3 %collective-permute-start.7 = (bf16[144,2048]{1,0:T(8,128)(2,1)S(1)}, bf16[144,2048]{1,0:T(8,128)(2,1)S(1)}, u32[]{:S(2)}, u32[]{:S(2)}) collective-permute-start(bf16[144,2048]{1,0:T(8,128)(2,1)S(1)} %copy-done.12), channel_id=1, source_target_pairs={{4,0},{8,4},{12,8},{16,12},{20,16},{24,20},{28,24},{5,1},{9,5},{13... | collective-permute-start | bytes 1769480 | tf_op jit(solution)/shard_map/ppermute | solution.py:308
  80.8 5.6 %collective-permute-done.9 = bf16[136,1024]{1,0:T(8,128)(2,1)S(1)} collective-permute-done((bf16[136,1024]{1,0:T(8,128)(2,1)S(1)}, bf16[136,1024]{1,0:T(8,128)(2,1)S(1)}, u32[]{:S(2)}, u32[]{:S(2)}) %collective-permute-start.9) | collective-permute-done | bytes 278560 | tf_op jit(solution)/shard_map/ppermute | solution.py:313
  86.9 12.2 %collective-permute-done.10 = bf16[136,1024]{1,0:T(8,128)(2,1)S(1)} collective-permute-done((bf16[136,1024]{1,0:T(8,128)(2,1)S(1)}, bf16[136,1024]{1,0:T(8,128)(2,1)S(1)}, u32[]{:S(2)}, u32[]{:S(2)}) %collective-permute-start.10) | collective-permute-done | bytes 278560 | tf_op jit(solution)/shard_map/ppermute | solution.py:313
  99.2 0.6 collective-permute-start.11
  99.9 1.0 %pad_maximum_fusion = bf16[256,2048]{1,0:T(8,128)(2,1)} fusion(bf16[144,2048]{1,0:T(8,128)(2,1)S(1)} %add_convert_fusion, bf16[112,2048]{1,0:T(8,128)(2,1)S(1)} %slice.15), kind=kLoop, calls=%fused_computation.6 | loop fusion | flops 2097152 | bytes 2097152 | tf_op jit(solution)/shard_map/concatenate | solution.py:354
  101.5 0.6 pad_maximum_fusion.1
  102.1 1.1 %fusion = f32[128,2048]{1,0:T(8,128)} fusion(f32[136,1024]{1,0:T(8,128)S(1)} %get-tuple-element.23, f32[136,1024]{1,0:T(8,128)S(1)} %get-tuple-element.22), kind=kLoop, calls=%fused_computation.5 | loop fusion | flops 262144 | bytes 2162688 | tf_op jit(solution)/shard_map/concatenate | solution.py:332
  (39 shorter events, 1.9 us)
Async XLA Ops:
  2.7 7.2 %collective-permute-start.3 = (bf16[64,2048]{1,0:T(8,128)(2,1)S(1)}, bf16[64,2048]{1,0:T(8,128)(2,1)S(1)}, u32[]{:S(2)}, u32[]{:S(2)}) collective-permute-start(bf16[64,2048]{1,0:T(8,128)(2,1)S(1)} %get-tuple-element.25), channel_id=1, source_target_pairs={{0,1},{1,2},{2,3},{3,0},{4,5},{5,6},{6,7},{7,4},{8,9},{9,10},{10,1... | collective-permute-start | bytes 786440 | tf_op jit(solution)/shard_map/ppermute | solution.py:301
  4.0 21.8 %collective-permute-start.4 = (bf16[64,2048]{1,0:T(8,128)(2,1)S(1)}, bf16[64,2048]{1,0:T(8,128)(2,1)S(1)}, u32[]{:S(2)}, u32[]{:S(2)}) collective-permute-start(bf16[64,2048]{1,0:T(8,128)(2,1)S(1)} %get-tuple-element.27), channel_id=1, source_target_pairs={{0,2},{1,3},{2,0},{3,1},{4,6},{5,7},{6,4},{7,5},{8,10},{9,11},{10,... | collective-permute-start | bytes 786440 | tf_op jit(solution)/shard_map/ppermute | solution.py:301
  5.0 23.7 %collective-permute-start.5 = (bf16[64,2048]{1,0:T(8,128)(2,1)S(1)}, bf16[64,2048]{1,0:T(8,128)(2,1)S(1)}, u32[]{:S(2)}, u32[]{:S(2)}) collective-permute-start(bf16[64,2048]{1,0:T(8,128)(2,1)S(1)} %get-tuple-element.24), channel_id=1, source_target_pairs={{0,3},{1,0},{2,1},{3,2},{4,7},{5,4},{6,5},{7,6},{8,11},{9,8},{10,9... | collective-permute-start | bytes 786440 | tf_op jit(solution)/shard_map/ppermute | solution.py:301
  9.8 18.8 %copy-start.13 = (bf16[64,2048]{1,0:T(8,128)(2,1)}, bf16[64,2048]{1,0:T(8,128)(2,1)S(1)}, u32[]{:S(2)}) copy-start(bf16[64,2048]{1,0:T(8,128)(2,1)S(1)} %collective-permute-done.3.refs_2_) | copy-start | bytes 786436
  25.8 2.9 %copy-start.14 = (bf16[64,2048]{1,0:T(8,128)(2,1)}, bf16[64,2048]{1,0:T(8,128)(2,1)S(1)}, u32[]{:S(2)}) copy-start(bf16[64,2048]{1,0:T(8,128)(2,1)S(1)} %collective-permute-done.4.refs_3_) | copy-start | bytes 786436
  28.6 0.7 copy-start.15
  29.3 13.2 %copy-start.3 = (f32[128,2048]{1,0:T(8,128)S(1)}, f32[128,2048]{1,0:T(8,128)}, u32[]{:S(2)}) copy-start(f32[128,2048]{1,0:T(8,128)} %h_ref.1) | copy-start | bytes 3145732
  31.7 10.8 %copy-start = (bf16[256,2048]{1,0:T(8,128)(2,1)S(1)}, bf16[256,2048]{1,0:T(8,128)(2,1)}, u32[]{:S(2)}) copy-start(bf16[256,2048]{1,0:T(8,128)(2,1)} %get-tuple-element.12.u_ref.refs_5_) | copy-start | bytes 3145732
  31.7 10.8 %copy-start.2 = (bf16[256,768]{1,0:T(8,128)(2,1)S(1)}, bf16[256,768]{1,0:T(8,128)(2,1)}, u32[]{:S(2)}) copy-start(bf16[256,768]{1,0:T(8,128)(2,1)} %constant.42.clone.inverse_ref.refs_13_) | copy-start | bytes 1179652
  31.7 10.8 %copy-start.9 = (f32[3,2048]{1,0:T(4,128)S(1)}, f32[3,2048]{1,0:T(4,128)}, u32[]{:S(2)}) copy-start(f32[3,2048]{1,0:T(4,128)} %refs_11_.1) | copy-start | bytes 73732
  31.7 10.8 %collective-permute-start.6 = (bf16[144,2048]{1,0:T(8,128)(2,1)}, bf16[144,2048]{1,0:T(8,128)(2,1)S(1)}, u32[]{:S(2)}, u32[]{:S(2)}) collective-permute-start(bf16[144,2048]{1,0:T(8,128)(2,1)} %get-tuple-element.13), channel_id=1, source_target_pairs={{0,4},{4,8},{8,12},{12,16},{16,20},{20,24},{24,28},{1,5},{5,9},{9,... | collective-permute-start | bytes 1769480 | tf_op jit(solution)/shard_map/ppermute | solution.py:308
  37.5 16.4 %collective-permute-start = (bf16[64,2048]{1,0:T(8,128)(2,1)}, bf16[64,2048]{1,0:T(8,128)(2,1)}, u32[]{:S(2)}, u32[]{:S(2)}) collective-permute-start(bf16[64,2048]{1,0:T(8,128)(2,1)} %get-tuple-element.29), channel_id=1, source_target_pairs={{0,1},{1,2},{2,3},{3,0},{4,5},{5,6},{6,7},{7,4},{8,9},{9,10},{10,1... | collective-permute-start | bytes 786440 | tf_op jit(solution)/shard_map/ppermute | solution.py:301
  37.5 22.4 %collective-permute-start.1 = (bf16[64,2048]{1,0:T(8,128)(2,1)}, bf16[64,2048]{1,0:T(8,128)(2,1)}, u32[]{:S(2)}, u32[]{:S(2)}) collective-permute-start(bf16[64,2048]{1,0:T(8,128)(2,1)} %get-tuple-element.31), channel_id=1, source_target_pairs={{0,2},{1,3},{2,0},{3,1},{4,6},{5,7},{6,4},{7,5},{8,10},{9,11},{10,... | collective-permute-start | bytes 786440 | tf_op jit(solution)/shard_map/ppermute | solution.py:301
  38.9 23.1 %collective-permute-start.2 = (bf16[64,2048]{1,0:T(8,128)(2,1)}, bf16[64,2048]{1,0:T(8,128)(2,1)}, u32[]{:S(2)}, u32[]{:S(2)}) collective-permute-start(bf16[64,2048]{1,0:T(8,128)(2,1)} %get-tuple-element.28), channel_id=1, source_target_pairs={{0,3},{1,0},{2,1},{3,2},{4,7},{5,4},{6,5},{7,6},{8,11},{9,8},{10,9... | collective-permute-start | bytes 786440 | tf_op jit(solution)/shard_map/ppermute | solution.py:301
  42.5 0.9 copy-start.6
  43.5 1.0 copy-start.8
  44.4 17.6 %copy-start.7 = (bf16[256,384]{1,0:T(8,128)(2,1)S(1)}, bf16[256,384]{1,0:T(8,128)(2,1)}, u32[]{:S(2)}) copy-start(bf16[256,384]{1,0:T(8,128)(2,1)} %constant.41.clone.short_ref.refs_12_) | copy-start | bytes 589828
  44.4 17.6 %copy-start.10 = (f32[3,2048]{1,0:T(4,128)S(1)}, f32[3,2048]{1,0:T(4,128)}, u32[]{:S(2)}) copy-start(f32[3,2048]{1,0:T(4,128)} %refs_10_.1) | copy-start | bytes 73732
  52.5 1.4 %copy-start.1 = (f32[256,2048]{1,0:T(8,128)}, f32[256,2048]{1,0:T(8,128)S(1)}, u32[]{:S(2)}) copy-start(f32[256,2048]{1,0:T(8,128)S(1)} %get-tuple-element.15.refs_8_) | copy-start | bytes 6291460
  73.3 1.0 copy-start.4
  74.2 0.8 copy-start.11
  75.0 3.4 %copy-start.12 = (bf16[144,2048]{1,0:T(8,128)(2,1)S(1)}, bf16[144,2048]{1,0:T(8,128)(2,1)}, u32[]{:S(2)}) copy-start(bf16[144,2048]{1,0:T(8,128)(2,1)} %copy-done.11) | copy-start | bytes 1769476
  75.1 11.7 %copy-start.5 = (bf16[256,2048]{1,0:T(8,128)(2,1)S(1)}, bf16[256,2048]{1,0:T(8,128)(2,1)}, u32[]{:S(2)}) copy-start(bf16[256,2048]{1,0:T(8,128)(2,1)} %copy-done.4) | copy-start | bytes 3145732
  75.1 2.2 %collective-permute-start.8 = (f32[136,1024]{1,0:T(8,128)S(1)}, f32[136,1024]{1,0:T(8,128)}, u32[]{:S(2)}, u32[]{:S(2)}) collective-permute-start(f32[136,1024]{1,0:T(8,128)S(1)} %constant_dynamic-slice_fusion), channel_id=1, source_target_pairs={{0,4},{4,0},{8,12},{12,8},{16,20},{20,16},{24,28},{28,24},{1,5},{5... | collective-permute-start | bytes 1671176 | tf_op jit(solution)/shard_map/ppermute | solution.py:313
  78.4 7.9 %collective-permute-start.9 = (bf16[136,1024]{1,0:T(8,128)(2,1)S(1)}, bf16[136,1024]{1,0:T(8,128)(2,1)S(1)}, u32[]{:S(2)}, u32[]{:S(2)}) collective-permute-start(bf16[136,1024]{1,0:T(8,128)(2,1)S(1)} %add_convert_fusion.2), channel_id=1, source_target_pairs={{0,8},{4,12},{8,0},{12,4},{16,24},{20,28},{24,16},{28,20},{1,9},{5... | collective-permute-start | bytes 835592 | tf_op jit(solution)/shard_map/ppermute | solution.py:313
  78.5 21.2 %collective-permute-start.7 = (bf16[144,2048]{1,0:T(8,128)(2,1)S(1)}, bf16[144,2048]{1,0:T(8,128)(2,1)S(1)}, u32[]{:S(2)}, u32[]{:S(2)}) collective-permute-start(bf16[144,2048]{1,0:T(8,128)(2,1)S(1)} %copy-done.12), channel_id=1, source_target_pairs={{4,0},{8,4},{12,8},{16,12},{20,16},{24,20},{28,24},{5,1},{9,5},{13... | collective-permute-start | bytes 1769480 | tf_op jit(solution)/shard_map/ppermute | solution.py:308
  86.4 12.7 %collective-permute-start.10 = (bf16[136,1024]{1,0:T(8,128)(2,1)S(1)}, bf16[136,1024]{1,0:T(8,128)(2,1)S(1)}, u32[]{:S(2)}, u32[]{:S(2)}) collective-permute-start(bf16[136,1024]{1,0:T(8,128)(2,1)S(1)} %add_convert_fusion.1), channel_id=1, source_target_pairs={{0,16},{4,20},{8,24},{12,28},{16,0},{20,4},{24,8},{28,12},{1,17},{... | collective-permute-start | bytes 835592 | tf_op jit(solution)/shard_map/ppermute | solution.py:313
  99.2 2.1 %collective-permute-start.11 = (f32[136,1024]{1,0:T(8,128)S(1)}, f32[136,1024]{1,0:T(8,128)S(1)}, u32[]{:S(2)}, u32[]{:S(2)}) collective-permute-start(f32[136,1024]{1,0:T(8,128)S(1)} %convert_add_fusion), channel_id=1, source_target_pairs={{0,4},{4,0},{8,12},{12,8},{16,20},{20,16},{24,28},{28,24},{1,5},{5... | collective-permute-start | bytes 1671176 | tf_op jit(solution)/shard_map/ppermute | solution.py:313

commit v2 on v0

v2 whole, which is shorter than its diff:
```python
import math

import jax
import jax.numpy as jnp
import numpy as np
from jax import lax
from jax.experimental import pallas as pl
from jax.experimental.pallas import tpu as pltpu
from jax.sharding import PartitionSpec as P

F32 = jnp.float32
BF16 = jnp.bfloat16
VMEM_LIMIT = 16 * 1024 * 1024
BLOCK = 1024
BRIEF = pl.CostEstimate(flops=1000, bytes_accessed=1000, transcendentals=0)
LONG = pl.CostEstimate(flops=20_000_000_000, bytes_accessed=100_000_000, transcendentals=0)


STRIP = 16


def strips(rows):
    return [slice(i, i + STRIP) for i in range(0, rows, STRIP)]


def put_halves(x, high_ref, low_ref, rows):
    high = x.astype(BF16)
    high_ref[rows] = high
    low_ref[rows] = (x - high.astype(F32)).astype(BF16)


def stacked_rows(high_ref, low_ref, rows=slice(None)):
    high = high_ref[rows]
    return jnp.concatenate([high, high, low_ref[rows]], axis=0)


def product(matrix, x):
    return jnp.dot(matrix, x, preferred_element_type=F32)


def transforms(extent):
    points = 2 * extent
    angle = np.pi * np.outer(2 * np.arange(extent) + 1, np.arange(points)) / points
    whole = np.concatenate([np.cos(angle), -np.sin(angle)])
    back = whole.T / extent

    def split(matrix, terms=3):
        high = matrix.astype(jnp.bfloat16)
        low = (matrix - high.astype(np.float64)).astype(jnp.bfloat16)
        return np.concatenate([high, low, high][:terms], axis=1)

    return {
        "both": split(whole, 2),
        "short": split(whole[:, :extent]),
        "inverse": split(np.concatenate([-back[extent:], back[:extent]])),
        "around": split(-back[extent - 8 :]),
    }


def delayed(before, x, by):
    return pltpu.roll(jnp.concatenate([before, x], axis=0), by, 0)[8:]


def advanced(x, after, by):
    both = jnp.concatenate([x, after], axis=0)
    return pltpu.roll(both, both.shape[0] - by, 0)[: x.shape[0]]


def folded(x):
    return sum(x[i : i + 8] for i in range(8, x.shape[0], 8)) + x[:8]


def filtered(u, before, taps):
    value = taps[0] * u
    for j in range(1, len(taps)):
        value = value + taps[j] * delayed(before, u, j)
    return value


def convolved(matrix, spectrum, hs_ref, high_ref, low_ref):
    for at in strips(hs_ref.shape[0] // 2):
        im = slice(at.start + hs_ref.shape[0] // 2, at.stop + hs_ref.shape[0] // 2)
        ur, ui, hr, hi = spectrum[at], spectrum[im], hs_ref[at], hs_ref[im]
        put_halves(ur * hr - ui * hi, high_ref, low_ref, at)
        put_halves(ur * hi + ui * hr, high_ref, low_ref, im)
    return product(matrix, stacked_rows(high_ref, low_ref))


def twice(x):
    return jnp.concatenate([x, x], axis=0)


def signal_kernel(
    u_ref, halo_ref, h_ref, w_ref, both_ref, short_ref, around_ref, us_ref, hs_ref, z_ref, *scratch
):
    high_h, low_h, high_p, low_p, p_ref = scratch
    extent = h_ref.shape[0]
    lead, width = halo_ref.shape
    blocks = us_ref.shape[0]
    for at in strips(extent):
        put_halves(-h_ref[at], high_h, low_h, at)
    hs_ref[...] = product(short_ref[...], stacked_rows(high_h, low_h))
    for b in range(blocks):
        last = u_ref[b * extent : (b + 1) * extent]
        first = halo_ref[lead - extent :] if b == 0 else u_ref[(b - 1) * extent : b * extent]
        us_ref[b] = product(both_ref[...], jnp.concatenate([first, last] * 2, axis=0))
    for b in range(blocks):
        matrix = around_ref[...] if b == 0 else around_ref[8:]
        rows = slice(0, extent + 8) if b == 0 else slice(8 + b * extent, 8 + (b + 1) * extent)
        p_ref[rows] = convolved(matrix, us_ref.at[b], hs_ref, high_p.at[b], low_p.at[b])
    ahead = halo_ref[lead - extent - STRIP : lead - extent].astype(F32)[STRIP - 1 :]
    final = u_ref[extent - STRIP : extent].astype(F32)[STRIP - 1 :]
    mend = h_ref[extent - 1 : extent] * (ahead + final)
    at_second = lax.broadcasted_iota(jnp.int32, (8, width), 0) == 6
    before = p_ref[:8] + jnp.where(at_second, mend, 0.0)
    w = [w_ref[i : i + 1] for i in range(w_ref.shape[0])]
    for at in strips(z_ref.shape[0]):
        p = p_ref[8 + at.start : 8 + at.stop]
        z_ref[at] = filtered(p, before, w)
        before = p[-8:]


def sums_kernel(
    scale, g_ref, u_ref, halo_ref, h_ref, us_ref, z_ref, gate_ref, w_ref, short_ref, inverse_ref,
    d_ref, dq_ref, sums_ref, *scratch
):
    high_d, low_d, high_c, low_c = scratch
    extent = h_ref.shape[0]
    rows, width = u_ref.shape
    taps = gate_ref.shape[0]
    blocks = rows // extent
    gate = [gate_ref[i : i + 1] for i in range(taps)]
    w = [w_ref[i : i + 1] for i in range(taps)]
    gate_sums = [jnp.zeros((8, width), F32) for _ in range(taps)]
    ahead = halo_ref[halo_ref.shape[0] - STRIP :].astype(F32)
    before = ahead[8:]
    first = halo_ref[halo_ref.shape[0] - extent - STRIP : halo_ref.shape[0] - extent].astype(F32)
    preceding = [first[STRIP - 1 :], ahead[STRIP - 1 :]]
    mend = None
    for at in strips(rows):
        g, u = g_ref[at].astype(F32), u_ref[at].astype(F32)
        late = [u] + [delayed(before, u, i) for i in range(1, taps)]
        before = u[8:]
        q = gate[0] * u
        for i in range(1, taps):
            q = q + gate[i] * late[i]
        dz, dq = g * q, g * z_ref[at]
        dq_ref[at] = dq
        put_halves(dz, high_d, low_d, at)
        gate_sums = [total + folded(dq * x) for total, x in zip(gate_sums, late)]
        if at.start % extent == 0:
            b, start = at.start // extent, dz[:1]
            if b >= 2:
                preceding.append(u_ref[(b - 1) * extent - STRIP : (b - 1) * extent].astype(F32)[STRIP - 1 :])
        if at.stop % extent == 0:
            term = start * (u[STRIP - 1 :] + preceding[b])
            mend = term if mend is None else mend + term
    for b in range(blocks):
        window = slice(b * extent, (b + 1) * extent)
        d_ref[b] = product(short_ref[...], stacked_rows(high_d, low_d, window))
    for at in strips(extent):
        im = slice(extent + at.start, extent + at.stop)
        cr = ci = None
        for b in range(blocks):
            dr, di, ur, ui = d_ref[b, at], d_ref[b, im], us_ref[b, at], us_ref[b, im]
            real, imaginary = dr * ur + di * ui, di * ur - dr * ui
            cr, ci = (real, imaginary) if cr is None else (cr + real, ci + imaginary)
        put_halves(cr, high_c, low_c, at)
        put_halves(ci, high_c, low_c, im)
    lags = product(inverse_ref[: extent + 8], stacked_rows(high_c, low_c)) * scale
    at_last = lax.broadcasted_iota(jnp.int32, (8, width), 0) == 1
    after = lags[extent:] + jnp.where(at_last, mend * scale, 0.0)
    value_sums = [jnp.zeros((8, width), F32) for _ in range(taps)]
    for row in range(extent - STRIP, -1, -STRIP):
        c = lags[row : row + STRIP]
        early = [c] + [advanced(c, after, i) for i in range(1, taps)]
        after = c[:8]
        total = w[0] * c
        for i in range(1, taps):
            total = total + w[i] * early[i]
        sums_ref[row : row + STRIP] = total
        h = h_ref[row : row + STRIP]
        value_sums = [sums + folded(h * x) for sums, x in zip(value_sums, early)]
    rest = [jnp.sum(x, axis=0, keepdims=True) * scale for x in gate_sums]
    rest += [jnp.sum(x, axis=0, keepdims=True) for x in value_sums]
    spare = sums_ref.shape[0] - extent - 2 * taps
    rest.append(jnp.zeros((spare, width), F32))
    sums_ref[extent:] = jnp.concatenate(rest, axis=0)


def input_kernel(
    lead, d_ref, dq_ref, hs_ref, gate_ref, w_ref, inverse_ref, grad_ref, end_ref, head_ref, *scratch
):
    high_r, low_r, r_ref = scratch
    extent = hs_ref.shape[0] // 2
    rows, width = dq_ref.shape
    taps = gate_ref.shape[0]
    blocks = rows // extent
    for at in strips(extent):
        im = slice(extent + at.start, extent + at.stop)
        hr, hi = hs_ref[at], hs_ref[im]
        for b in range(blocks):
            dr, di = d_ref[b, at], d_ref[b, im]
            put_halves(dr * hr + di * hi, high_r.at[b], low_r.at[b], at)
            put_halves(di * hr - dr * hi, high_r.at[b], low_r.at[b], im)
    for b in range(blocks):
        r_ref[b] = product(inverse_ref[...], stacked_rows(high_r.at[b], low_r.at[b]))
    w = [-w_ref[i : i + 1] for i in range(taps)]
    gate = [gate_ref[i : i + 1] for i in range(taps)]
    nothing = jnp.zeros((STRIP, width), F32)
    after_r = after_dq = nothing[:8]
    for row in range(rows - STRIP, -lead - 1, -STRIP):
        block, at = (row + extent) // extent, (row + extent) % extent
        if row < -extent:
            r = nothing
        elif block == 0:
            r = r_ref[0, at : at + STRIP]
        elif block == blocks:
            r = r_ref[blocks - 1, extent + at : extent + at + STRIP]
        else:
            r = r_ref[block - 1, extent + at : extent + at + STRIP] + r_ref[block, at : at + STRIP]
        total = w[0] * r
        for i in range(1, taps):
            total = total + w[i] * advanced(r, after_r, i)
        after_r = r[:8]
        if row >= -STRIP:
            dq = dq_ref[row : row + STRIP] if row >= 0 else nothing
            if row >= 0:
                total = total + gate[0] * dq
            for i in range(1, taps):
                total = total + gate[i] * advanced(dq, after_dq, i)
            after_dq = dq[:8]
        if row < 0:
            head_ref[lead + row : lead + row + STRIP] = total.astype(BF16)
        elif row < rows - lead:
            grad_ref[row : row + STRIP] = total.astype(BF16)
        else:
            end_ref[row - rows + lead : row - rows + lead + STRIP] = total


IN_VMEM = pl.BlockSpec(memory_space=pltpu.VMEM)
IN_SMEM = pl.BlockSpec(memory_space=pltpu.SMEM)
ANYWHERE = pl.BlockSpec(memory_space=pl.ANY)


def place_of(me_ref, k, pieces, piece):
    return pl.ds(pl.multiple_of(lax.rem(me_ref[0] + (pieces - k), pieces) * piece, piece), piece)


def call(name, body, inputs, constants, outs, scratch, block, cost, me, pieces=()):
    moved = [isinstance(x, list) for x in inputs]
    arrays = [x[0] if isinstance(x, list) else x for x in inputs]
    put = [isinstance(x, list) for x in outs]
    shapes = [x[0] if isinstance(x, list) else x for x in outs]
    width = shapes[0].shape[-1]
    blocks = width // block
    n_pieces, n_in, n_const, n_out = len(pieces), len(arrays), len(constants), len(shapes)
    held = [x for x, move in zip(arrays, moved) if move] + list(constants)
    held += [x for x, move in zip(shapes, put) if move]
    if pieces:
        held.append(jax.ShapeDtypeStruct((n_pieces * pieces[0].shape[0], width), pieces[0].dtype))

    def kernel(*refs):
        me_ref, piece_refs, refs = refs[0], refs[1 : 1 + n_pieces], refs[1 + n_pieces :]
        given, refs = refs[: n_in + n_const], refs[n_in + n_const :]
        results, refs = refs[:n_out], refs[n_out:]
        temporary, kept, sems, const_sems = refs[: len(scratch)], list(refs[len(scratch) : -2]), *refs[-2:]
        ins, sources, sinks = [], [], []
        for ref, move in zip(given, moved):
            ins.append(kept.pop(0) if move else ref)
            if move:
                sources.append((ref, ins[-1]))
        whole = [kept.pop(0) for _ in range(n_const)]
        shown = []
        for ref, move in zip(results, put):
            shown.append(kept.pop(0) if move else ref)
            if move:
                sinks.append((shown[-1], ref))
        if pieces:
            ins.insert(0, kept.pop(0))
            sources += [
                (ref, ins[0].at[place_of(me_ref, k, n_pieces, ref.shape[0])]) for k, ref in enumerate(piece_refs)
            ]

        def cut(ref, j):
            place = pl.ds(pl.multiple_of(j * block, block), block)
            return ref.at[(slice(None),) * (len(ref.shape) - 1) + (place,)]

        def copies(pairs, j, first):
            return [
                pltpu.make_async_copy(cut(a, j), cut(b, j), sems.at[first + i, j]) for i, (a, b) in enumerate(pairs)
            ]

        constant_copies = [
            pltpu.make_async_copy(a, b, const_sems.at[i]) for i, (a, b) in enumerate(zip(given[n_in:], whole))
        ]
        for copy in constant_copies:
            copy.start()
        for j in range(blocks):
            for copy in copies(sources, j, 0):
                copy.start()
        for copy in constant_copies:
            copy.wait()

        def one(j):
            for copy in copies(sources, j, 0):
                copy.wait()
            body(*[cut(x, j) for x in ins], *whole, *[cut(x, j) for x in shown], *temporary)
            for copy in copies(sinks, j, len(sources)):
                copy.start()

        pl.loop(0, blocks)(one)
        for j in range(blocks):
            for copy in copies(sinks, j, len(sources)):
                copy.wait()

    return pl.pallas_call(
        kernel,
        in_specs=[IN_SMEM]
        + [ANYWHERE] * n_pieces
        + [ANYWHERE if move else IN_VMEM for move in moved]
        + [ANYWHERE] * n_const,
        out_specs=[ANYWHERE if move else IN_VMEM for move in put],
        scratch_shapes=[pltpu.VMEM(shape, dtype) for shape, dtype in scratch]
        + [pltpu.VMEM(x.shape, x.dtype) for x in held]
        + [
            pltpu.SemaphoreType.DMA((n_pieces + sum(moved) + sum(put) + 1, blocks)),
            pltpu.SemaphoreType.DMA((n_const,)),
        ],
        out_shape=shapes,
        compiler_params=pltpu.CompilerParams(vmem_limit_bytes=VMEM_LIMIT),
        cost_estimate=cost,
        name=name,
    )(me, *pieces, *arrays, *constants)


def tail_step(pieces, me, lead):
    piece, width = pieces[0].shape
    rows = piece * len(pieces)

    def kernel(me_ref, *refs):
        tail_ref, held, sems, sem = refs[len(pieces) :]
        copies = [
            pltpu.make_async_copy(ref, held.at[place_of(me_ref, k, len(pieces), piece)], sems.at[k])
            for k, ref in enumerate(refs[: len(pieces)])
        ]
        for copy in copies:
            copy.start()
        for copy in copies:
            copy.wait()
        out = pltpu.make_async_copy(held.at[pl.ds(rows - lead, lead), :], tail_ref, sem)
        out.start()
        out.wait()

    return pl.pallas_call(
        kernel,
        in_specs=[IN_SMEM] + [ANYWHERE] * len(pieces),
        out_specs=ANYWHERE,
        scratch_shapes=[
            pltpu.VMEM((rows, width), BF16),
            pltpu.SemaphoreType.DMA((len(pieces),)),
            pltpu.SemaphoreType.DMA,
        ],
        out_shape=jax.ShapeDtypeStruct((lead, width), BF16),
        compiler_params=pltpu.CompilerParams(vmem_limit_bytes=VMEM_LIMIT),
        cost_estimate=BRIEF,
        name="tail_step",
    )(me, *pieces)


def signal_step(u_pieces, me, halo, h, w, matrices, block):
    width = h.shape[1]
    rows, extent = u_pieces[0].shape[0] * len(u_pieces), h.shape[0]
    blocks = rows // extent
    outs = [
        jax.ShapeDtypeStruct((blocks, 2 * extent, width), F32),
        jax.ShapeDtypeStruct((2 * extent, width), F32),
        jax.ShapeDtypeStruct((rows, width), F32),
        jax.ShapeDtypeStruct((rows, width), BF16),
    ]
    scratch = [((extent, block), BF16)] * 2 + [((blocks, 2 * extent, block), BF16)] * 2
    scratch += [((8 + rows, block), F32)]
    constants = [matrices[name] for name in ("both", "short", "around")]

    def body(u_ref, *refs):
        refs[9][...] = u_ref[...]
        signal_kernel(u_ref, *refs[:9], *refs[10:])

    return call(
        "signal_step", body, [[halo], [h], [w]], constants, outs, scratch, block, BRIEF, me, u_pieces
    )


def gradient_step(g_pieces, me, u, halo, h, us, hs, z, gate, w, matrices, scale, block):
    rows, width = u.shape
    extent, taps, lead = h.shape[0], gate.shape[0], halo.shape[0]
    blocks = rows // extent
    outs = [
        jax.ShapeDtypeStruct((extent + -(-2 * taps // 8) * 8, width), F32),
        jax.ShapeDtypeStruct((rows - lead, width), BF16),
        jax.ShapeDtypeStruct((lead, width), F32),
        jax.ShapeDtypeStruct((lead, width), BF16),
    ]
    spectra = (blocks, 2 * extent, block)
    scratch = [(spectra, F32), ((rows, block), F32)]
    scratch += [((rows, block), BF16)] * 2 + [((2 * extent, block), BF16)] * 2
    scratch += [(spectra, BF16)] * 2 + [(spectra, F32)]

    def body(g, u, halo, h, us, hs, z, gate, w, short, inverse, sums, grad, end, head, d, dq, *temporary):
        sums_kernel(scale, g, u, halo, h, us, z, gate, w, short, inverse, d, dq, sums, *temporary[:4])
        input_kernel(lead, d, dq, hs, gate, w, inverse, grad, end, head, *temporary[4:])

    return call(
        "gradient_step", body, [u, [halo], [h], us, hs, z, [gate], [w]],
        [matrices[name] for name in ("short", "inverse")], outs, scratch, block, LONG, me, g_pieces,
    )


def slices(x, axis, start, part):
    count = lax.axis_size(axis)
    me = lax.axis_index(axis)
    width = x.shape[1] // count
    return [
        lax.dynamic_slice_in_dim(x, lax.rem(me + k, count) * width + start, part, axis=1)
        for k in range(count)
    ]


def exchange(pieces, axis):
    count = lax.axis_size(axis)
    got = [pieces[0]] + [None] * (count - 1)
    for k in sorted(range(1, count), key=lambda k: abs(2 * k - count)):
        got[k] = lax.ppermute(pieces[k], axis, [(i, (i + k) % count) for i in range(count)])
    return got


def shifted(x, axis, by):
    count = lax.axis_size(axis)
    pairs = [(i, i + by) for i in range(count) if 0 <= i + by < count]
    return lax.ppermute(x, axis, pairs)


def at_once(exchange_of, x, axis):
    return lax.cond(lax.axis_index(axis) >= 0, exchange_of, lambda x: x, x)


def partner(x, axis, bit):
    count = lax.axis_size(axis)
    return lax.ppermute(x, axis, [(i, i ^ bit) for i in range(count)])


def summed(x, axis):
    total, bit, count = x + partner(x, axis, 1), 2, lax.axis_size(axis)
    while bit < count:
        short = total.astype(BF16)
        total = short.astype(F32) + partner(short, axis, bit).astype(F32)
        bit *= 2
    return total


def finish_step(terms, mine, sizes):
    part = terms[0].shape[1]
    width = part * len(terms)

    def kernel(mine_ref, *refs):
        terms, outs, held, sems = refs[:4], refs[4 : 4 + len(sizes)], refs[4 + len(sizes) : -1], refs[-1]
        copies = []
        for k, term in enumerate(terms):
            place = pl.ds(pl.multiple_of((mine_ref[0] ^ k) * part, part), part)
            x, row = term[...].astype(F32), 0
            for i, (size, out, ref) in enumerate(zip(sizes, outs, held)):
                ref[:, place] = x[row : row + size]
                row += size
                copies.append(pltpu.make_async_copy(ref.at[:, place], out.at[:, place], sems.at[i, k]))
                copies[-1].start()
        for copy in copies:
            copy.wait()

    return pl.pallas_call(
        kernel,
        in_specs=[IN_SMEM] + [IN_VMEM] * 4,
        out_specs=[ANYWHERE] * len(sizes),
        scratch_shapes=[pltpu.VMEM((size, width), F32) for size in sizes]
        + [pltpu.SemaphoreType.DMA((len(sizes), 4))],
        out_shape=[jax.ShapeDtypeStruct((size, width), F32) for size in sizes],
        compiler_params=pltpu.CompilerParams(vmem_limit_bytes=VMEM_LIMIT),
        cost_estimate=BRIEF,
        name="finish_step",
    )(mine, *terms)


def shards(out_grad, saved_input, explicit_filter_weights, gate_taps, value_featurizer_weights):
    extent, width = explicit_filter_weights.shape
    taps = gate_taps.shape[0]
    me = lax.axis_index("tp").astype(jnp.int32).reshape(1)
    rows = out_grad.shape[0] * lax.axis_size("tp")
    lead = -(-(extent + taps - 2) // 16) * 16
    block = min(BLOCK, width)
    matrices = {name: jnp.asarray(m) for name, m in transforms(extent).items()}
    scale = 1.0 / math.sqrt(rows * lax.axis_size("ctx"))
    h, gate, w = explicit_filter_weights, gate_taps, value_featurizer_weights
    u_pieces = exchange(slices(saved_input, "tp", 0, width), "tp")
    g_slices = slices(out_grad, "tp", 0, width)
    u_pieces, g_slices = lax.optimization_barrier((u_pieces, g_slices))
    g_pieces = exchange(g_slices, "tp")
    tail = tail_step(u_pieces, me, lead)
    halo = at_once(lambda x: shifted(x, "ctx", 1), tail, "ctx")
    us, hs, z, u = signal_step(u_pieces, me, halo, h, w, matrices, block)
    partial, main, end, head = gradient_step(
        g_pieces, me, u, halo, h, us, hs, z, gate, w, matrices, scale, block
    )
    incoming = shifted(head, "ctx", -1)
    sizes = (extent, taps, taps)
    if lax.axis_size("ctx") == 8:
        mine = (lax.axis_index("ctx") // 2).astype(jnp.int32)
        part = width // 4
        quarters = [lax.dynamic_slice_in_dim(partial, (mine ^ k) * part, part, axis=1) for k in range(4)]
        got = [partner(quarters[k].astype(BF16), "ctx", 2 * k) for k in range(1, 4)]
        total = (quarters[0] + got[0].astype(F32)) + (got[1].astype(F32) + got[2].astype(F32))
        total = total + partner(total, "ctx", 1)
        total, incoming = lax.optimization_barrier((total, incoming))
        total = total.astype(BF16)
        terms = [total] + [partner(total, "ctx", 2 * k) for k in range(1, 4)]
        sums = finish_step(terms, mine.reshape(1), sizes)
    else:
        total = summed(partial, "ctx")
        ends = np.cumsum(sizes)
        sums = [total[stop - size : stop] for size, stop in zip(sizes, ends)]
    end = (end + incoming.astype(F32)).astype(BF16)
    return (jnp.concatenate([main, end], axis=0), *sums)


def solution(mesh):
    placed = (
        P(("ctx", "tp"), None),
        P(("ctx", "tp"), None),
        P(None, "tp"),
        P(None, "tp"),
        P(None, "tp"),
    )
    return jax.shard_map(
        shards,
        mesh=mesh,
        in_specs=placed,
        out_specs=(P("ctx", "tp"), P(None, "tp"), P(None, "tp"), P(None, "tp")),
        check_vma=False,
    )
```

time: 361 us -> 90.3 us (0.25); the launches traced: 357 us -> 90 us
  matrix products: 112 us -> 0 us
  local copies, waits for them, and re-layouts: 108 us -> 5.83 us
  waiting for transfers between devices: 64.6 us -> 32.5 us
  blocking collectives: 26.6 us -> 0 us
  starting transfers between devices: 9.98 us -> 31.3 us
  other arithmetic: 20.7 us -> 2.25 us
  Pallas kernels: 0 us -> 17.3 us
  between operations: 14.7 us -> 0.87 us
    conv_general_dilated x8 -> x0, matrix products: 111 us -> none  [depthwise(): lax.conv_general_dilated(signal[None], kernel[:, None, :], (1,), 'VALID',...]
    all_to_all x1 -> x0, waiting for transfers between devices: 34.8 us -> none  [shards(): lax.all_to_all(stacked, 'tp', split_axis=2, concat_axis=1, tiled=True)]
    ppermute x2 -> x15, waiting for transfers between devices: 0.01 us -> 32.5 us  [the longest x6 19.3 us: exchange(): lax.ppermute(pieces[k], axis, [(i, (i + k) % count) for i in range(count)])]
    conv_general_dilated x10 -> x0, local copies, waits for them, and re-layouts: 32.3 us -> none  [depthwise(): lax.conv_general_dilated(signal[None], kernel[:, None, :], (1,), 'VALID',...]
    psum x1 -> x0, waiting for transfers between devices: 29.8 us -> none  [shards(): lax.psum((explicit_filter_term, gate_part, value_part), 'ctx')]
    ppermute x2 -> x15, starting transfers between devices: 3.53 us -> 31.3 us  [the longest x6 15.5 us: exchange(): lax.ppermute(pieces[k], axis, [(i, (i + k) % count) for i in range(count)])]
    psum x1 -> x0, blocking collectives: 26.6 us -> none  [shards(): lax.psum((explicit_filter_term, gate_part, value_part), 'ctx')]
    pallas_call x0 -> x4, Pallas kernels: none -> 17.3 us  [the longest x2 15.2 us: call(): pl.pallas_call(kernel, in_specs=[IN_SMEM] + [ANYWHERE] * n_pieces + [ANYW...]
  transfers between devices with their start and end apart: 4 -> 15, of which waited for: 2 -> 10; matrix products, arithmetic and copies ran while one was open for 10% -> 4% of each run, Pallas kernels for 0% -> 7%
where the time goes in v2:
time: 90.3 us; the launch traced here: 90 us
  waiting for transfers between devices  32.5 us (36%)
  starting transfers between devices  31.3 us (35%)
  Pallas kernels  17.3 us (19%)
  local copies, waits for them, and re-layouts  5.83 us (6%)
  other arithmetic  2.25 us (2%)
    ppermute x6, waiting for transfers between devices, exchange(): lax.ppermute(pieces[k], axis, [(i, (i + k) % count) for i in range(count)])  19.3 us
    ppermute x6, starting transfers between devices, exchange(): lax.ppermute(pieces[k], axis, [(i, (i + k) % count) for i in range(count)])  15.5 us
    pallas_call x2, Pallas kernels, call(): pl.pallas_call(kernel, in_specs=[IN_SMEM] + [ANYWHERE] * n_pieces + [ANYW...  15.2 us
    ppermute x7, starting transfers between devices, partner(): return lax.ppermute(x, axis, [(i, i ^ bit) for i in range(count)])  13.1 us
    ppermute x7, waiting for transfers between devices, partner(): return lax.ppermute(x, axis, [(i, i ^ bit) for i in range(count)])  11.5 us
    unnamed x24, local copies, waits for them, and re-layouts  2.68 us
    ppermute x2, starting transfers between devices, shifted(): return lax.ppermute(x, axis, pairs)  2.68 us
    dynamic_slice x2, local copies, waits for them, and re-layouts, slices(): lax.dynamic_slice_in_dim(x, lax.rem(me + k, count) * width + start, part,...  2.28 us
  transfers between devices with their start and end apart: 15, of which 10 were waited for; matrix products, arithmetic and copies ran while one was open for 4% of the time, Pallas kernels for 7%

profile of v2, /device:TPU:0, one launch (start us, length us, event | category | flops | bytes accessed | tf_op | source)
XLA Modules:
  0.0 90.0 jit_solution(10983688299456627114)
XLA Ops:
  0.7 1.4 %constant_dynamic-slice_fusion.4 = (bf16[64,2048]{1,0:T(8,128)(2,1)S(1)}, bf16[64,2048]{1,0:T(8,128)(2,1)S(1)}, bf16[64,2048]{1,0:T(8,128)(2,1)S(1)}, bf16[64,2048]{1,0:T(8,128)(2,1)S(1)}) fusion(bf16[64,8192]{1,0:T(8,128)(2,1)} %param.12, s32[]{:T(128)S(6)} %select_n.36, s32[]{:T(128)S(6)} %select_n.34, s32[]{:T(128)S(6)} %select_n.33, s32[]{:T(128)S(6)} %select_n.35), kind=kLoop, calls=%fused_computation.10 | loop fusion | bytes 2097168 | tf_op jit(solution)/shard_map/dynamic_slice | solution.py:424
  2.0 3.1 %collective-permute-start.1 = (bf16[64,2048]{1,0:T(8,128)(2,1)S(1)}, bf16[64,2048]{1,0:T(8,128)(2,1)S(1)}, u32[]{:S(2)}, u32[]{:S(2)}) collective-permute-start(bf16[64,2048]{1,0:T(8,128)(2,1)S(1)} %get-tuple-element.59), channel_id=1, source_target_pairs={{0,1},{1,2},{2,3},{3,0},{4,5},{5,6},{6,7},{7,4},{8,9},{9,10},{10,1... | collective-permute-start | bytes 786440 | tf_op jit(solution)/shard_map/ppermute | solution.py:433
  5.1 2.6 %collective-permute-start.2 = (bf16[64,2048]{1,0:T(8,128)(2,1)S(1)}, bf16[64,2048]{1,0:T(8,128)(2,1)S(1)}, u32[]{:S(2)}, u32[]{:S(2)}) collective-permute-start(bf16[64,2048]{1,0:T(8,128)(2,1)S(1)} %get-tuple-element.61), channel_id=1, source_target_pairs={{0,2},{1,3},{2,0},{3,1},{4,6},{5,7},{6,4},{7,5},{8,10},{9,11},{10,... | collective-permute-start | bytes 786440 | tf_op jit(solution)/shard_map/ppermute | solution.py:433
  7.7 1.3 %collective-permute-start.3 = (bf16[64,2048]{1,0:T(8,128)(2,1)S(1)}, bf16[64,2048]{1,0:T(8,128)(2,1)S(1)}, u32[]{:S(2)}, u32[]{:S(2)}) collective-permute-start(bf16[64,2048]{1,0:T(8,128)(2,1)S(1)} %get-tuple-element.58), channel_id=1, source_target_pairs={{0,3},{1,0},{2,1},{3,2},{4,7},{5,4},{6,5},{7,6},{8,11},{9,8},{10,9... | collective-permute-start | bytes 786440 | tf_op jit(solution)/shard_map/ppermute | solution.py:433
  9.1 0.9 %constant_dynamic-slice_fusion = (bf16[64,2048]{1,0:T(8,128)(2,1)}, bf16[64,2048]{1,0:T(8,128)(2,1)}, bf16[64,2048]{1,0:T(8,128)(2,1)S(1)}, bf16[64,2048]{1,0:T(8,128)(2,1)}) fusion(bf16[64,8192]{1,0:T(8,128)(2,1)S(1)} %copy-done.11, s32[]{:T(128)S(6)} %select_n.36, s32[]{:T(128)S(6)} %select_n.34, s32[]{:T(128)S(6)} %select_n.33, s32[]{:T(128)S(6)} %select_n.35), kind=kLoop, calls=%fused_computation.6 | loop fusion | bytes 2097168 | tf_op jit(solution)/shard_map/dynamic_slice | solution.py:424
  10.0 4.5 %collective-permute-done.1.refs_1_.refs_2_ = bf16[64,2048]{1,0:T(8,128)(2,1)S(1)} collective-permute-done((bf16[64,2048]{1,0:T(8,128)(2,1)S(1)}, bf16[64,2048]{1,0:T(8,128)(2,1)S(1)}, u32[]{:S(2)}, u32[]{:S(2)}) %collective-permute-start.1) | collective-permute-done | bytes 262176 | tf_op jit(solution)/shard_map/ppermute | solution.py:433
  14.4 10.4 %collective-permute-done.2.refs_2_.refs_3_ = bf16[64,2048]{1,0:T(8,128)(2,1)S(1)} collective-permute-done((bf16[64,2048]{1,0:T(8,128)(2,1)S(1)}, bf16[64,2048]{1,0:T(8,128)(2,1)S(1)}, u32[]{:S(2)}, u32[]{:S(2)}) %collective-permute-start.2) | collective-permute-done | bytes 262176 | tf_op jit(solution)/shard_map/ppermute | solution.py:433
  24.8 6.1 %collective-permute-start.4 = (bf16[64,2048]{1,0:T(8,128)(2,1)}, bf16[64,2048]{1,0:T(8,128)(2,1)S(1)}, u32[]{:S(2)}, u32[]{:S(2)}) collective-permute-start(bf16[64,2048]{1,0:T(8,128)(2,1)} %get-tuple-element.31), channel_id=1, source_target_pairs={{0,1},{1,2},{2,3},{3,0},{4,5},{5,6},{6,7},{7,4},{8,9},{9,10},{10,1... | collective-permute-start | bytes 786440 | tf_op jit(solution)/shard_map/ppermute | solution.py:433
  30.9 1.6 %collective-permute-start.5 = (bf16[64,2048]{1,0:T(8,128)(2,1)}, bf16[64,2048]{1,0:T(8,128)(2,1)}, u32[]{:S(2)}, u32[]{:S(2)}) collective-permute-start(bf16[64,2048]{1,0:T(8,128)(2,1)} %get-tuple-element.32), channel_id=1, source_target_pairs={{0,2},{1,3},{2,0},{3,1},{4,6},{5,7},{6,4},{7,5},{8,10},{9,11},{10,... | collective-permute-start | bytes 786440 | tf_op jit(solution)/shard_map/ppermute | solution.py:433
  33.3 1.0 %tail_step.1 = bf16[144,2048]{1,0:T(8,128)(2,1)} custom-call(s32[1]{0:T(128)} %bitcast.me_ref.refs_0_, bf16[64,2048]{1,0:T(8,128)(2,1)S(1)} %get-tuple-element.34.refs_0_.refs_1_, bf16[64,2048]{1,0:T(8,128)(2,1)S(1)} %collective-permute-done.1.refs_1_.refs_2_, bf16[64,2048]{1,0:T(8,128)(2,1)S(1)} %collective-permute-done.2.refs_2_.refs_3_, ...), custom_call_target="tpu_custom_call" | custom-call | flops 1000 | bytes 1000 | tf_op jit(solution)/shard_map/tail_step/pallas_call | solution.py:355
  34.3 4.0 %conditional.1 = (bf16[144,2048]{1,0:T(8,128)(2,1)}) conditional(s32[]{:T(128)} %convert_element_type.30, bf16[144,2048]{1,0:T(8,128)(2,1)} %tail_step.1, bf16[144,2048]{1,0:T(8,128)(2,1)} %tail_step.1), branch_computations={%region_0.0_spmd, %region_1.0_spmd} | conditional | bytes 3538992 | solution.py:444
  34.3 1.4 %collective-permute-start = (bf16[144,2048]{1,0:T(8,128)(2,1)}, bf16[144,2048]{1,0:T(8,128)(2,1)S(1)}, u32[]{:S(2)}, u32[]{:S(2)}) collective-permute-start(bf16[144,2048]{1,0:T(8,128)(2,1)} %param.1), channel_id=1, source_target_pairs={{0,4},{4,8},{8,12},{12,16},{16,20},{20,24},{24,28},{1,5},{5,9},{9,... | collective-permute-start | bytes 1769480 | tf_op jit(solution)/shard_map/cond/branch_1_fun/ppermute | solution.py:440
  35.7 1.8 %collective-permute-done = bf16[144,2048]{1,0:T(8,128)(2,1)S(1)} collective-permute-done((bf16[144,2048]{1,0:T(8,128)(2,1)}, bf16[144,2048]{1,0:T(8,128)(2,1)S(1)}, u32[]{:S(2)}, u32[]{:S(2)}) %collective-permute-start) | collective-permute-done | bytes 589856 | tf_op jit(solution)/shard_map/cond/branch_1_fun/ppermute | solution.py:440
  38.3 5.6 %signal_step.1 = (f32[2,256,2048]{2,1,0:T(8,128)S(1)}, f32[256,2048]{1,0:T(8,128)S(1)}, f32[256,2048]{1,0:T(8,128)S(1)}, bf16[256,2048]{1,0:T(8,128)(2,1)S(1)}) custom-call(s32[1]{0:T(128)} %bitcast.me_ref.refs_0_, bf16[64,2048]{1,0:T(8,128)(2,1)S(1)} %get-tuple-element.34.refs_0_.refs_1_, bf16[64,2048]{1,0:T(8,128)(2,1)S(1)} %collective-permute-done.1.refs_1_.refs_2_, ...), custom_call_target="tpu_custom_call" | custom-call | flops 1000 | bytes 1000 | tf_op jit(solution)/shard_map/signal_step/pallas_call | solution.py:317
  44.7 4.4 %collective-permute-done.5.refs_3_ = bf16[64,2048]{1,0:T(8,128)(2,1)} collective-permute-done((bf16[64,2048]{1,0:T(8,128)(2,1)}, bf16[64,2048]{1,0:T(8,128)(2,1)}, u32[]{:S(2)}, u32[]{:S(2)}) %collective-permute-start.5) | collective-permute-done | bytes 262176 | tf_op jit(solution)/shard_map/ppermute | solution.py:433
  49.1 0.9 %copy-done.7 = bf16[64,2048]{1,0:T(8,128)(2,1)S(1)} copy-done((bf16[64,2048]{1,0:T(8,128)(2,1)S(1)}, bf16[64,2048]{1,0:T(8,128)(2,1)}, u32[]{:S(2)}) %copy-start.7) | copy-done | bytes 262168
  50.0 9.6 %gradient_step.1 = (f32[136,2048]{1,0:T(8,128)S(1)}, bf16[112,2048]{1,0:T(8,128)(2,1)S(1)}, f32[144,2048]{1,0:T(8,128)S(1)}, bf16[144,2048]{1,0:T(8,128)(2,1)}) custom-call(s32[1]{0:T(128)} %bitcast.me_ref.refs_0_, bf16[64,2048]{1,0:T(8,128)(2,1)S(1)} %get-tuple-element.30.refs_1_, bf16[64,2048]{1,0:T(8,128)(2,1)S(1)} %copy-done.7, ...), custom_call_target="tpu_custom_call" | custom-call | flops 20000000000 | bytes 100000000 | tf_op jit(solution)/shard_map/gradient_step/pallas_call | solution.py:317
  59.7 1.0 %copy-done.1 = f32[136,2048]{1,0:T(8,128)} copy-done((f32[136,2048]{1,0:T(8,128)}, f32[136,2048]{1,0:T(8,128)S(1)}, u32[]{:S(2)}) %copy-start.1) | copy-done | bytes 1114136
  60.7 5.4 %collective-permute-start.7 = (bf16[136,512]{1,0:T(8,128)(2,1)S(1)}, bf16[136,512]{1,0:T(8,128)(2,1)S(1)}, u32[]{:S(2)}, u32[]{:S(2)}) collective-permute-start(bf16[136,512]{1,0:T(8,128)(2,1)S(1)} %get-tuple-element.51), channel_id=1, source_target_pairs={{0,8},{4,12},{8,0},{12,4},{16,24},{20,28},{24,16},{28,20},{1,9},{5... | collective-permute-start | bytes 417800 | tf_op jit(solution)/shard_map/ppermute | solution.py:449
  66.1 1.5 %collective-permute-start.8 = (bf16[136,512]{1,0:T(8,128)(2,1)S(1)}, bf16[136,512]{1,0:T(8,128)(2,1)S(1)}, u32[]{:S(2)}, u32[]{:S(2)}) collective-permute-start(bf16[136,512]{1,0:T(8,128)(2,1)S(1)} %get-tuple-element.53), channel_id=1, source_target_pairs={{0,16},{4,20},{8,24},{12,28},{16,0},{20,4},{24,8},{28,12},{1,17},{... | collective-permute-start | bytes 417800 | tf_op jit(solution)/shard_map/ppermute | solution.py:449
  67.6 0.9 collective-permute-start.9
  68.5 1.3 %collective-permute-start.11 = (bf16[144,2048]{1,0:T(8,128)(2,1)}, bf16[144,2048]{1,0:T(8,128)(2,1)S(1)}, u32[]{:S(2)}, u32[]{:S(2)}) collective-permute-start(bf16[144,2048]{1,0:T(8,128)(2,1)} %get-tuple-element.45), channel_id=1, source_target_pairs={{4,0},{8,4},{12,8},{16,12},{20,16},{24,20},{28,24},{5,1},{9,5},{13... | collective-permute-start | bytes 1769480 | tf_op jit(solution)/shard_map/ppermute | solution.py:440
  70.0 2.8 %collective-permute-done.8 = bf16[136,512]{1,0:T(8,128)(2,1)S(1)} collective-permute-done((bf16[136,512]{1,0:T(8,128)(2,1)S(1)}, bf16[136,512]{1,0:T(8,128)(2,1)S(1)}, u32[]{:S(2)}, u32[]{:S(2)}) %collective-permute-start.8) | collective-permute-done | bytes 139296 | tf_op jit(solution)/shard_map/ppermute | solution.py:449
  73.6 1.0 %add_add_fusion = f32[136,512]{1,0:T(8,128)S(1)} fusion(bf16[136,512]{1,0:T(8,128)(2,1)S(1)} %collective-permute-done.9, bf16[136,512]{1,0:T(8,128)(2,1)S(1)} %collective-permute-done.8, bf16[136,512]{1,0:T(8,128)(2,1)S(1)} %collective-permute-done.7, f32[136,2048]{1,0:T(8,128)} %copy-done.1, s32[]{:T(128)S(6)} %select_n.38), kind=kLoop, calls=%fused_computation.2 | loop fusion | flops 417792 | bytes 974852 | tf_op jit(solution)/shard_map/add | solution.py:519
  74.7 1.5 %collective-permute-done.10 = f32[136,512]{1,0:T(8,128)S(1)} collective-permute-done((f32[136,512]{1,0:T(8,128)S(1)}, f32[136,512]{1,0:T(8,128)S(1)}, u32[]{:S(2)}, u32[]{:S(2)}) %collective-permute-start.10) | collective-permute-done | bytes 278560 | tf_op jit(solution)/shard_map/ppermute | solution.py:449
  76.3 2.9 %collective-permute-start.12 = (bf16[136,512]{1,0:T(8,128)(2,1)S(1)}, bf16[136,512]{1,0:T(8,128)(2,1)S(1)}, u32[]{:S(2)}, u32[]{:S(2)}) collective-permute-start(bf16[136,512]{1,0:T(8,128)(2,1)S(1)} %add.70.refs_0_), channel_id=1, source_target_pairs={{0,8},{4,12},{8,0},{12,4},{16,24},{20,28},{24,16},{28,20},{1,9},{5... | collective-permute-start | bytes 417800 | tf_op jit(solution)/shard_map/ppermute | solution.py:449
  79.2 1.5 %collective-permute-start.13 = (bf16[136,512]{1,0:T(8,128)(2,1)S(1)}, bf16[136,512]{1,0:T(8,128)(2,1)S(1)}, u32[]{:S(2)}, u32[]{:S(2)}) collective-permute-start(bf16[136,512]{1,0:T(8,128)(2,1)S(1)} %add.70.refs_0_), channel_id=1, source_target_pairs={{0,16},{4,20},{8,24},{12,28},{16,0},{20,4},{24,8},{28,12},{1,17},{... | collective-permute-start | bytes 417800 | tf_op jit(solution)/shard_map/ppermute | solution.py:449
  80.7 0.9 collective-permute-start.14
  81.7 1.1 %pad_maximum_fusion = bf16[256,2048]{1,0:T(8,128)(2,1)} fusion(bf16[144,2048]{1,0:T(8,128)(2,1)S(1)} %add_convert_fusion, bf16[112,2048]{1,0:T(8,128)(2,1)S(1)} %get-tuple-element.42), kind=kLoop, calls=%fused_computation.1 | loop fusion | flops 2097152 | bytes 2097152 | tf_op jit(solution)/shard_map/concatenate | solution.py:530
  82.8 4.9 %collective-permute-done.13.refs_2_ = bf16[136,512]{1,0:T(8,128)(2,1)S(1)} collective-permute-done((bf16[136,512]{1,0:T(8,128)(2,1)S(1)}, bf16[136,512]{1,0:T(8,128)(2,1)S(1)}, u32[]{:S(2)}, u32[]{:S(2)}) %collective-permute-start.13) | collective-permute-done | bytes 139296 | tf_op jit(solution)/shard_map/ppermute | solution.py:449
  87.7 1.2 %collective-permute-done.14.refs_3_ = bf16[136,512]{1,0:T(8,128)(2,1)S(1)} collective-permute-done((bf16[136,512]{1,0:T(8,128)(2,1)S(1)}, bf16[136,512]{1,0:T(8,128)(2,1)S(1)}, u32[]{:S(2)}, u32[]{:S(2)}) %collective-permute-start.14) | collective-permute-done | bytes 139296 | tf_op jit(solution)/shard_map/ppermute | solution.py:449
  88.9 1.1 %finish_step.1 = (f32[128,2048]{1,0:T(8,128)}, f32[3,2048]{1,0:T(4,128)}, f32[3,2048]{1,0:T(4,128)}) custom-call(s32[1]{0:T(128)} %bitcast.1.mine_ref, bf16[136,512]{1,0:T(8,128)(2,1)S(1)} %add.70.refs_0_, bf16[136,512]{1,0:T(8,128)(2,1)S(1)} %collective-permute-done.12.refs_1_, bf16[136,512]{1,0:T(8,128)(2,1)S(1)} %collective-permute-done.13.refs_2_, ...), custom_call_target="tpu_custom_call" | custom-call | flops 1000 | bytes 1000 | tf_op jit(solution)/shard_map/finish_step/pallas_call | solution.py:479
  (35 shorter events, 3.7 us)
Async XLA Ops:
  0.6 8.4 %copy-start.11 = (bf16[64,8192]{1,0:T(8,128)(2,1)S(1)}, bf16[64,8192]{1,0:T(8,128)(2,1)}, u32[]{:S(2)}) copy-start(bf16[64,8192]{1,0:T(8,128)(2,1)} %param.11) | copy-start | bytes 3145732
  2.0 12.4 %collective-permute-start.1 = (bf16[64,2048]{1,0:T(8,128)(2,1)S(1)}, bf16[64,2048]{1,0:T(8,128)(2,1)S(1)}, u32[]{:S(2)}, u32[]{:S(2)}) collective-permute-start(bf16[64,2048]{1,0:T(8,128)(2,1)S(1)} %get-tuple-element.59), channel_id=1, source_target_pairs={{0,1},{1,2},{2,3},{3,0},{4,5},{5,6},{6,7},{7,4},{8,9},{9,10},{10,1... | collective-permute-start | bytes 786440 | tf_op jit(solution)/shard_map/ppermute | solution.py:433
  5.1 19.7 %collective-permute-start.2 = (bf16[64,2048]{1,0:T(8,128)(2,1)S(1)}, bf16[64,2048]{1,0:T(8,128)(2,1)S(1)}, u32[]{:S(2)}, u32[]{:S(2)}) collective-permute-start(bf16[64,2048]{1,0:T(8,128)(2,1)S(1)} %get-tuple-element.61), channel_id=1, source_target_pairs={{0,2},{1,3},{2,0},{3,1},{4,6},{5,7},{6,4},{7,5},{8,10},{9,11},{10,... | collective-permute-start | bytes 786440 | tf_op jit(solution)/shard_map/ppermute | solution.py:433
  7.7 17.1 %collective-permute-start.3 = (bf16[64,2048]{1,0:T(8,128)(2,1)S(1)}, bf16[64,2048]{1,0:T(8,128)(2,1)S(1)}, u32[]{:S(2)}, u32[]{:S(2)}) collective-permute-start(bf16[64,2048]{1,0:T(8,128)(2,1)S(1)} %get-tuple-element.58), channel_id=1, source_target_pairs={{0,3},{1,0},{2,1},{3,2},{4,7},{5,4},{6,5},{7,6},{8,11},{9,8},{10,9... | collective-permute-start | bytes 786440 | tf_op jit(solution)/shard_map/ppermute | solution.py:433
  24.8 19.1 %collective-permute-start.4 = (bf16[64,2048]{1,0:T(8,128)(2,1)}, bf16[64,2048]{1,0:T(8,128)(2,1)S(1)}, u32[]{:S(2)}, u32[]{:S(2)}) collective-permute-start(bf16[64,2048]{1,0:T(8,128)(2,1)} %get-tuple-element.31), channel_id=1, source_target_pairs={{0,1},{1,2},{2,3},{3,0},{4,5},{5,6},{6,7},{7,4},{8,9},{9,10},{10,1... | collective-permute-start | bytes 786440 | tf_op jit(solution)/shard_map/ppermute | solution.py:433
  30.9 18.1 %collective-permute-start.5 = (bf16[64,2048]{1,0:T(8,128)(2,1)}, bf16[64,2048]{1,0:T(8,128)(2,1)}, u32[]{:S(2)}, u32[]{:S(2)}) collective-permute-start(bf16[64,2048]{1,0:T(8,128)(2,1)} %get-tuple-element.32), channel_id=1, source_target_pairs={{0,2},{1,3},{2,0},{3,1},{4,6},{5,7},{6,4},{7,5},{8,10},{9,11},{10,... | collective-permute-start | bytes 786440 | tf_op jit(solution)/shard_map/ppermute | solution.py:433
  32.5 16.6 %collective-permute-start.6 = (bf16[64,2048]{1,0:T(8,128)(2,1)}, bf16[64,2048]{1,0:T(8,128)(2,1)}, u32[]{:S(2)}, u32[]{:S(2)}) collective-permute-start(bf16[64,2048]{1,0:T(8,128)(2,1)} %get-tuple-element.33), channel_id=1, source_target_pairs={{0,3},{1,0},{2,1},{3,2},{4,7},{5,4},{6,5},{7,6},{8,11},{9,8},{10,9... | collective-permute-start | bytes 786440 | tf_op jit(solution)/shard_map/ppermute | solution.py:433
  33.3 5.0 %copy-start = (f32[128,2048]{1,0:T(8,128)S(1)}, f32[128,2048]{1,0:T(8,128)}, u32[]{:S(2)}) copy-start(f32[128,2048]{1,0:T(8,128)} %refs_7_.3) | copy-start | bytes 3145732
  33.3 5.0 %copy-start.2 = (bf16[256,512]{1,0:T(8,128)(2,1)S(1)}, bf16[256,512]{1,0:T(8,128)(2,1)}, u32[]{:S(2)}) copy-start(bf16[256,512]{1,0:T(8,128)(2,1)} %constant.51.clone.refs_8_) | copy-start | bytes 786436
  33.3 5.0 %copy-start.3 = (bf16[136,768]{1,0:T(8,128)(2,1)S(1)}, bf16[136,768]{1,0:T(8,128)(2,1)}, u32[]{:S(2)}) copy-start(bf16[136,768]{1,0:T(8,128)(2,1)} %constant.54.clone.refs_10_) | copy-start | bytes 626692
  33.3 5.0 %copy-start.4 = (bf16[256,384]{1,0:T(8,128)(2,1)S(1)}, bf16[256,384]{1,0:T(8,128)(2,1)}, u32[]{:S(2)}) copy-start(bf16[256,384]{1,0:T(8,128)(2,1)} %constant.52.clone.refs_9_.refs_13_) | copy-start | bytes 589828
  33.3 5.0 %copy-start.5 = (f32[3,2048]{1,0:T(4,128)S(1)}, f32[3,2048]{1,0:T(4,128)}, u32[]{:S(2)}) copy-start(f32[3,2048]{1,0:T(4,128)} %refs_12_.1) | copy-start | bytes 73732
  34.3 3.2 %collective-permute-start = (bf16[144,2048]{1,0:T(8,128)(2,1)}, bf16[144,2048]{1,0:T(8,128)(2,1)S(1)}, u32[]{:S(2)}, u32[]{:S(2)}) collective-permute-start(bf16[144,2048]{1,0:T(8,128)(2,1)} %param.1), channel_id=1, source_target_pairs={{0,4},{4,8},{8,12},{12,16},{16,20},{20,24},{24,28},{1,5},{5,9},{9,... | collective-permute-start | bytes 1769480 | tf_op jit(solution)/shard_map/cond/branch_1_fun/ppermute | solution.py:440
  38.3 10.8 %copy-start.8 = (f32[3,2048]{1,0:T(4,128)S(1)}, f32[3,2048]{1,0:T(4,128)}, u32[]{:S(2)}) copy-start(f32[3,2048]{1,0:T(4,128)} %refs_11_.1) | copy-start | bytes 73732
  38.3 10.7 %copy-start.9 = (bf16[256,768]{1,0:T(8,128)(2,1)S(1)}, bf16[256,768]{1,0:T(8,128)(2,1)}, u32[]{:S(2)}) copy-start(bf16[256,768]{1,0:T(8,128)(2,1)} %constant.53.clone.refs_14_) | copy-start | bytes 1179652
  38.3 10.7 %copy-start.10 = (bf16[144,2048]{1,0:T(8,128)(2,1)S(1)}, bf16[144,2048]{1,0:T(8,128)(2,1)}, u32[]{:S(2)}) copy-start(bf16[144,2048]{1,0:T(8,128)(2,1)} %get-tuple-element.62.refs_5_.refs_6_) | copy-start | bytes 1769476
  43.9 0.7 copy-start.6
  49.1 1.0 %copy-start.7 = (bf16[64,2048]{1,0:T(8,128)(2,1)S(1)}, bf16[64,2048]{1,0:T(8,128)(2,1)}, u32[]{:S(2)}) copy-start(bf16[64,2048]{1,0:T(8,128)(2,1)} %copy-done.6) | copy-start | bytes 786436
  59.7 1.0 %copy-start.1 = (f32[136,2048]{1,0:T(8,128)}, f32[136,2048]{1,0:T(8,128)S(1)}, u32[]{:S(2)}) copy-start(f32[136,2048]{1,0:T(8,128)S(1)} %get-tuple-element.44) | copy-start | bytes 3342340
  60.7 9.3 %collective-permute-start.7 = (bf16[136,512]{1,0:T(8,128)(2,1)S(1)}, bf16[136,512]{1,0:T(8,128)(2,1)S(1)}, u32[]{:S(2)}, u32[]{:S(2)}) collective-permute-start(bf16[136,512]{1,0:T(8,128)(2,1)S(1)} %get-tuple-element.51), channel_id=1, source_target_pairs={{0,8},{4,12},{8,0},{12,4},{16,24},{20,28},{24,16},{28,20},{1,9},{5... | collective-permute-start | bytes 417800 | tf_op jit(solution)/shard_map/ppermute | solution.py:449
  66.1 6.6 %collective-permute-start.8 = (bf16[136,512]{1,0:T(8,128)(2,1)S(1)}, bf16[136,512]{1,0:T(8,128)(2,1)S(1)}, u32[]{:S(2)}, u32[]{:S(2)}) collective-permute-start(bf16[136,512]{1,0:T(8,128)(2,1)S(1)} %get-tuple-element.53), channel_id=1, source_target_pairs={{0,16},{4,20},{8,24},{12,28},{16,0},{20,4},{24,8},{28,12},{1,17},{... | collective-permute-start | bytes 417800 | tf_op jit(solution)/shard_map/ppermute | solution.py:449
  67.6 6.0 %collective-permute-start.9 = (bf16[136,512]{1,0:T(8,128)(2,1)S(1)}, bf16[136,512]{1,0:T(8,128)(2,1)S(1)}, u32[]{:S(2)}, u32[]{:S(2)}) collective-permute-start(bf16[136,512]{1,0:T(8,128)(2,1)S(1)} %get-tuple-element.52), channel_id=1, source_target_pairs={{0,24},{4,28},{8,16},{12,20},{16,8},{20,12},{24,0},{28,4},{1,25},{... | collective-permute-start | bytes 417800 | tf_op jit(solution)/shard_map/ppermute | solution.py:449
  68.5 7.8 %collective-permute-start.11 = (bf16[144,2048]{1,0:T(8,128)(2,1)}, bf16[144,2048]{1,0:T(8,128)(2,1)S(1)}, u32[]{:S(2)}, u32[]{:S(2)}) collective-permute-start(bf16[144,2048]{1,0:T(8,128)(2,1)} %get-tuple-element.45), channel_id=1, source_target_pairs={{4,0},{8,4},{12,8},{16,12},{20,16},{24,20},{28,24},{5,1},{9,5},{13... | collective-permute-start | bytes 1769480 | tf_op jit(solution)/shard_map/ppermute | solution.py:440
  74.7 1.6 %collective-permute-start.10 = (f32[136,512]{1,0:T(8,128)S(1)}, f32[136,512]{1,0:T(8,128)S(1)}, u32[]{:S(2)}, u32[]{:S(2)}) collective-permute-start(f32[136,512]{1,0:T(8,128)S(1)} %add_add_fusion), channel_id=1, source_target_pairs={{0,4},{4,0},{8,12},{12,8},{16,20},{20,16},{24,28},{28,24},{1,5},{5... | collective-permute-start | bytes 835592 | tf_op jit(solution)/shard_map/ppermute | solution.py:449
  76.3 6.5 %collective-permute-start.12 = (bf16[136,512]{1,0:T(8,128)(2,1)S(1)}, bf16[136,512]{1,0:T(8,128)(2,1)S(1)}, u32[]{:S(2)}, u32[]{:S(2)}) collective-permute-start(bf16[136,512]{1,0:T(8,128)(2,1)S(1)} %add.70.refs_0_), channel_id=1, source_target_pairs={{0,8},{4,12},{8,0},{12,4},{16,24},{20,28},{24,16},{28,20},{1,9},{5... | collective-permute-start | bytes 417800 | tf_op jit(solution)/shard_map/ppermute | solution.py:449
  79.2 8.5 %collective-permute-start.13 = (bf16[136,512]{1,0:T(8,128)(2,1)S(1)}, bf16[136,512]{1,0:T(8,128)(2,1)S(1)}, u32[]{:S(2)}, u32[]{:S(2)}) collective-permute-start(bf16[136,512]{1,0:T(8,128)(2,1)S(1)} %add.70.refs_0_), channel_id=1, source_target_pairs={{0,16},{4,20},{8,24},{12,28},{16,0},{20,4},{24,8},{28,12},{1,17},{... | collective-permute-start | bytes 417800 | tf_op jit(solution)/shard_map/ppermute | solution.py:449
  80.7 8.2 %collective-permute-start.14 = (bf16[136,512]{1,0:T(8,128)(2,1)S(1)}, bf16[136,512]{1,0:T(8,128)(2,1)S(1)}, u32[]{:S(2)}, u32[]{:S(2)}) collective-permute-start(bf16[136,512]{1,0:T(8,128)(2,1)S(1)} %add.70.refs_0_), channel_id=1, source_target_pairs={{0,24},{4,28},{8,16},{12,20},{16,8},{20,12},{24,0},{28,4},{1,25},{... | collective-permute-start | bytes 417800 | tf_op jit(solution)/shard_map/ppermute | solution.py:449

commit v3 on v2

--- a/solution.py
+++ b/solution.py
@@ -247,16 +247,15 @@
     return pl.ds(pl.multiple_of(lax.rem(me_ref[0] + (pieces - k), pieces) * piece, piece), piece)
 
 
-def call(name, body, inputs, constants, outs, scratch, block, cost, me, pieces=()):
+def call(name, body, inputs, constants, outs, scratch, block, cost, me, pieces=(), kept_outs=(), at_end=None):
     moved = [isinstance(x, list) for x in inputs]
     arrays = [x[0] if isinstance(x, list) else x for x in inputs]
-    put = [isinstance(x, list) for x in outs]
-    shapes = [x[0] if isinstance(x, list) else x for x in outs]
-    width = shapes[0].shape[-1]
+    width = arrays[0].shape[-1]
     blocks = width // block
-    n_pieces, n_in, n_const, n_out = len(pieces), len(arrays), len(constants), len(shapes)
-    held = [x for x, move in zip(arrays, moved) if move] + list(constants)
-    held += [x for x, move in zip(shapes, put) if move]
+    last_outs = () if at_end is None else at_end[0]
+    n_pieces, n_in, n_const = len(pieces), len(arrays), len(constants)
+    n_out = len(outs) + len(last_outs)
+    held = [x for x, move in zip(arrays, moved) if move] + list(constants) + list(kept_outs)
     if pieces:
         held.append(jax.ShapeDtypeStruct((n_pieces * pieces[0].shape[0], width), pieces[0].dtype))
 
@@ -265,17 +264,13 @@
         given, refs = refs[: n_in + n_const], refs[n_in + n_const :]
         results, refs = refs[:n_out], refs[n_out:]
         temporary, kept, sems, const_sems = refs[: len(scratch)], list(refs[len(scratch) : -2]), *refs[-2:]
-        ins, sources, sinks = [], [], []
+        ins, sources = [], []
         for ref, move in zip(given, moved):
             ins.append(kept.pop(0) if move else ref)
             if move:
                 sources.append((ref, ins[-1]))
         whole = [kept.pop(0) for _ in range(n_const)]
-        shown = []
-        for ref, move in zip(results, put):
-            shown.append(kept.pop(0) if move else ref)
-            if move:
-                sinks.append((shown[-1], ref))
+        stay = [kept.pop(0) for _ in kept_outs]
         if pieces:
             ins.insert(0, kept.pop(0))
             sources += [
@@ -286,10 +281,8 @@
             place = pl.ds(pl.multiple_of(j * block, block), block)
             return ref.at[(slice(None),) * (len(ref.shape) - 1) + (place,)]
 
-        def copies(pairs, j, first):
-            return [
-                pltpu.make_async_copy(cut(a, j), cut(b, j), sems.at[first + i, j]) for i, (a, b) in enumerate(pairs)
-            ]
+        def copies(j):
+            return [pltpu.make_async_copy(cut(a, j), cut(b, j), sems.at[i, j]) for i, (a, b) in enumerate(sources)]
 
         constant_copies = [
             pltpu.make_async_copy(a, b, const_sems.at[i]) for i, (a, b) in enumerate(zip(given[n_in:], whole))
@@ -297,22 +290,20 @@
         for copy in constant_copies:
             copy.start()
         for j in range(blocks):
-            for copy in copies(sources, j, 0):
+            for copy in copies(j):
                 copy.start()
         for copy in constant_copies:
             copy.wait()
 
         def one(j):
-            for copy in copies(sources, j, 0):
+            for copy in copies(j):
                 copy.wait()
+            shown = list(results[: len(outs)]) + stay
             body(*[cut(x, j) for x in ins], *whole, *[cut(x, j) for x in shown], *temporary)
-            for copy in copies(sinks, j, len(sources)):
-                copy.start()
 
         pl.loop(0, blocks)(one)
-        for j in range(blocks):
-            for copy in copies(sinks, j, len(sources)):
-                copy.wait()
+        if at_end is not None:
+            at_end[1](me_ref, stay, results[len(outs) :])
 
     return pl.pallas_call(
         kernel,
@@ -320,14 +311,14 @@
         + [ANYWHERE] * n_pieces
         + [ANYWHERE if move else IN_VMEM for move in moved]
         + [ANYWHERE] * n_const,
-        out_specs=[ANYWHERE if move else IN_VMEM for move in put],
+        out_specs=[IN_VMEM] * n_out,
         scratch_shapes=[pltpu.VMEM(shape, dtype) for shape, dtype in scratch]
         + [pltpu.VMEM(x.shape, x.dtype) for x in held]
         + [
-            pltpu.SemaphoreType.DMA((n_pieces + sum(moved) + sum(put) + 1, blocks)),
+            pltpu.SemaphoreType.DMA((n_pieces + sum(moved) + 1, blocks)),
             pltpu.SemaphoreType.DMA((n_const,)),
         ],
-        out_shape=shapes,
+        out_shape=[*outs, *last_outs],
         compiler_params=pltpu.CompilerParams(vmem_limit_bytes=VMEM_LIMIT),
         cost_estimate=cost,
         name=name,
@@ -391,29 +382,38 @@
     )
 
 
-def gradient_step(g_pieces, me, u, halo, h, us, hs, z, gate, w, matrices, scale, block):
+def gradient_step(g_pieces, me, u, halo, h, us, hs, z, gate, w, matrices, scale, block, shares):
     rows, width = u.shape
     extent, taps, lead = h.shape[0], gate.shape[0], halo.shape[0]
     blocks = rows // extent
+    count, part = extent + -(-2 * taps // 8) * 8, width // shares
     outs = [
-        jax.ShapeDtypeStruct((extent + -(-2 * taps // 8) * 8, width), F32),
         jax.ShapeDtypeStruct((rows - lead, width), BF16),
         jax.ShapeDtypeStruct((lead, width), F32),
         jax.ShapeDtypeStruct((lead, width), BF16),
     ]
+    sums = [jax.ShapeDtypeStruct((count, width), F32)]
     spectra = (blocks, 2 * extent, block)
     scratch = [(spectra, F32), ((rows, block), F32)]
     scratch += [((rows, block), BF16)] * 2 + [((2 * extent, block), BF16)] * 2
     scratch += [(spectra, BF16)] * 2 + [(spectra, F32)]
-
-    def body(g, u, halo, h, us, hs, z, gate, w, short, inverse, sums, grad, end, head, d, dq, *temporary):
+    ends = [jax.ShapeDtypeStruct((count, part), BF16 if k else F32) for k in range(shares)]
+
+    def body(g, u, halo, h, us, hs, z, gate, w, short, inverse, grad, end, head, sums, d, dq, *temporary):
         sums_kernel(scale, g, u, halo, h, us, z, gate, w, short, inverse, d, dq, sums, *temporary[:4])
         input_kernel(lead, d, dq, hs, gate, w, inverse, grad, end, head, *temporary[4:])
 
-    return call(
+    def share(me_ref, kept, refs):
+        for k, ref in enumerate(refs):
+            start = pl.multiple_of((me_ref[1] ^ k) * part, part) if shares > 1 else 0
+            ref[...] = kept[0][:, pl.ds(start, part)].astype(ref.dtype)
+
+    main, end, head, *terms = call(
         "gradient_step", body, [u, [halo], [h], us, hs, z, [gate], [w]],
-        [matrices[name] for name in ("short", "inverse")], outs, scratch, block, LONG, me, g_pieces,
+        [matrices[name] for name in ("short", "inverse")], outs, scratch, block, LONG, me, g_pieces, sums,
+        (ends, share),
     )
+    return main, end, head, terms
 
 
 def slices(x, axis, start, part):
@@ -441,7 +441,7 @@
 
 
 def at_once(exchange_of, x, axis):
-    return lax.cond(lax.axis_index(axis) >= 0, exchange_of, lambda x: x, x)
+    return lax.cond(lax.axis_index(axis) >= 0, exchange_of, jnp.zeros_like, x)
 
 
 def partner(x, axis, bit):
@@ -458,15 +458,15 @@
     return total
 
 
-def finish_step(terms, mine, sizes):
-    part = terms[0].shape[1]
-    width = part * len(terms)
-
-    def kernel(mine_ref, *refs):
-        terms, outs, held, sems = refs[:4], refs[4 : 4 + len(sizes)], refs[4 + len(sizes) : -1], refs[-1]
+def finish_step(terms, me, sizes):
+    part, shares = terms[0].shape[1], len(terms)
+    width = part * shares
+
+    def kernel(me_ref, *refs):
+        terms, outs, held, sems = refs[:shares], refs[shares : shares + len(sizes)], refs[shares + len(sizes) : -1], refs[-1]
         copies = []
         for k, term in enumerate(terms):
-            place = pl.ds(pl.multiple_of((mine_ref[0] ^ k) * part, part), part)
+            place = pl.ds(pl.multiple_of((me_ref[1] ^ k) * part, part), part)
             x, row = term[...].astype(F32), 0
             for i, (size, out, ref) in enumerate(zip(sizes, outs, held)):
                 ref[:, place] = x[row : row + size]
@@ -478,21 +478,21 @@
 
     return pl.pallas_call(
         kernel,
-        in_specs=[IN_SMEM] + [IN_VMEM] * 4,
+        in_specs=[IN_SMEM] + [IN_VMEM] * shares,
         out_specs=[ANYWHERE] * len(sizes),
         scratch_shapes=[pltpu.VMEM((size, width), F32) for size in sizes]
-        + [pltpu.SemaphoreType.DMA((len(sizes), 4))],
+        + [pltpu.SemaphoreType.DMA((len(sizes), shares))],
         out_shape=[jax.ShapeDtypeStruct((size, width), F32) for size in sizes],
         compiler_params=pltpu.CompilerParams(vmem_limit_bytes=VMEM_LIMIT),
         cost_estimate=BRIEF,
         name="finish_step",
-    )(mine, *terms)
+    )(me, *terms)
 
 
 def shards(out_grad, saved_input, explicit_filter_weights, gate_taps, value_featurizer_weights):
     extent, width = explicit_filter_weights.shape
     taps = gate_taps.shape[0]
-    me = lax.axis_index("tp").astype(jnp.int32).reshape(1)
+    me = jnp.stack([lax.axis_index("tp"), lax.axis_index("ctx") // 2]).astype(jnp.int32)
     rows = out_grad.shape[0] * lax.axis_size("tp")
     lead = -(-(extent + taps - 2) // 16) * 16
     block = min(BLOCK, width)
@@ -506,24 +506,25 @@
     tail = tail_step(u_pieces, me, lead)
     halo = at_once(lambda x: shifted(x, "ctx", 1), tail, "ctx")
     us, hs, z, u = signal_step(u_pieces, me, halo, h, w, matrices, block)
-    partial, main, end, head = gradient_step(
-        g_pieces, me, u, halo, h, us, hs, z, gate, w, matrices, scale, block
+    chips = lax.axis_size("ctx") // 2
+    shares = chips if chips == 4 and width % (128 * chips) == 0 else 1
+    main, end, head, terms = gradient_step(
+        g_pieces, me, u, halo, h, us, hs, z, gate, w, matrices, scale, block, shares
     )
-    incoming = shifted(head, "ctx", -1)
     sizes = (extent, taps, taps)
-    if lax.axis_size("ctx") == 8:
-        mine = (lax.axis_index("ctx") // 2).astype(jnp.int32)
-        part = width // 4
-        quarters = [lax.dynamic_slice_in_dim(partial, (mine ^ k) * part, part, axis=1) for k in range(4)]
-        got = [partner(quarters[k].astype(BF16), "ctx", 2 * k) for k in range(1, 4)]
-        total = (quarters[0] + got[0].astype(F32)) + (got[1].astype(F32) + got[2].astype(F32))
-        total = total + partner(total, "ctx", 1)
+    if shares > 1:
+        terms = [terms[0]] + [partner(terms[k], "ctx", 2 * k).astype(F32) for k in range(1, shares)]
+        incoming = shifted(head, "ctx", -1)
+        while len(terms) > 1:
+            terms = [a + b for a, b in zip(terms[::2], terms[1::2])]
+        total = terms[0] + partner(terms[0], "ctx", 1)
         total, incoming = lax.optimization_barrier((total, incoming))
         total = total.astype(BF16)
-        terms = [total] + [partner(total, "ctx", 2 * k) for k in range(1, 4)]
-        sums = finish_step(terms, mine.reshape(1), sizes)
+        terms = [total] + [partner(total, "ctx", 2 * k) for k in range(1, shares)]
+        sums = finish_step(terms, me, sizes)
     else:
-        total = summed(partial, "ctx")
+        incoming = shifted(head, "ctx", -1)
+        total = summed(terms[0], "ctx")
         ends = np.cumsum(sizes)
         sums = [total[stop - size : stop] for size, stop in zip(sizes, ends)]
     end = (end + incoming.astype(F32)).astype(BF16)

time: 90.3 us -> 88.2 us (0.977)
  waiting for transfers between devices: 32.5 us -> 38.9 us
  starting transfers between devices: 31.3 us -> 25.8 us
  local copies, waits for them, and re-layouts: 5.83 us -> 2.33 us
  Pallas kernels: 17.3 us -> 18.7 us
    ppermute x6, waiting for transfers between devices: 19.3 us -> 26.2 us  [exchange(): lax.ppermute(pieces[k], axis, [(i, (i + k) % count) for i in range(count)])]
    ppermute x6, starting transfers between devices: 15.5 us -> 9.99 us  [exchange(): lax.ppermute(pieces[k], axis, [(i, (i + k) % count) for i in range(count)])]
    unnamed x24 -> x16, local copies, waits for them, and re-layouts: 2.68 us -> 0.04 us
    add x2, other arithmetic: 1.06 us -> 0.12 us  [the longest x1 0.07 us: shards(): terms = [a + b for a, b in zip(terms[::2], terms[1::2])]]
  transfers between devices with their start and end apart: 15 -> 15, of which waited for: 10 -> 12; matrix products, arithmetic and copies ran while one was open for 4% -> 3% of each run, Pallas kernels for 7% -> 9%
where the time goes in v3:
time: 88.2 us; the launch traced here: 87.9 us
  waiting for transfers between devices  38.9 us (44%)
  starting transfers between devices  25.8 us (29%)
  Pallas kernels  18.7 us (21%)
  local copies, waits for them, and re-layouts  2.33 us (3%)
  other arithmetic  1.38 us (2%)
    ppermute x6, waiting for transfers between devices, exchange(): lax.ppermute(pieces[k], axis, [(i, (i + k) % count) for i in range(count)])  26.2 us
    pallas_call x2, Pallas kernels, call(): pl.pallas_call(kernel, in_specs=[IN_SMEM] + [ANYWHERE] * n_pieces + [ANYW...  15.6 us
    ppermute x7, starting transfers between devices, partner(): return lax.ppermute(x, axis, [(i, i ^ bit) for i in range(count)])  12.4 us
    ppermute x7, waiting for transfers between devices, partner(): return lax.ppermute(x, axis, [(i, i ^ bit) for i in range(count)])  11.6 us
    ppermute x6, starting transfers between devices, exchange(): lax.ppermute(pieces[k], axis, [(i, (i + k) % count) for i in range(count)])  9.99 us
    ppermute x2, starting transfers between devices, shifted(): return lax.ppermute(x, axis, pairs)  3.43 us
    dynamic_slice x2, local copies, waits for them, and re-layouts, slices(): lax.dynamic_slice_in_dim(x, lax.rem(me + k, count) * width + start, part,...  2.29 us
  transfers between devices with their start and end apart: 15, of which 12 were waited for; matrix products, arithmetic and copies ran while one was open for 3% of the time, Pallas kernels for 9%

profile of v3, /device:TPU:0, one launch (start us, length us, event | category | flops | bytes accessed | tf_op | source)
XLA Modules:
  0.0 87.9 jit_solution(6269910031139327875)
XLA Ops:
  0.7 1.4 %constant_dynamic-slice_fusion.4 = (bf16[64,2048]{1,0:T(8,128)(2,1)S(1)}, bf16[64,2048]{1,0:T(8,128)(2,1)S(1)}, bf16[64,2048]{1,0:T(8,128)(2,1)S(1)}, bf16[64,2048]{1,0:T(8,128)(2,1)S(1)}) fusion(bf16[64,8192]{1,0:T(8,128)(2,1)} %param.12, s32[]{:T(128)S(6)} %select_n.25, s32[]{:T(128)S(6)} %select_n.23, s32[]{:T(128)S(6)} %select_n.22, s32[]{:T(128)S(6)} %select_n.24), kind=kLoop, calls=%fused_computation.7 | loop fusion | bytes 2097168 | tf_op jit(solution)/shard_map/dynamic_slice | solution.py:424
  2.1 5.1 %collective-permute-start.3 = (bf16[64,2048]{1,0:T(8,128)(2,1)S(1)}, bf16[64,2048]{1,0:T(8,128)(2,1)S(1)}, u32[]{:S(2)}, u32[]{:S(2)}) collective-permute-start(bf16[64,2048]{1,0:T(8,128)(2,1)S(1)} %get-tuple-element.60), channel_id=1, source_target_pairs={{0,3},{1,0},{2,1},{3,2},{4,7},{5,4},{6,5},{7,6},{8,11},{9,8},{10,9... | collective-permute-start | bytes 786440 | tf_op jit(solution)/shard_map/ppermute | solution.py:433
  7.2 1.1 %collective-permute-start.2 = (bf16[64,2048]{1,0:T(8,128)(2,1)S(1)}, bf16[64,2048]{1,0:T(8,128)(2,1)S(1)}, u32[]{:S(2)}, u32[]{:S(2)}) collective-permute-start(bf16[64,2048]{1,0:T(8,128)(2,1)S(1)} %get-tuple-element.63), channel_id=1, source_target_pairs={{0,2},{1,3},{2,0},{3,1},{4,6},{5,7},{6,4},{7,5},{8,10},{9,11},{10,... | collective-permute-start | bytes 786440 | tf_op jit(solution)/shard_map/ppermute | solution.py:433
  8.3 0.9 %constant_dynamic-slice_fusion = (bf16[64,2048]{1,0:T(8,128)(2,1)}, bf16[64,2048]{1,0:T(8,128)(2,1)}, bf16[64,2048]{1,0:T(8,128)(2,1)S(1)}, bf16[64,2048]{1,0:T(8,128)(2,1)}) fusion(bf16[64,8192]{1,0:T(8,128)(2,1)S(1)} %copy-done.7, s32[]{:T(128)S(6)} %select_n.25, s32[]{:T(128)S(6)} %select_n.23, s32[]{:T(128)S(6)} %select_n.22, s32[]{:T(128)S(6)} %select_n.24), kind=kLoop, calls=%fused_computation.3 | loop fusion | bytes 2097168 | tf_op jit(solution)/shard_map/dynamic_slice | solution.py:424
  9.2 4.7 %collective-permute-done.3.refs_3_.refs_4_ = bf16[64,2048]{1,0:T(8,128)(2,1)S(1)} collective-permute-done((bf16[64,2048]{1,0:T(8,128)(2,1)S(1)}, bf16[64,2048]{1,0:T(8,128)(2,1)S(1)}, u32[]{:S(2)}, u32[]{:S(2)}) %collective-permute-start.3) | collective-permute-done | bytes 262176 | tf_op jit(solution)/shard_map/ppermute | solution.py:433
  13.9 6.6 %collective-permute-done.1.refs_1_.refs_2_ = bf16[64,2048]{1,0:T(8,128)(2,1)S(1)} collective-permute-done((bf16[64,2048]{1,0:T(8,128)(2,1)S(1)}, bf16[64,2048]{1,0:T(8,128)(2,1)S(1)}, u32[]{:S(2)}, u32[]{:S(2)}) %collective-permute-start.1) | collective-permute-done | bytes 262176 | tf_op jit(solution)/shard_map/ppermute | solution.py:433
  20.5 9.0 %collective-permute-done.2.refs_2_.refs_3_ = bf16[64,2048]{1,0:T(8,128)(2,1)S(1)} collective-permute-done((bf16[64,2048]{1,0:T(8,128)(2,1)S(1)}, bf16[64,2048]{1,0:T(8,128)(2,1)S(1)}, u32[]{:S(2)}, u32[]{:S(2)}) %collective-permute-start.2) | collective-permute-done | bytes 262176 | tf_op jit(solution)/shard_map/ppermute | solution.py:433
  29.5 0.2 collective-permute-start.4
  29.7 3.4 %collective-permute-start.5 = (bf16[64,2048]{1,0:T(8,128)(2,1)}, bf16[64,2048]{1,0:T(8,128)(2,1)}, u32[]{:S(2)}, u32[]{:S(2)}) collective-permute-start(bf16[64,2048]{1,0:T(8,128)(2,1)} %get-tuple-element.34), channel_id=1, source_target_pairs={{0,2},{1,3},{2,0},{3,1},{4,6},{5,7},{6,4},{7,5},{8,10},{9,11},{10,... | collective-permute-start | bytes 786440 | tf_op jit(solution)/shard_map/ppermute | solution.py:433
  33.0 0.3 collective-permute-start.6
  33.4 1.5 %tail_step.1 = bf16[144,2048]{1,0:T(8,128)(2,1)} custom-call(s32[2]{0:T(128)S(1)} %pad_add_fusion.me_ref.refs_0_, bf16[64,2048]{1,0:T(8,128)(2,1)S(1)} %get-tuple-element.36.refs_0_.refs_1_, bf16[64,2048]{1,0:T(8,128)(2,1)S(1)} %collective-permute-done.1.refs_1_.refs_2_, bf16[64,2048]{1,0:T(8,128)(2,1)S(1)} %collective-permute-done.2.refs_2_.refs_3_, ...), custom_call_target="tpu_custom_call" | custom-call | flops 1000 | bytes 1000 | tf_op jit(solution)/shard_map/tail_step/pallas_call | solution.py:346
  34.9 3.3 %conditional.1 = (bf16[144,2048]{1,0:T(8,128)(2,1)}) conditional(s32[]{:T(128)} %convert_element_type.21, () %tuple.17, bf16[144,2048]{1,0:T(8,128)(2,1)} %tail_step.1), branch_computations={%region_0.1_spmd, %region_1.2_spmd} | conditional | bytes 2359344 | solution.py:444
  34.9 2.1 %collective-permute-start = (bf16[144,2048]{1,0:T(8,128)(2,1)}, bf16[144,2048]{1,0:T(8,128)(2,1)}, u32[]{:S(2)}, u32[]{:S(2)}) collective-permute-start(bf16[144,2048]{1,0:T(8,128)(2,1)} %param.1), channel_id=1, source_target_pairs={{0,4},{4,8},{8,12},{12,16},{16,20},{20,24},{24,28},{1,5},{5,9},{9,... | collective-permute-start | bytes 1769480 | tf_op jit(solution)/shard_map/cond/branch_1_fun/ppermute | solution.py:440
  37.0 1.1 %collective-permute-done = bf16[144,2048]{1,0:T(8,128)(2,1)} collective-permute-done((bf16[144,2048]{1,0:T(8,128)(2,1)}, bf16[144,2048]{1,0:T(8,128)(2,1)}, u32[]{:S(2)}, u32[]{:S(2)}) %collective-permute-start) | collective-permute-done | bytes 589856 | tf_op jit(solution)/shard_map/cond/branch_1_fun/ppermute | solution.py:440
  38.2 6.1 %signal_step.1 = (f32[2,256,2048]{2,1,0:T(8,128)S(1)}, f32[256,2048]{1,0:T(8,128)S(1)}, f32[256,2048]{1,0:T(8,128)S(1)}, bf16[256,2048]{1,0:T(8,128)(2,1)S(1)}) custom-call(s32[2]{0:T(128)S(1)} %pad_add_fusion.me_ref.refs_0_, bf16[64,2048]{1,0:T(8,128)(2,1)S(1)} %get-tuple-element.36.refs_0_.refs_1_, ...), custom_call_target="tpu_custom_call" | custom-call | flops 1000 | bytes 1000 | tf_op jit(solution)/shard_map/signal_step/pallas_call | solution.py:308
  44.3 5.9 %collective-permute-done.5.refs_3_ = bf16[64,2048]{1,0:T(8,128)(2,1)} collective-permute-done((bf16[64,2048]{1,0:T(8,128)(2,1)}, bf16[64,2048]{1,0:T(8,128)(2,1)}, u32[]{:S(2)}, u32[]{:S(2)}) %collective-permute-start.5) | collective-permute-done | bytes 262176 | tf_op jit(solution)/shard_map/ppermute | solution.py:433
  50.2 9.5 %gradient_step.1 = (bf16[112,2048]{1,0:T(8,128)(2,1)S(1)}, f32[144,2048]{1,0:T(8,128)S(1)}, bf16[144,2048]{1,0:T(8,128)(2,1)S(1)}, f32[136,512]{1,0:T(8,128)S(1)...) custom-call(s32[2]{0:T(128)S(1)} %pad_add_fusion.me_ref.refs_0_, ...), custom_call_target="tpu_custom_call" | custom-call | flops 20000000000 | bytes 100000000 | tf_op jit(solution)/shard_map/gradient_step/pallas_call | solution.py:308
  59.7 4.0 %collective-permute-start.7 = (bf16[136,512]{1,0:T(8,128)(2,1)S(1)}, bf16[136,512]{1,0:T(8,128)(2,1)S(1)}, u32[]{:S(2)}, u32[]{:S(2)}) collective-permute-start(bf16[136,512]{1,0:T(8,128)(2,1)S(1)} %get-tuple-element.47), channel_id=1, source_target_pairs={{0,8},{4,12},{8,0},{12,4},{16,24},{20,28},{24,16},{28,20},{1,9},{5... | collective-permute-start | bytes 417800 | tf_op jit(solution)/shard_map/ppermute | solution.py:449
  63.7 1.5 %collective-permute-start.8 = (bf16[136,512]{1,0:T(8,128)(2,1)S(1)}, bf16[136,512]{1,0:T(8,128)(2,1)S(1)}, u32[]{:S(2)}, u32[]{:S(2)}) collective-permute-start(bf16[136,512]{1,0:T(8,128)(2,1)S(1)} %get-tuple-element.48), channel_id=1, source_target_pairs={{0,16},{4,20},{8,24},{12,28},{16,0},{20,4},{24,8},{28,12},{1,17},{... | collective-permute-start | bytes 417800 | tf_op jit(solution)/shard_map/ppermute | solution.py:449
  65.2 0.9 collective-permute-start.9
  66.1 1.3 %collective-permute-start.11 = (bf16[144,2048]{1,0:T(8,128)(2,1)S(1)}, bf16[144,2048]{1,0:T(8,128)(2,1)S(1)}, u32[]{:S(2)}, u32[]{:S(2)}) collective-permute-start(bf16[144,2048]{1,0:T(8,128)(2,1)S(1)} %get-tuple-element.50), channel_id=1, source_target_pairs={{4,0},{8,4},{12,8},{16,12},{20,16},{24,20},{28,24},{5,1},{9,5},{13... | collective-permute-start | bytes 1769480 | tf_op jit(solution)/shard_map/ppermute | solution.py:440
  67.5 2.8 %collective-permute-done.8 = bf16[136,512]{1,0:T(8,128)(2,1)S(1)} collective-permute-done((bf16[136,512]{1,0:T(8,128)(2,1)S(1)}, bf16[136,512]{1,0:T(8,128)(2,1)S(1)}, u32[]{:S(2)}, u32[]{:S(2)}) %collective-permute-start.8) | collective-permute-done | bytes 139296 | tf_op jit(solution)/shard_map/ppermute | solution.py:449
  70.2 0.9 %collective-permute-done.9 = bf16[136,512]{1,0:T(8,128)(2,1)S(1)} collective-permute-done((bf16[136,512]{1,0:T(8,128)(2,1)S(1)}, bf16[136,512]{1,0:T(8,128)(2,1)S(1)}, u32[]{:S(2)}, u32[]{:S(2)}) %collective-permute-start.9) | collective-permute-done | bytes 139296 | tf_op jit(solution)/shard_map/ppermute | solution.py:449
  71.3 1.5 %collective-permute-done.10 = f32[136,512]{1,0:T(8,128)S(1)} collective-permute-done((f32[136,512]{1,0:T(8,128)S(1)}, f32[136,512]{1,0:T(8,128)S(1)}, u32[]{:S(2)}, u32[]{:S(2)}) %collective-permute-start.10) | collective-permute-done | bytes 278560 | tf_op jit(solution)/shard_map/ppermute | solution.py:449
  72.9 4.5 %collective-permute-start.14 = (bf16[136,512]{1,0:T(8,128)(2,1)S(1)}, bf16[136,512]{1,0:T(8,128)(2,1)S(1)}, u32[]{:S(2)}, u32[]{:S(2)}) collective-permute-start(bf16[136,512]{1,0:T(8,128)(2,1)S(1)} %add.54.refs_0_), channel_id=1, source_target_pairs={{0,24},{4,28},{8,16},{12,20},{16,8},{20,12},{24,0},{28,4},{1,25},{... | collective-permute-start | bytes 417800 | tf_op jit(solution)/shard_map/ppermute | solution.py:449
  77.4 0.5 collective-permute-start.13
  77.9 0.9 %collective-permute-start.12 = (bf16[136,512]{1,0:T(8,128)(2,1)S(1)}, bf16[136,512]{1,0:T(8,128)(2,1)S(1)}, u32[]{:S(2)}, u32[]{:S(2)}) collective-permute-start(bf16[136,512]{1,0:T(8,128)(2,1)S(1)} %add.54.refs_0_), channel_id=1, source_target_pairs={{0,8},{4,12},{8,0},{12,4},{16,24},{20,28},{24,16},{28,20},{1,9},{5... | collective-permute-start | bytes 417800 | tf_op jit(solution)/shard_map/ppermute | solution.py:449
  79.0 1.1 %pad_maximum_fusion = bf16[256,2048]{1,0:T(8,128)(2,1)} fusion(bf16[144,2048]{1,0:T(8,128)(2,1)S(1)} %add_convert_fusion, bf16[112,2048]{1,0:T(8,128)(2,1)S(1)} %get-tuple-element.44), kind=kLoop, calls=%fused_computation.1 | loop fusion | flops 2097152 | bytes 2097152 | tf_op jit(solution)/shard_map/concatenate | solution.py:531
  80.0 0.6 collective-permute-done.14.refs_3_
  80.6 4.3 %collective-permute-done.13.refs_2_ = bf16[136,512]{1,0:T(8,128)(2,1)S(1)} collective-permute-done((bf16[136,512]{1,0:T(8,128)(2,1)S(1)}, bf16[136,512]{1,0:T(8,128)(2,1)S(1)}, u32[]{:S(2)}, u32[]{:S(2)}) %collective-permute-start.13) | collective-permute-done | bytes 139296 | tf_op jit(solution)/shard_map/ppermute | solution.py:449
  84.9 1.4 %collective-permute-done.12.refs_1_ = bf16[136,512]{1,0:T(8,128)(2,1)S(1)} collective-permute-done((bf16[136,512]{1,0:T(8,128)(2,1)S(1)}, bf16[136,512]{1,0:T(8,128)(2,1)S(1)}, u32[]{:S(2)}, u32[]{:S(2)}) %collective-permute-start.12) | collective-permute-done | bytes 139296 | tf_op jit(solution)/shard_map/ppermute | solution.py:449
  86.3 1.7 %finish_step.1 = (f32[128,2048]{1,0:T(8,128)}, f32[3,2048]{1,0:T(4,128)}, f32[3,2048]{1,0:T(4,128)}) custom-call(s32[2]{0:T(128)S(1)} %pad_add_fusion.me_ref.refs_0_, bf16[136,512]{1,0:T(8,128)(2,1)S(1)} %add.54.refs_0_, bf16[136,512]{1,0:T(8,128)(2,1)S(1)} %collective-permute-done.12.refs_1_, bf16[136,512]{1,0:T(8,128)(2,1)S(1)} %collective-permute-done.13.refs_2_, ...), custom_call_target="tpu_custom_call" | custom-call | flops 1000 | bytes 1000 | tf_op jit(solution)/shard_map/finish_step/pallas_call | solution.py:479
  (26 shorter events, 0.6 us)
Async XLA Ops:
  0.7 7.6 %copy-start.7 = (bf16[64,8192]{1,0:T(8,128)(2,1)S(1)}, bf16[64,8192]{1,0:T(8,128)(2,1)}, u32[]{:S(2)}) copy-start(bf16[64,8192]{1,0:T(8,128)(2,1)} %param.11) | copy-start | bytes 3145732
  2.1 11.8 %collective-permute-start.3 = (bf16[64,2048]{1,0:T(8,128)(2,1)S(1)}, bf16[64,2048]{1,0:T(8,128)(2,1)S(1)}, u32[]{:S(2)}, u32[]{:S(2)}) collective-permute-start(bf16[64,2048]{1,0:T(8,128)(2,1)S(1)} %get-tuple-element.60), channel_id=1, source_target_pairs={{0,3},{1,0},{2,1},{3,2},{4,7},{5,4},{6,5},{7,6},{8,11},{9,8},{10,9... | collective-permute-start | bytes 786440 | tf_op jit(solution)/shard_map/ppermute | solution.py:433
  7.2 13.3 %collective-permute-start.1 = (bf16[64,2048]{1,0:T(8,128)(2,1)S(1)}, bf16[64,2048]{1,0:T(8,128)(2,1)S(1)}, u32[]{:S(2)}, u32[]{:S(2)}) collective-permute-start(bf16[64,2048]{1,0:T(8,128)(2,1)S(1)} %get-tuple-element.61), channel_id=1, source_target_pairs={{0,1},{1,2},{2,3},{3,0},{4,5},{5,6},{6,7},{7,4},{8,9},{9,10},{10,1... | collective-permute-start | bytes 786440 | tf_op jit(solution)/shard_map/ppermute | solution.py:433
  7.2 31.0 %copy-start = (f32[128,2048]{1,0:T(8,128)S(1)}, f32[128,2048]{1,0:T(8,128)}, u32[]{:S(2)}) copy-start(f32[128,2048]{1,0:T(8,128)} %refs_7_.3) | copy-start | bytes 3145732
  7.2 31.0 %copy-start.1 = (bf16[256,512]{1,0:T(8,128)(2,1)S(1)}, bf16[256,512]{1,0:T(8,128)(2,1)}, u32[]{:S(2)}) copy-start(bf16[256,512]{1,0:T(8,128)(2,1)} %constant.51.clone.refs_8_) | copy-start | bytes 786436
  7.2 31.0 %copy-start.2 = (bf16[136,768]{1,0:T(8,128)(2,1)S(1)}, bf16[136,768]{1,0:T(8,128)(2,1)}, u32[]{:S(2)}) copy-start(bf16[136,768]{1,0:T(8,128)(2,1)} %constant.54.clone.refs_10_) | copy-start | bytes 626692
  7.2 31.0 %copy-start.3 = (bf16[256,384]{1,0:T(8,128)(2,1)S(1)}, bf16[256,384]{1,0:T(8,128)(2,1)}, u32[]{:S(2)}) copy-start(bf16[256,384]{1,0:T(8,128)(2,1)} %constant.52.clone.refs_9_.refs_13_) | copy-start | bytes 589828
  7.2 31.0 %copy-start.4 = (f32[3,2048]{1,0:T(4,128)S(1)}, f32[3,2048]{1,0:T(4,128)}, u32[]{:S(2)}) copy-start(f32[3,2048]{1,0:T(4,128)} %refs_12_.1) | copy-start | bytes 73732
  7.2 22.3 %collective-permute-start.2 = (bf16[64,2048]{1,0:T(8,128)(2,1)S(1)}, bf16[64,2048]{1,0:T(8,128)(2,1)S(1)}, u32[]{:S(2)}, u32[]{:S(2)}) collective-permute-start(bf16[64,2048]{1,0:T(8,128)(2,1)S(1)} %get-tuple-element.63), channel_id=1, source_target_pairs={{0,2},{1,3},{2,0},{3,1},{4,6},{5,7},{6,4},{7,5},{8,10},{9,11},{10,... | collective-permute-start | bytes 786440 | tf_op jit(solution)/shard_map/ppermute | solution.py:433
  29.5 14.8 %collective-permute-start.4 = (bf16[64,2048]{1,0:T(8,128)(2,1)}, bf16[64,2048]{1,0:T(8,128)(2,1)S(1)}, u32[]{:S(2)}, u32[]{:S(2)}) collective-permute-start(bf16[64,2048]{1,0:T(8,128)(2,1)} %get-tuple-element.33), channel_id=1, source_target_pairs={{0,1},{1,2},{2,3},{3,0},{4,5},{5,6},{6,7},{7,4},{8,9},{9,10},{10,1... | collective-permute-start | bytes 786440 | tf_op jit(solution)/shard_map/ppermute | solution.py:433
  29.7 20.5 %collective-permute-start.5 = (bf16[64,2048]{1,0:T(8,128)(2,1)}, bf16[64,2048]{1,0:T(8,128)(2,1)}, u32[]{:S(2)}, u32[]{:S(2)}) collective-permute-start(bf16[64,2048]{1,0:T(8,128)(2,1)} %get-tuple-element.34), channel_id=1, source_target_pairs={{0,2},{1,3},{2,0},{3,1},{4,6},{5,7},{6,4},{7,5},{8,10},{9,11},{10,... | collective-permute-start | bytes 786440 | tf_op jit(solution)/shard_map/ppermute | solution.py:433
  33.0 17.2 %collective-permute-start.6 = (bf16[64,2048]{1,0:T(8,128)(2,1)}, bf16[64,2048]{1,0:T(8,128)(2,1)}, u32[]{:S(2)}, u32[]{:S(2)}) collective-permute-start(bf16[64,2048]{1,0:T(8,128)(2,1)} %get-tuple-element.35), channel_id=1, source_target_pairs={{0,3},{1,0},{2,1},{3,2},{4,7},{5,4},{6,5},{7,6},{8,11},{9,8},{10,9... | collective-permute-start | bytes 786440 | tf_op jit(solution)/shard_map/ppermute | solution.py:433
  34.9 15.3 %copy-start.5 = (f32[3,2048]{1,0:T(4,128)S(1)}, f32[3,2048]{1,0:T(4,128)}, u32[]{:S(2)}) copy-start(f32[3,2048]{1,0:T(4,128)} %refs_11_.1) | copy-start | bytes 73732
  34.9 3.3 %collective-permute-start = (bf16[144,2048]{1,0:T(8,128)(2,1)}, bf16[144,2048]{1,0:T(8,128)(2,1)}, u32[]{:S(2)}, u32[]{:S(2)}) collective-permute-start(bf16[144,2048]{1,0:T(8,128)(2,1)} %param.1), channel_id=1, source_target_pairs={{0,4},{4,8},{8,12},{12,16},{16,20},{20,24},{24,28},{1,5},{5,9},{9,... | collective-permute-start | bytes 1769480 | tf_op jit(solution)/shard_map/cond/branch_1_fun/ppermute | solution.py:440
  38.2 12.0 %copy-start.6 = (bf16[256,768]{1,0:T(8,128)(2,1)S(1)}, bf16[256,768]{1,0:T(8,128)(2,1)}, u32[]{:S(2)}) copy-start(bf16[256,768]{1,0:T(8,128)(2,1)} %constant.53.clone.refs_14_) | copy-start | bytes 1179652
  59.7 7.8 %collective-permute-start.7 = (bf16[136,512]{1,0:T(8,128)(2,1)S(1)}, bf16[136,512]{1,0:T(8,128)(2,1)S(1)}, u32[]{:S(2)}, u32[]{:S(2)}) collective-permute-start(bf16[136,512]{1,0:T(8,128)(2,1)S(1)} %get-tuple-element.47), channel_id=1, source_target_pairs={{0,8},{4,12},{8,0},{12,4},{16,24},{20,28},{24,16},{28,20},{1,9},{5... | collective-permute-start | bytes 417800 | tf_op jit(solution)/shard_map/ppermute | solution.py:449
  63.7 6.6 %collective-permute-start.8 = (bf16[136,512]{1,0:T(8,128)(2,1)S(1)}, bf16[136,512]{1,0:T(8,128)(2,1)S(1)}, u32[]{:S(2)}, u32[]{:S(2)}) collective-permute-start(bf16[136,512]{1,0:T(8,128)(2,1)S(1)} %get-tuple-element.48), channel_id=1, source_target_pairs={{0,16},{4,20},{8,24},{12,28},{16,0},{20,4},{24,8},{28,12},{1,17},{... | collective-permute-start | bytes 417800 | tf_op jit(solution)/shard_map/ppermute | solution.py:449
  65.2 6.0 %collective-permute-start.9 = (bf16[136,512]{1,0:T(8,128)(2,1)S(1)}, bf16[136,512]{1,0:T(8,128)(2,1)S(1)}, u32[]{:S(2)}, u32[]{:S(2)}) collective-permute-start(bf16[136,512]{1,0:T(8,128)(2,1)S(1)} %get-tuple-element.49), channel_id=1, source_target_pairs={{0,24},{4,28},{8,16},{12,20},{16,8},{20,12},{24,0},{28,4},{1,25},{... | collective-permute-start | bytes 417800 | tf_op jit(solution)/shard_map/ppermute | solution.py:449
  66.1 6.8 %collective-permute-start.11 = (bf16[144,2048]{1,0:T(8,128)(2,1)S(1)}, bf16[144,2048]{1,0:T(8,128)(2,1)S(1)}, u32[]{:S(2)}, u32[]{:S(2)}) collective-permute-start(bf16[144,2048]{1,0:T(8,128)(2,1)S(1)} %get-tuple-element.50), channel_id=1, source_target_pairs={{4,0},{8,4},{12,8},{16,12},{20,16},{24,20},{28,24},{5,1},{9,5},{13... | collective-permute-start | bytes 1769480 | tf_op jit(solution)/shard_map/ppermute | solution.py:440
  71.2 1.6 %collective-permute-start.10 = (f32[136,512]{1,0:T(8,128)S(1)}, f32[136,512]{1,0:T(8,128)S(1)}, u32[]{:S(2)}, u32[]{:S(2)}) collective-permute-start(f32[136,512]{1,0:T(8,128)S(1)} %add_add_fusion), channel_id=1, source_target_pairs={{0,4},{4,0},{8,12},{12,8},{16,20},{20,16},{24,28},{28,24},{1,5},{5... | collective-permute-start | bytes 835592 | tf_op jit(solution)/shard_map/ppermute | solution.py:449
  72.9 7.7 %collective-permute-start.14 = (bf16[136,512]{1,0:T(8,128)(2,1)S(1)}, bf16[136,512]{1,0:T(8,128)(2,1)S(1)}, u32[]{:S(2)}, u32[]{:S(2)}) collective-permute-start(bf16[136,512]{1,0:T(8,128)(2,1)S(1)} %add.54.refs_0_), channel_id=1, source_target_pairs={{0,24},{4,28},{8,16},{12,20},{16,8},{20,12},{24,0},{28,4},{1,25},{... | collective-permute-start | bytes 417800 | tf_op jit(solution)/shard_map/ppermute | solution.py:449
  77.4 7.5 %collective-permute-start.13 = (bf16[136,512]{1,0:T(8,128)(2,1)S(1)}, bf16[136,512]{1,0:T(8,128)(2,1)S(1)}, u32[]{:S(2)}, u32[]{:S(2)}) collective-permute-start(bf16[136,512]{1,0:T(8,128)(2,1)S(1)} %add.54.refs_0_), channel_id=1, source_target_pairs={{0,16},{4,20},{8,24},{12,28},{16,0},{20,4},{24,8},{28,12},{1,17},{... | collective-permute-start | bytes 417800 | tf_op jit(solution)/shard_map/ppermute | solution.py:449
  77.9 8.4 %collective-permute-start.12 = (bf16[136,512]{1,0:T(8,128)(2,1)S(1)}, bf16[136,512]{1,0:T(8,128)(2,1)S(1)}, u32[]{:S(2)}, u32[]{:S(2)}) collective-permute-start(bf16[136,512]{1,0:T(8,128)(2,1)S(1)} %add.54.refs_0_), channel_id=1, source_target_pairs={{0,8},{4,12},{8,0},{12,4},{16,24},{20,28},{24,16},{28,20},{1,9},{5... | collective-permute-start | bytes 417800 | tf_op jit(solution)/shard_map/ppermute | solution.py:449

commit v4 on v3

--- a/solution.py
+++ b/solution.py
@@ -53,7 +53,7 @@
         "both": split(whole, 2),
         "short": split(whole[:, :extent]),
         "inverse": split(np.concatenate([-back[extent:], back[:extent]])),
-        "around": split(-back[extent - 8 :]),
+        "around": split(-back[extent - STRIP :]),
     }
 
 
@@ -105,17 +105,17 @@
         first = halo_ref[lead - extent :] if b == 0 else u_ref[(b - 1) * extent : b * extent]
         us_ref[b] = product(both_ref[...], jnp.concatenate([first, last] * 2, axis=0))
     for b in range(blocks):
-        matrix = around_ref[...] if b == 0 else around_ref[8:]
-        rows = slice(0, extent + 8) if b == 0 else slice(8 + b * extent, 8 + (b + 1) * extent)
+        matrix = around_ref[...] if b == 0 else around_ref[STRIP:]
+        rows = slice(0 if b == 0 else STRIP + b * extent, STRIP + (b + 1) * extent)
         p_ref[rows] = convolved(matrix, us_ref.at[b], hs_ref, high_p.at[b], low_p.at[b])
     ahead = halo_ref[lead - extent - STRIP : lead - extent].astype(F32)[STRIP - 1 :]
     final = u_ref[extent - STRIP : extent].astype(F32)[STRIP - 1 :]
     mend = h_ref[extent - 1 : extent] * (ahead + final)
     at_second = lax.broadcasted_iota(jnp.int32, (8, width), 0) == 6
-    before = p_ref[:8] + jnp.where(at_second, mend, 0.0)
+    before = p_ref[8:STRIP] + jnp.where(at_second, mend, 0.0)
     w = [w_ref[i : i + 1] for i in range(w_ref.shape[0])]
     for at in strips(z_ref.shape[0]):
-        p = p_ref[8 + at.start : 8 + at.stop]
+        p = p_ref[STRIP + at.start : STRIP + at.stop]
         z_ref[at] = filtered(p, before, w)
         before = p[-8:]
 
@@ -167,9 +167,9 @@
             cr, ci = (real, imaginary) if cr is None else (cr + real, ci + imaginary)
         put_halves(cr, high_c, low_c, at)
         put_halves(ci, high_c, low_c, im)
-    lags = product(inverse_ref[: extent + 8], stacked_rows(high_c, low_c)) * scale
+    lags = product(inverse_ref[: extent + STRIP], stacked_rows(high_c, low_c)) * scale
     at_last = lax.broadcasted_iota(jnp.int32, (8, width), 0) == 1
-    after = lags[extent:] + jnp.where(at_last, mend * scale, 0.0)
+    after = lags[extent : extent + 8] + jnp.where(at_last, mend * scale, 0.0)
     value_sums = [jnp.zeros((8, width), F32) for _ in range(taps)]
     for row in range(extent - STRIP, -1, -STRIP):
         c = lags[row : row + STRIP]
@@ -370,7 +370,7 @@
         jax.ShapeDtypeStruct((rows, width), BF16),
     ]
     scratch = [((extent, block), BF16)] * 2 + [((blocks, 2 * extent, block), BF16)] * 2
-    scratch += [((8 + rows, block), F32)]
+    scratch += [((STRIP + rows, block), F32)]
     constants = [matrices[name] for name in ("both", "short", "around")]
 
     def body(u_ref, *refs):
@@ -386,7 +386,7 @@
     rows, width = u.shape
     extent, taps, lead = h.shape[0], gate.shape[0], halo.shape[0]
     blocks = rows // extent
-    count, part = extent + -(-2 * taps // 8) * 8, width // shares
+    count, part = extent + -(-2 * taps // 16) * 16, width // shares
     outs = [
         jax.ShapeDtypeStruct((rows - lead, width), BF16),
         jax.ShapeDtypeStruct((lead, width), F32),

time: 88.2 us -> 88.6 us (level)
  transfers between devices with their start and end apart: 15 -> 15, of which waited for: 12 -> 11; matrix products, arithmetic and copies ran while one was open for 3% -> 3% of each run, Pallas kernels for 9% -> 9%
where the time goes in v4:
time: 88.6 us; the launch traced here: 88.3 us
  waiting for transfers between devices  39.5 us (45%)
  starting transfers between devices  25.5 us (29%)
  Pallas kernels  18.8 us (21%)
  local copies, waits for them, and re-layouts  2.33 us (3%)
  other arithmetic  1.38 us (2%)
    ppermute x6, waiting for transfers between devices, exchange(): lax.ppermute(pieces[k], axis, [(i, (i + k) % count) for i in range(count)])  26.2 us
    pallas_call x2, Pallas kernels, call(): pl.pallas_call(kernel, in_specs=[IN_SMEM] + [ANYWHERE] * n_pieces + [ANYW...  15.6 us
    ppermute x7, waiting for transfers between devices, partner(): return lax.ppermute(x, axis, [(i, i ^ bit) for i in range(count)])  12.2 us
    ppermute x7, starting transfers between devices, partner(): return lax.ppermute(x, axis, [(i, i ^ bit) for i in range(count)])  12.1 us
    ppermute x6, starting transfers between devices, exchange(): lax.ppermute(pieces[k], axis, [(i, (i + k) % count) for i in range(count)])  9.99 us
    ppermute x2, starting transfers between devices, shifted(): return lax.ppermute(x, axis, pairs)  3.43 us
    dynamic_slice x2, local copies, waits for them, and re-layouts, slices(): lax.dynamic_slice_in_dim(x, lax.rem(me + k, count) * width + start, part,...  2.29 us
  transfers between devices with their start and end apart: 15, of which 11 were waited for; matrix products, arithmetic and copies ran while one was open for 3% of the time, Pallas kernels for 9%

profile of v4, /device:TPU:0, one launch (start us, length us, event | category | flops | bytes accessed | tf_op | source)
XLA Modules:
  0.0 88.3 jit_solution(17732905085714703502)
XLA Ops:
  0.7 1.4 %constant_dynamic-slice_fusion.4 = (bf16[64,2048]{1,0:T(8,128)(2,1)S(1)}, bf16[64,2048]{1,0:T(8,128)(2,1)S(1)}, bf16[64,2048]{1,0:T(8,128)(2,1)S(1)}, bf16[64,2048]{1,0:T(8,128)(2,1)S(1)}) fusion(bf16[64,8192]{1,0:T(8,128)(2,1)} %param.12, s32[]{:T(128)S(6)} %select_n.25, s32[]{:T(128)S(6)} %select_n.23, s32[]{:T(128)S(6)} %select_n.22, s32[]{:T(128)S(6)} %select_n.24), kind=kLoop, calls=%fused_computation.7 | loop fusion | bytes 2097168 | tf_op jit(solution)/shard_map/dynamic_slice | solution.py:424
  2.1 5.1 %collective-permute-start.3 = (bf16[64,2048]{1,0:T(8,128)(2,1)S(1)}, bf16[64,2048]{1,0:T(8,128)(2,1)S(1)}, u32[]{:S(2)}, u32[]{:S(2)}) collective-permute-start(bf16[64,2048]{1,0:T(8,128)(2,1)S(1)} %get-tuple-element.60), channel_id=1, source_target_pairs={{0,3},{1,0},{2,1},{3,2},{4,7},{5,4},{6,5},{7,6},{8,11},{9,8},{10,9... | collective-permute-start | bytes 786440 | tf_op jit(solution)/shard_map/ppermute | solution.py:433
  7.2 1.1 %collective-permute-start.2 = (bf16[64,2048]{1,0:T(8,128)(2,1)S(1)}, bf16[64,2048]{1,0:T(8,128)(2,1)S(1)}, u32[]{:S(2)}, u32[]{:S(2)}) collective-permute-start(bf16[64,2048]{1,0:T(8,128)(2,1)S(1)} %get-tuple-element.63), channel_id=1, source_target_pairs={{0,2},{1,3},{2,0},{3,1},{4,6},{5,7},{6,4},{7,5},{8,10},{9,11},{10,... | collective-permute-start | bytes 786440 | tf_op jit(solution)/shard_map/ppermute | solution.py:433
  8.3 0.9 %constant_dynamic-slice_fusion = (bf16[64,2048]{1,0:T(8,128)(2,1)}, bf16[64,2048]{1,0:T(8,128)(2,1)}, bf16[64,2048]{1,0:T(8,128)(2,1)S(1)}, bf16[64,2048]{1,0:T(8,128)(2,1)}) fusion(bf16[64,8192]{1,0:T(8,128)(2,1)S(1)} %copy-done.7, s32[]{:T(128)S(6)} %select_n.25, s32[]{:T(128)S(6)} %select_n.23, s32[]{:T(128)S(6)} %select_n.22, s32[]{:T(128)S(6)} %select_n.24), kind=kLoop, calls=%fused_computation.3 | loop fusion | bytes 2097168 | tf_op jit(solution)/shard_map/dynamic_slice | solution.py:424
  9.2 4.7 %collective-permute-done.3.refs_3_.refs_4_ = bf16[64,2048]{1,0:T(8,128)(2,1)S(1)} collective-permute-done((bf16[64,2048]{1,0:T(8,128)(2,1)S(1)}, bf16[64,2048]{1,0:T(8,128)(2,1)S(1)}, u32[]{:S(2)}, u32[]{:S(2)}) %collective-permute-start.3) | collective-permute-done | bytes 262176 | tf_op jit(solution)/shard_map/ppermute | solution.py:433
  13.9 6.6 %collective-permute-done.1.refs_1_.refs_2_ = bf16[64,2048]{1,0:T(8,128)(2,1)S(1)} collective-permute-done((bf16[64,2048]{1,0:T(8,128)(2,1)S(1)}, bf16[64,2048]{1,0:T(8,128)(2,1)S(1)}, u32[]{:S(2)}, u32[]{:S(2)}) %collective-permute-start.1) | collective-permute-done | bytes 262176 | tf_op jit(solution)/shard_map/ppermute | solution.py:433
  20.5 9.0 %collective-permute-done.2.refs_2_.refs_3_ = bf16[64,2048]{1,0:T(8,128)(2,1)S(1)} collective-permute-done((bf16[64,2048]{1,0:T(8,128)(2,1)S(1)}, bf16[64,2048]{1,0:T(8,128)(2,1)S(1)}, u32[]{:S(2)}, u32[]{:S(2)}) %collective-permute-start.2) | collective-permute-done | bytes 262176 | tf_op jit(solution)/shard_map/ppermute | solution.py:433
  29.5 0.2 collective-permute-start.4
  29.7 3.4 %collective-permute-start.5 = (bf16[64,2048]{1,0:T(8,128)(2,1)}, bf16[64,2048]{1,0:T(8,128)(2,1)}, u32[]{:S(2)}, u32[]{:S(2)}) collective-permute-start(bf16[64,2048]{1,0:T(8,128)(2,1)} %get-tuple-element.34), channel_id=1, source_target_pairs={{0,2},{1,3},{2,0},{3,1},{4,6},{5,7},{6,4},{7,5},{8,10},{9,11},{10,... | collective-permute-start | bytes 786440 | tf_op jit(solution)/shard_map/ppermute | solution.py:433
  33.0 0.3 collective-permute-start.6
  33.4 1.5 %tail_step.1 = bf16[144,2048]{1,0:T(8,128)(2,1)} custom-call(s32[2]{0:T(128)S(1)} %pad_add_fusion.me_ref.refs_0_, bf16[64,2048]{1,0:T(8,128)(2,1)S(1)} %get-tuple-element.36.refs_0_.refs_1_, bf16[64,2048]{1,0:T(8,128)(2,1)S(1)} %collective-permute-done.1.refs_1_.refs_2_, bf16[64,2048]{1,0:T(8,128)(2,1)S(1)} %collective-permute-done.2.refs_2_.refs_3_, ...), custom_call_target="tpu_custom_call" | custom-call | flops 1000 | bytes 1000 | tf_op jit(solution)/shard_map/tail_step/pallas_call | solution.py:346
  34.9 3.3 %conditional.1 = (bf16[144,2048]{1,0:T(8,128)(2,1)}) conditional(s32[]{:T(128)} %convert_element_type.21, () %tuple.17, bf16[144,2048]{1,0:T(8,128)(2,1)} %tail_step.1), branch_computations={%region_0.1_spmd, %region_1.2_spmd} | conditional | bytes 2359344 | solution.py:444
  34.9 2.1 %collective-permute-start = (bf16[144,2048]{1,0:T(8,128)(2,1)}, bf16[144,2048]{1,0:T(8,128)(2,1)}, u32[]{:S(2)}, u32[]{:S(2)}) collective-permute-start(bf16[144,2048]{1,0:T(8,128)(2,1)} %param.1), channel_id=1, source_target_pairs={{0,4},{4,8},{8,12},{12,16},{16,20},{20,24},{24,28},{1,5},{5,9},{9,... | collective-permute-start | bytes 1769480 | tf_op jit(solution)/shard_map/cond/branch_1_fun/ppermute | solution.py:440
  37.0 1.1 %collective-permute-done = bf16[144,2048]{1,0:T(8,128)(2,1)} collective-permute-done((bf16[144,2048]{1,0:T(8,128)(2,1)}, bf16[144,2048]{1,0:T(8,128)(2,1)}, u32[]{:S(2)}, u32[]{:S(2)}) %collective-permute-start) | collective-permute-done | bytes 589856 | tf_op jit(solution)/shard_map/cond/branch_1_fun/ppermute | solution.py:440
  38.2 6.1 %signal_step.1 = (f32[2,256,2048]{2,1,0:T(8,128)S(1)}, f32[256,2048]{1,0:T(8,128)S(1)}, f32[256,2048]{1,0:T(8,128)S(1)}, bf16[256,2048]{1,0:T(8,128)(2,1)S(1)}) custom-call(s32[2]{0:T(128)S(1)} %pad_add_fusion.me_ref.refs_0_, bf16[64,2048]{1,0:T(8,128)(2,1)S(1)} %get-tuple-element.36.refs_0_.refs_1_, ...), custom_call_target="tpu_custom_call" | custom-call | flops 1000 | bytes 1000 | tf_op jit(solution)/shard_map/signal_step/pallas_call | solution.py:308
  44.3 5.9 %collective-permute-done.5.refs_3_ = bf16[64,2048]{1,0:T(8,128)(2,1)} collective-permute-done((bf16[64,2048]{1,0:T(8,128)(2,1)}, bf16[64,2048]{1,0:T(8,128)(2,1)}, u32[]{:S(2)}, u32[]{:S(2)}) %collective-permute-start.5) | collective-permute-done | bytes 262176 | tf_op jit(solution)/shard_map/ppermute | solution.py:433
  50.2 9.5 %gradient_step.1 = (bf16[112,2048]{1,0:T(8,128)(2,1)S(1)}, f32[144,2048]{1,0:T(8,128)S(1)}, bf16[144,2048]{1,0:T(8,128)(2,1)S(1)}, f32[144,512]{1,0:T(8,128)S(1)...) custom-call(s32[2]{0:T(128)S(1)} %pad_add_fusion.me_ref.refs_0_, ...), custom_call_target="tpu_custom_call" | custom-call | flops 20000000000 | bytes 100000000 | tf_op jit(solution)/shard_map/gradient_step/pallas_call | solution.py:308
  59.7 4.0 %collective-permute-start.7 = (bf16[144,512]{1,0:T(8,128)(2,1)S(1)}, bf16[144,512]{1,0:T(8,128)(2,1)S(1)}, u32[]{:S(2)}, u32[]{:S(2)}) collective-permute-start(bf16[144,512]{1,0:T(8,128)(2,1)S(1)} %get-tuple-element.47), channel_id=1, source_target_pairs={{0,8},{4,12},{8,0},{12,4},{16,24},{20,28},{24,16},{28,20},{1,9},{5... | collective-permute-start | bytes 442376 | tf_op jit(solution)/shard_map/ppermute | solution.py:449
  63.7 1.5 %collective-permute-start.8 = (bf16[144,512]{1,0:T(8,128)(2,1)S(1)}, bf16[144,512]{1,0:T(8,128)(2,1)S(1)}, u32[]{:S(2)}, u32[]{:S(2)}) collective-permute-start(bf16[144,512]{1,0:T(8,128)(2,1)S(1)} %get-tuple-element.48), channel_id=1, source_target_pairs={{0,16},{4,20},{8,24},{12,28},{16,0},{20,4},{24,8},{28,12},{1,17},{... | collective-permute-start | bytes 442376 | tf_op jit(solution)/shard_map/ppermute | solution.py:449
  65.2 0.9 collective-permute-start.9
  66.1 1.3 %collective-permute-start.11 = (bf16[144,2048]{1,0:T(8,128)(2,1)S(1)}, bf16[144,2048]{1,0:T(8,128)(2,1)S(1)}, u32[]{:S(2)}, u32[]{:S(2)}) collective-permute-start(bf16[144,2048]{1,0:T(8,128)(2,1)S(1)} %get-tuple-element.50), channel_id=1, source_target_pairs={{4,0},{8,4},{12,8},{16,12},{20,16},{24,20},{28,24},{5,1},{9,5},{13... | collective-permute-start | bytes 1769480 | tf_op jit(solution)/shard_map/ppermute | solution.py:440
  67.4 0.5 collective-permute-done.7
  67.8 3.6 %collective-permute-done.8 = bf16[144,512]{1,0:T(8,128)(2,1)S(1)} collective-permute-done((bf16[144,512]{1,0:T(8,128)(2,1)S(1)}, bf16[144,512]{1,0:T(8,128)(2,1)S(1)}, u32[]{:S(2)}, u32[]{:S(2)}) %collective-permute-start.8) | collective-permute-done | bytes 147488 | tf_op jit(solution)/shard_map/ppermute | solution.py:449
  71.6 1.6 %collective-permute-done.10 = f32[144,512]{1,0:T(8,128)S(1)} collective-permute-done((f32[144,512]{1,0:T(8,128)S(1)}, f32[144,512]{1,0:T(8,128)S(1)}, u32[]{:S(2)}, u32[]{:S(2)}) %collective-permute-start.10) | collective-permute-done | bytes 294944 | tf_op jit(solution)/shard_map/ppermute | solution.py:449
  73.2 4.2 %collective-permute-start.14 = (bf16[144,512]{1,0:T(8,128)(2,1)S(1)}, bf16[144,512]{1,0:T(8,128)(2,1)S(1)}, u32[]{:S(2)}, u32[]{:S(2)}) collective-permute-start(bf16[144,512]{1,0:T(8,128)(2,1)S(1)} %add.54.refs_0_), channel_id=1, source_target_pairs={{0,24},{4,28},{8,16},{12,20},{16,8},{20,12},{24,0},{28,4},{1,25},{... | collective-permute-start | bytes 442376 | tf_op jit(solution)/shard_map/ppermute | solution.py:449
  77.4 0.5 collective-permute-start.13
  78.0 0.9 %collective-permute-start.12 = (bf16[144,512]{1,0:T(8,128)(2,1)S(1)}, bf16[144,512]{1,0:T(8,128)(2,1)S(1)}, u32[]{:S(2)}, u32[]{:S(2)}) collective-permute-start(bf16[144,512]{1,0:T(8,128)(2,1)S(1)} %add.54.refs_0_), channel_id=1, source_target_pairs={{0,8},{4,12},{8,0},{12,4},{16,24},{20,28},{24,16},{28,20},{1,9},{5... | collective-permute-start | bytes 442376 | tf_op jit(solution)/shard_map/ppermute | solution.py:449
  79.0 1.1 %pad_maximum_fusion = bf16[256,2048]{1,0:T(8,128)(2,1)} fusion(bf16[144,2048]{1,0:T(8,128)(2,1)S(1)} %add_convert_fusion, bf16[112,2048]{1,0:T(8,128)(2,1)S(1)} %get-tuple-element.44), kind=kLoop, calls=%fused_computation.1 | loop fusion | flops 2097152 | bytes 2097152 | tf_op jit(solution)/shard_map/concatenate | solution.py:531
  80.1 0.8 collective-permute-done.14.refs_3_
  80.8 4.5 %collective-permute-done.13.refs_2_ = bf16[144,512]{1,0:T(8,128)(2,1)S(1)} collective-permute-done((bf16[144,512]{1,0:T(8,128)(2,1)S(1)}, bf16[144,512]{1,0:T(8,128)(2,1)S(1)}, u32[]{:S(2)}, u32[]{:S(2)}) %collective-permute-start.13) | collective-permute-done | bytes 147488 | tf_op jit(solution)/shard_map/ppermute | solution.py:449
  85.3 1.4 %collective-permute-done.12.refs_1_ = bf16[144,512]{1,0:T(8,128)(2,1)S(1)} collective-permute-done((bf16[144,512]{1,0:T(8,128)(2,1)S(1)}, bf16[144,512]{1,0:T(8,128)(2,1)S(1)}, u32[]{:S(2)}, u32[]{:S(2)}) %collective-permute-start.12) | collective-permute-done | bytes 147488 | tf_op jit(solution)/shard_map/ppermute | solution.py:449
  86.7 1.7 %finish_step.1 = (f32[128,2048]{1,0:T(8,128)}, f32[3,2048]{1,0:T(4,128)}, f32[3,2048]{1,0:T(4,128)}) custom-call(s32[2]{0:T(128)S(1)} %pad_add_fusion.me_ref.refs_0_, bf16[144,512]{1,0:T(8,128)(2,1)S(1)} %add.54.refs_0_, bf16[144,512]{1,0:T(8,128)(2,1)S(1)} %collective-permute-done.12.refs_1_, bf16[144,512]{1,0:T(8,128)(2,1)S(1)} %collective-permute-done.13.refs_2_, ...), custom_call_target="tpu_custom_call" | custom-call | flops 1000 | bytes 1000 | tf_op jit(solution)/shard_map/finish_step/pallas_call | solution.py:479
  (26 shorter events, 0.4 us)
Async XLA Ops:
  0.7 7.6 %copy-start.7 = (bf16[64,8192]{1,0:T(8,128)(2,1)S(1)}, bf16[64,8192]{1,0:T(8,128)(2,1)}, u32[]{:S(2)}) copy-start(bf16[64,8192]{1,0:T(8,128)(2,1)} %param.11) | copy-start | bytes 3145732
  2.1 11.8 %collective-permute-start.3 = (bf16[64,2048]{1,0:T(8,128)(2,1)S(1)}, bf16[64,2048]{1,0:T(8,128)(2,1)S(1)}, u32[]{:S(2)}, u32[]{:S(2)}) collective-permute-start(bf16[64,2048]{1,0:T(8,128)(2,1)S(1)} %get-tuple-element.60), channel_id=1, source_target_pairs={{0,3},{1,0},{2,1},{3,2},{4,7},{5,4},{6,5},{7,6},{8,11},{9,8},{10,9... | collective-permute-start | bytes 786440 | tf_op jit(solution)/shard_map/ppermute | solution.py:433
  7.2 13.3 %collective-permute-start.1 = (bf16[64,2048]{1,0:T(8,128)(2,1)S(1)}, bf16[64,2048]{1,0:T(8,128)(2,1)S(1)}, u32[]{:S(2)}, u32[]{:S(2)}) collective-permute-start(bf16[64,2048]{1,0:T(8,128)(2,1)S(1)} %get-tuple-element.61), channel_id=1, source_target_pairs={{0,1},{1,2},{2,3},{3,0},{4,5},{5,6},{6,7},{7,4},{8,9},{9,10},{10,1... | collective-permute-start | bytes 786440 | tf_op jit(solution)/shard_map/ppermute | solution.py:433
  7.2 31.0 %copy-start = (f32[128,2048]{1,0:T(8,128)S(1)}, f32[128,2048]{1,0:T(8,128)}, u32[]{:S(2)}) copy-start(f32[128,2048]{1,0:T(8,128)} %refs_7_.3) | copy-start | bytes 3145732
  7.2 31.0 %copy-start.1 = (bf16[256,512]{1,0:T(8,128)(2,1)S(1)}, bf16[256,512]{1,0:T(8,128)(2,1)}, u32[]{:S(2)}) copy-start(bf16[256,512]{1,0:T(8,128)(2,1)} %constant.51.clone.refs_8_) | copy-start | bytes 786436
  7.2 31.0 %copy-start.2 = (bf16[144,768]{1,0:T(8,128)(2,1)S(1)}, bf16[144,768]{1,0:T(8,128)(2,1)}, u32[]{:S(2)}) copy-start(bf16[144,768]{1,0:T(8,128)(2,1)} %constant.54.clone.refs_10_) | copy-start | bytes 663556
  7.2 31.0 %copy-start.3 = (bf16[256,384]{1,0:T(8,128)(2,1)S(1)}, bf16[256,384]{1,0:T(8,128)(2,1)}, u32[]{:S(2)}) copy-start(bf16[256,384]{1,0:T(8,128)(2,1)} %constant.52.clone.refs_9_.refs_13_) | copy-start | bytes 589828
  7.2 31.0 %copy-start.4 = (f32[3,2048]{1,0:T(4,128)S(1)}, f32[3,2048]{1,0:T(4,128)}, u32[]{:S(2)}) copy-start(f32[3,2048]{1,0:T(4,128)} %refs_12_.1) | copy-start | bytes 73732
  7.2 22.3 %collective-permute-start.2 = (bf16[64,2048]{1,0:T(8,128)(2,1)S(1)}, bf16[64,2048]{1,0:T(8,128)(2,1)S(1)}, u32[]{:S(2)}, u32[]{:S(2)}) collective-permute-start(bf16[64,2048]{1,0:T(8,128)(2,1)S(1)} %get-tuple-element.63), channel_id=1, source_target_pairs={{0,2},{1,3},{2,0},{3,1},{4,6},{5,7},{6,4},{7,5},{8,10},{9,11},{10,... | collective-permute-start | bytes 786440 | tf_op jit(solution)/shard_map/ppermute | solution.py:433
  29.5 14.8 %collective-permute-start.4 = (bf16[64,2048]{1,0:T(8,128)(2,1)}, bf16[64,2048]{1,0:T(8,128)(2,1)S(1)}, u32[]{:S(2)}, u32[]{:S(2)}) collective-permute-start(bf16[64,2048]{1,0:T(8,128)(2,1)} %get-tuple-element.33), channel_id=1, source_target_pairs={{0,1},{1,2},{2,3},{3,0},{4,5},{5,6},{6,7},{7,4},{8,9},{9,10},{10,1... | collective-permute-start | bytes 786440 | tf_op jit(solution)/shard_map/ppermute | solution.py:433
  29.7 20.5 %collective-permute-start.5 = (bf16[64,2048]{1,0:T(8,128)(2,1)}, bf16[64,2048]{1,0:T(8,128)(2,1)}, u32[]{:S(2)}, u32[]{:S(2)}) collective-permute-start(bf16[64,2048]{1,0:T(8,128)(2,1)} %get-tuple-element.34), channel_id=1, source_target_pairs={{0,2},{1,3},{2,0},{3,1},{4,6},{5,7},{6,4},{7,5},{8,10},{9,11},{10,... | collective-permute-start | bytes 786440 | tf_op jit(solution)/shard_map/ppermute | solution.py:433
  33.0 17.2 %collective-permute-start.6 = (bf16[64,2048]{1,0:T(8,128)(2,1)}, bf16[64,2048]{1,0:T(8,128)(2,1)}, u32[]{:S(2)}, u32[]{:S(2)}) collective-permute-start(bf16[64,2048]{1,0:T(8,128)(2,1)} %get-tuple-element.35), channel_id=1, source_target_pairs={{0,3},{1,0},{2,1},{3,2},{4,7},{5,4},{6,5},{7,6},{8,11},{9,8},{10,9... | collective-permute-start | bytes 786440 | tf_op jit(solution)/shard_map/ppermute | solution.py:433
  34.9 15.3 %copy-start.5 = (f32[3,2048]{1,0:T(4,128)S(1)}, f32[3,2048]{1,0:T(4,128)}, u32[]{:S(2)}) copy-start(f32[3,2048]{1,0:T(4,128)} %refs_11_.1) | copy-start | bytes 73732
  34.9 3.3 %collective-permute-start = (bf16[144,2048]{1,0:T(8,128)(2,1)}, bf16[144,2048]{1,0:T(8,128)(2,1)}, u32[]{:S(2)}, u32[]{:S(2)}) collective-permute-start(bf16[144,2048]{1,0:T(8,128)(2,1)} %param.1), channel_id=1, source_target_pairs={{0,4},{4,8},{8,12},{12,16},{16,20},{20,24},{24,28},{1,5},{5,9},{9,... | collective-permute-start | bytes 1769480 | tf_op jit(solution)/shard_map/cond/branch_1_fun/ppermute | solution.py:440
  38.2 12.0 %copy-start.6 = (bf16[256,768]{1,0:T(8,128)(2,1)S(1)}, bf16[256,768]{1,0:T(8,128)(2,1)}, u32[]{:S(2)}) copy-start(bf16[256,768]{1,0:T(8,128)(2,1)} %constant.53.clone.refs_14_) | copy-start | bytes 1179652
  59.7 8.1 %collective-permute-start.7 = (bf16[144,512]{1,0:T(8,128)(2,1)S(1)}, bf16[144,512]{1,0:T(8,128)(2,1)S(1)}, u32[]{:S(2)}, u32[]{:S(2)}) collective-permute-start(bf16[144,512]{1,0:T(8,128)(2,1)S(1)} %get-tuple-element.47), channel_id=1, source_target_pairs={{0,8},{4,12},{8,0},{12,4},{16,24},{20,28},{24,16},{28,20},{1,9},{5... | collective-permute-start | bytes 442376 | tf_op jit(solution)/shard_map/ppermute | solution.py:449
  63.7 7.7 %collective-permute-start.8 = (bf16[144,512]{1,0:T(8,128)(2,1)S(1)}, bf16[144,512]{1,0:T(8,128)(2,1)S(1)}, u32[]{:S(2)}, u32[]{:S(2)}) collective-permute-start(bf16[144,512]{1,0:T(8,128)(2,1)S(1)} %get-tuple-element.48), channel_id=1, source_target_pairs={{0,16},{4,20},{8,24},{12,28},{16,0},{20,4},{24,8},{28,12},{1,17},{... | collective-permute-start | bytes 442376 | tf_op jit(solution)/shard_map/ppermute | solution.py:449
  65.2 6.2 %collective-permute-start.9 = (bf16[144,512]{1,0:T(8,128)(2,1)S(1)}, bf16[144,512]{1,0:T(8,128)(2,1)S(1)}, u32[]{:S(2)}, u32[]{:S(2)}) collective-permute-start(bf16[144,512]{1,0:T(8,128)(2,1)S(1)} %get-tuple-element.49), channel_id=1, source_target_pairs={{0,24},{4,28},{8,16},{12,20},{16,8},{20,12},{24,0},{28,4},{1,25},{... | collective-permute-start | bytes 442376 | tf_op jit(solution)/shard_map/ppermute | solution.py:449
  66.1 7.1 %collective-permute-start.11 = (bf16[144,2048]{1,0:T(8,128)(2,1)S(1)}, bf16[144,2048]{1,0:T(8,128)(2,1)S(1)}, u32[]{:S(2)}, u32[]{:S(2)}) collective-permute-start(bf16[144,2048]{1,0:T(8,128)(2,1)S(1)} %get-tuple-element.50), channel_id=1, source_target_pairs={{4,0},{8,4},{12,8},{16,12},{20,16},{24,20},{28,24},{5,1},{9,5},{13... | collective-permute-start | bytes 1769480 | tf_op jit(solution)/shard_map/ppermute | solution.py:440
  71.5 1.6 %collective-permute-start.10 = (f32[144,512]{1,0:T(8,128)S(1)}, f32[144,512]{1,0:T(8,128)S(1)}, u32[]{:S(2)}, u32[]{:S(2)}) collective-permute-start(f32[144,512]{1,0:T(8,128)S(1)} %add_add_fusion), channel_id=1, source_target_pairs={{0,4},{4,0},{8,12},{12,8},{16,20},{20,16},{24,28},{28,24},{1,5},{5... | collective-permute-start | bytes 884744 | tf_op jit(solution)/shard_map/ppermute | solution.py:449
  73.2 7.6 %collective-permute-start.14 = (bf16[144,512]{1,0:T(8,128)(2,1)S(1)}, bf16[144,512]{1,0:T(8,128)(2,1)S(1)}, u32[]{:S(2)}, u32[]{:S(2)}) collective-permute-start(bf16[144,512]{1,0:T(8,128)(2,1)S(1)} %add.54.refs_0_), channel_id=1, source_target_pairs={{0,24},{4,28},{8,16},{12,20},{16,8},{20,12},{24,0},{28,4},{1,25},{... | collective-permute-start | bytes 442376 | tf_op jit(solution)/shard_map/ppermute | solution.py:449
  77.4 7.8 %collective-permute-start.13 = (bf16[144,512]{1,0:T(8,128)(2,1)S(1)}, bf16[144,512]{1,0:T(8,128)(2,1)S(1)}, u32[]{:S(2)}, u32[]{:S(2)}) collective-permute-start(bf16[144,512]{1,0:T(8,128)(2,1)S(1)} %add.54.refs_0_), channel_id=1, source_target_pairs={{0,16},{4,20},{8,24},{12,28},{16,0},{20,4},{24,8},{28,12},{1,17},{... | collective-permute-start | bytes 442376 | tf_op jit(solution)/shard_map/ppermute | solution.py:449
  78.0 8.7 %collective-permute-start.12 = (bf16[144,512]{1,0:T(8,128)(2,1)S(1)}, bf16[144,512]{1,0:T(8,128)(2,1)S(1)}, u32[]{:S(2)}, u32[]{:S(2)}) collective-permute-start(bf16[144,512]{1,0:T(8,128)(2,1)S(1)} %add.54.refs_0_), channel_id=1, source_target_pairs={{0,8},{4,12},{8,0},{12,4},{16,24},{20,28},{24,16},{28,20},{1,9},{5... | collective-permute-start | bytes 442376 | tf_op jit(solution)/shard_map/ppermute | solution.py:449

commit v5 on v4

--- a/solution.py
+++ b/solution.py
@@ -429,7 +429,7 @@
 def exchange(pieces, axis):
     count = lax.axis_size(axis)
     got = [pieces[0]] + [None] * (count - 1)
-    for k in sorted(range(1, count), key=lambda k: abs(2 * k - count)):
+    for k in sorted(range(1, count), key=lambda k: -abs(2 * k - count)):
         got[k] = lax.ppermute(pieces[k], axis, [(i, (i + k) % count) for i in range(count)])
     return got
 

time: 88.6 us -> 88.6 us (level)
  no operation moved by 1% of the time
where the time goes in v5:
time: 88.6 us; the launch traced here: 88.3 us
  waiting for transfers between devices  39.5 us (45%)
  starting transfers between devices  25.5 us (29%)
  Pallas kernels  18.8 us (21%)
  local copies, waits for them, and re-layouts  2.33 us (3%)
  other arithmetic  1.38 us (2%)
    ppermute x6, waiting for transfers between devices, exchange(): lax.ppermute(pieces[k], axis, [(i, (i + k) % count) for i in range(count)])  26.2 us
    pallas_call x2, Pallas kernels, call(): pl.pallas_call(kernel, in_specs=[IN_SMEM] + [ANYWHERE] * n_pieces + [ANYW...  15.6 us
    ppermute x7, waiting for transfers between devices, partner(): return lax.ppermute(x, axis, [(i, i ^ bit) for i in range(count)])  12.2 us
    ppermute x7, starting transfers between devices, partner(): return lax.ppermute(x, axis, [(i, i ^ bit) for i in range(count)])  12.1 us
    ppermute x6, starting transfers between devices, exchange(): lax.ppermute(pieces[k], axis, [(i, (i + k) % count) for i in range(count)])  9.99 us
    ppermute x2, starting transfers between devices, shifted(): return lax.ppermute(x, axis, pairs)  3.43 us
    dynamic_slice x2, local copies, waits for them, and re-layouts, slices(): lax.dynamic_slice_in_dim(x, lax.rem(me + k, count) * width + start, part,...  2.29 us
  transfers between devices with their start and end apart: 15, of which 11 were waited for; matrix products, arithmetic and copies ran while one was open for 3% of the time, Pallas kernels for 9%

profile of v5, /device:TPU:0, one launch (start us, length us, event | category | flops | bytes accessed | tf_op | source)
XLA Modules:
  0.0 88.3 jit_solution(17732905085714703502)
XLA Ops:
  0.7 1.4 %constant_dynamic-slice_fusion.4 = (bf16[64,2048]{1,0:T(8,128)(2,1)S(1)}, bf16[64,2048]{1,0:T(8,128)(2,1)S(1)}, bf16[64,2048]{1,0:T(8,128)(2,1)S(1)}, bf16[64,2048]{1,0:T(8,128)(2,1)S(1)}) fusion(bf16[64,8192]{1,0:T(8,128)(2,1)} %param.12, s32[]{:T(128)S(6)} %select_n.25, s32[]{:T(128)S(6)} %select_n.23, s32[]{:T(128)S(6)} %select_n.22, s32[]{:T(128)S(6)} %select_n.24), kind=kLoop, calls=%fused_computation.7 | loop fusion | bytes 2097168 | tf_op jit(solution)/shard_map/dynamic_slice | solution.py:424
  2.1 5.1 %collective-permute-start.3 = (bf16[64,2048]{1,0:T(8,128)(2,1)S(1)}, bf16[64,2048]{1,0:T(8,128)(2,1)S(1)}, u32[]{:S(2)}, u32[]{:S(2)}) collective-permute-start(bf16[64,2048]{1,0:T(8,128)(2,1)S(1)} %get-tuple-element.60), channel_id=1, source_target_pairs={{0,3},{1,0},{2,1},{3,2},{4,7},{5,4},{6,5},{7,6},{8,11},{9,8},{10,9... | collective-permute-start | bytes 786440 | tf_op jit(solution)/shard_map/ppermute | solution.py:433
  7.2 1.1 %collective-permute-start.2 = (bf16[64,2048]{1,0:T(8,128)(2,1)S(1)}, bf16[64,2048]{1,0:T(8,128)(2,1)S(1)}, u32[]{:S(2)}, u32[]{:S(2)}) collective-permute-start(bf16[64,2048]{1,0:T(8,128)(2,1)S(1)} %get-tuple-element.63), channel_id=1, source_target_pairs={{0,2},{1,3},{2,0},{3,1},{4,6},{5,7},{6,4},{7,5},{8,10},{9,11},{10,... | collective-permute-start | bytes 786440 | tf_op jit(solution)/shard_map/ppermute | solution.py:433
  8.3 0.9 %constant_dynamic-slice_fusion = (bf16[64,2048]{1,0:T(8,128)(2,1)}, bf16[64,2048]{1,0:T(8,128)(2,1)}, bf16[64,2048]{1,0:T(8,128)(2,1)S(1)}, bf16[64,2048]{1,0:T(8,128)(2,1)}) fusion(bf16[64,8192]{1,0:T(8,128)(2,1)S(1)} %copy-done.7, s32[]{:T(128)S(6)} %select_n.25, s32[]{:T(128)S(6)} %select_n.23, s32[]{:T(128)S(6)} %select_n.22, s32[]{:T(128)S(6)} %select_n.24), kind=kLoop, calls=%fused_computation.3 | loop fusion | bytes 2097168 | tf_op jit(solution)/shard_map/dynamic_slice | solution.py:424
  9.2 4.7 %collective-permute-done.3.refs_3_.refs_4_ = bf16[64,2048]{1,0:T(8,128)(2,1)S(1)} collective-permute-done((bf16[64,2048]{1,0:T(8,128)(2,1)S(1)}, bf16[64,2048]{1,0:T(8,128)(2,1)S(1)}, u32[]{:S(2)}, u32[]{:S(2)}) %collective-permute-start.3) | collective-permute-done | bytes 262176 | tf_op jit(solution)/shard_map/ppermute | solution.py:433
  13.9 6.6 %collective-permute-done.1.refs_1_.refs_2_ = bf16[64,2048]{1,0:T(8,128)(2,1)S(1)} collective-permute-done((bf16[64,2048]{1,0:T(8,128)(2,1)S(1)}, bf16[64,2048]{1,0:T(8,128)(2,1)S(1)}, u32[]{:S(2)}, u32[]{:S(2)}) %collective-permute-start.1) | collective-permute-done | bytes 262176 | tf_op jit(solution)/shard_map/ppermute | solution.py:433
  20.5 9.0 %collective-permute-done.2.refs_2_.refs_3_ = bf16[64,2048]{1,0:T(8,128)(2,1)S(1)} collective-permute-done((bf16[64,2048]{1,0:T(8,128)(2,1)S(1)}, bf16[64,2048]{1,0:T(8,128)(2,1)S(1)}, u32[]{:S(2)}, u32[]{:S(2)}) %collective-permute-start.2) | collective-permute-done | bytes 262176 | tf_op jit(solution)/shard_map/ppermute | solution.py:433
  29.5 0.2 collective-permute-start.4
  29.7 3.4 %collective-permute-start.5 = (bf16[64,2048]{1,0:T(8,128)(2,1)}, bf16[64,2048]{1,0:T(8,128)(2,1)}, u32[]{:S(2)}, u32[]{:S(2)}) collective-permute-start(bf16[64,2048]{1,0:T(8,128)(2,1)} %get-tuple-element.34), channel_id=1, source_target_pairs={{0,2},{1,3},{2,0},{3,1},{4,6},{5,7},{6,4},{7,5},{8,10},{9,11},{10,... | collective-permute-start | bytes 786440 | tf_op jit(solution)/shard_map/ppermute | solution.py:433
  33.0 0.3 collective-permute-start.6
  33.4 1.5 %tail_step.1 = bf16[144,2048]{1,0:T(8,128)(2,1)} custom-call(s32[2]{0:T(128)S(1)} %pad_add_fusion.me_ref.refs_0_, bf16[64,2048]{1,0:T(8,128)(2,1)S(1)} %get-tuple-element.36.refs_0_.refs_1_, bf16[64,2048]{1,0:T(8,128)(2,1)S(1)} %collective-permute-done.1.refs_1_.refs_2_, bf16[64,2048]{1,0:T(8,128)(2,1)S(1)} %collective-permute-done.2.refs_2_.refs_3_, ...), custom_call_target="tpu_custom_call" | custom-call | flops 1000 | bytes 1000 | tf_op jit(solution)/shard_map/tail_step/pallas_call | solution.py:346
  34.9 3.3 %conditional.1 = (bf16[144,2048]{1,0:T(8,128)(2,1)}) conditional(s32[]{:T(128)} %convert_element_type.21, () %tuple.17, bf16[144,2048]{1,0:T(8,128)(2,1)} %tail_step.1), branch_computations={%region_0.1_spmd, %region_1.2_spmd} | conditional | bytes 2359344 | solution.py:444
  34.9 2.1 %collective-permute-start = (bf16[144,2048]{1,0:T(8,128)(2,1)}, bf16[144,2048]{1,0:T(8,128)(2,1)}, u32[]{:S(2)}, u32[]{:S(2)}) collective-permute-start(bf16[144,2048]{1,0:T(8,128)(2,1)} %param.1), channel_id=1, source_target_pairs={{0,4},{4,8},{8,12},{12,16},{16,20},{20,24},{24,28},{1,5},{5,9},{9,... | collective-permute-start | bytes 1769480 | tf_op jit(solution)/shard_map/cond/branch_1_fun/ppermute | solution.py:440
  37.0 1.1 %collective-permute-done = bf16[144,2048]{1,0:T(8,128)(2,1)} collective-permute-done((bf16[144,2048]{1,0:T(8,128)(2,1)}, bf16[144,2048]{1,0:T(8,128)(2,1)}, u32[]{:S(2)}, u32[]{:S(2)}) %collective-permute-start) | collective-permute-done | bytes 589856 | tf_op jit(solution)/shard_map/cond/branch_1_fun/ppermute | solution.py:440
  38.2 6.1 %signal_step.1 = (f32[2,256,2048]{2,1,0:T(8,128)S(1)}, f32[256,2048]{1,0:T(8,128)S(1)}, f32[256,2048]{1,0:T(8,128)S(1)}, bf16[256,2048]{1,0:T(8,128)(2,1)S(1)}) custom-call(s32[2]{0:T(128)S(1)} %pad_add_fusion.me_ref.refs_0_, bf16[64,2048]{1,0:T(8,128)(2,1)S(1)} %get-tuple-element.36.refs_0_.refs_1_, ...), custom_call_target="tpu_custom_call" | custom-call | flops 1000 | bytes 1000 | tf_op jit(solution)/shard_map/signal_step/pallas_call | solution.py:308
  44.3 5.9 %collective-permute-done.5.refs_3_ = bf16[64,2048]{1,0:T(8,128)(2,1)} collective-permute-done((bf16[64,2048]{1,0:T(8,128)(2,1)}, bf16[64,2048]{1,0:T(8,128)(2,1)}, u32[]{:S(2)}, u32[]{:S(2)}) %collective-permute-start.5) | collective-permute-done | bytes 262176 | tf_op jit(solution)/shard_map/ppermute | solution.py:433
  50.2 9.5 %gradient_step.1 = (bf16[112,2048]{1,0:T(8,128)(2,1)S(1)}, f32[144,2048]{1,0:T(8,128)S(1)}, bf16[144,2048]{1,0:T(8,128)(2,1)S(1)}, f32[144,512]{1,0:T(8,128)S(1)...) custom-call(s32[2]{0:T(128)S(1)} %pad_add_fusion.me_ref.refs_0_, ...), custom_call_target="tpu_custom_call" | custom-call | flops 20000000000 | bytes 100000000 | tf_op jit(solution)/shard_map/gradient_step/pallas_call | solution.py:308
  59.7 4.0 %collective-permute-start.7 = (bf16[144,512]{1,0:T(8,128)(2,1)S(1)}, bf16[144,512]{1,0:T(8,128)(2,1)S(1)}, u32[]{:S(2)}, u32[]{:S(2)}) collective-permute-start(bf16[144,512]{1,0:T(8,128)(2,1)S(1)} %get-tuple-element.47), channel_id=1, source_target_pairs={{0,8},{4,12},{8,0},{12,4},{16,24},{20,28},{24,16},{28,20},{1,9},{5... | collective-permute-start | bytes 442376 | tf_op jit(solution)/shard_map/ppermute | solution.py:449
  63.7 1.5 %collective-permute-start.8 = (bf16[144,512]{1,0:T(8,128)(2,1)S(1)}, bf16[144,512]{1,0:T(8,128)(2,1)S(1)}, u32[]{:S(2)}, u32[]{:S(2)}) collective-permute-start(bf16[144,512]{1,0:T(8,128)(2,1)S(1)} %get-tuple-element.48), channel_id=1, source_target_pairs={{0,16},{4,20},{8,24},{12,28},{16,0},{20,4},{24,8},{28,12},{1,17},{... | collective-permute-start | bytes 442376 | tf_op jit(solution)/shard_map/ppermute | solution.py:449
  65.2 0.9 collective-permute-start.9
  66.1 1.3 %collective-permute-start.11 = (bf16[144,2048]{1,0:T(8,128)(2,1)S(1)}, bf16[144,2048]{1,0:T(8,128)(2,1)S(1)}, u32[]{:S(2)}, u32[]{:S(2)}) collective-permute-start(bf16[144,2048]{1,0:T(8,128)(2,1)S(1)} %get-tuple-element.50), channel_id=1, source_target_pairs={{4,0},{8,4},{12,8},{16,12},{20,16},{24,20},{28,24},{5,1},{9,5},{13... | collective-permute-start | bytes 1769480 | tf_op jit(solution)/shard_map/ppermute | solution.py:440
  67.4 0.5 collective-permute-done.7
  67.8 3.6 %collective-permute-done.8 = bf16[144,512]{1,0:T(8,128)(2,1)S(1)} collective-permute-done((bf16[144,512]{1,0:T(8,128)(2,1)S(1)}, bf16[144,512]{1,0:T(8,128)(2,1)S(1)}, u32[]{:S(2)}, u32[]{:S(2)}) %collective-permute-start.8) | collective-permute-done | bytes 147488 | tf_op jit(solution)/shard_map/ppermute | solution.py:449
  71.6 1.6 %collective-permute-done.10 = f32[144,512]{1,0:T(8,128)S(1)} collective-permute-done((f32[144,512]{1,0:T(8,128)S(1)}, f32[144,512]{1,0:T(8,128)S(1)}, u32[]{:S(2)}, u32[]{:S(2)}) %collective-permute-start.10) | collective-permute-done | bytes 294944 | tf_op jit(solution)/shard_map/ppermute | solution.py:449
  73.2 4.2 %collective-permute-start.14 = (bf16[144,512]{1,0:T(8,128)(2,1)S(1)}, bf16[144,512]{1,0:T(8,128)(2,1)S(1)}, u32[]{:S(2)}, u32[]{:S(2)}) collective-permute-start(bf16[144,512]{1,0:T(8,128)(2,1)S(1)} %add.54.refs_0_), channel_id=1, source_target_pairs={{0,24},{4,28},{8,16},{12,20},{16,8},{20,12},{24,0},{28,4},{1,25},{... | collective-permute-start | bytes 442376 | tf_op jit(solution)/shard_map/ppermute | solution.py:449
  77.4 0.5 collective-permute-start.13
  78.0 0.9 %collective-permute-start.12 = (bf16[144,512]{1,0:T(8,128)(2,1)S(1)}, bf16[144,512]{1,0:T(8,128)(2,1)S(1)}, u32[]{:S(2)}, u32[]{:S(2)}) collective-permute-start(bf16[144,512]{1,0:T(8,128)(2,1)S(1)} %add.54.refs_0_), channel_id=1, source_target_pairs={{0,8},{4,12},{8,0},{12,4},{16,24},{20,28},{24,16},{28,20},{1,9},{5... | collective-permute-start | bytes 442376 | tf_op jit(solution)/shard_map/ppermute | solution.py:449
  79.0 1.1 %pad_maximum_fusion = bf16[256,2048]{1,0:T(8,128)(2,1)} fusion(bf16[144,2048]{1,0:T(8,128)(2,1)S(1)} %add_convert_fusion, bf16[112,2048]{1,0:T(8,128)(2,1)S(1)} %get-tuple-element.44), kind=kLoop, calls=%fused_computation.1 | loop fusion | flops 2097152 | bytes 2097152 | tf_op jit(solution)/shard_map/concatenate | solution.py:531
  80.1 0.8 collective-permute-done.14.refs_3_
  80.8 4.5 %collective-permute-done.13.refs_2_ = bf16[144,512]{1,0:T(8,128)(2,1)S(1)} collective-permute-done((bf16[144,512]{1,0:T(8,128)(2,1)S(1)}, bf16[144,512]{1,0:T(8,128)(2,1)S(1)}, u32[]{:S(2)}, u32[]{:S(2)}) %collective-permute-start.13) | collective-permute-done | bytes 147488 | tf_op jit(solution)/shard_map/ppermute | solution.py:449
  85.3 1.4 %collective-permute-done.12.refs_1_ = bf16[144,512]{1,0:T(8,128)(2,1)S(1)} collective-permute-done((bf16[144,512]{1,0:T(8,128)(2,1)S(1)}, bf16[144,512]{1,0:T(8,128)(2,1)S(1)}, u32[]{:S(2)}, u32[]{:S(2)}) %collective-permute-start.12) | collective-permute-done | bytes 147488 | tf_op jit(solution)/shard_map/ppermute | solution.py:449
  86.7 1.7 %finish_step.1 = (f32[128,2048]{1,0:T(8,128)}, f32[3,2048]{1,0:T(4,128)}, f32[3,2048]{1,0:T(4,128)}) custom-call(s32[2]{0:T(128)S(1)} %pad_add_fusion.me_ref.refs_0_, bf16[144,512]{1,0:T(8,128)(2,1)S(1)} %add.54.refs_0_, bf16[144,512]{1,0:T(8,128)(2,1)S(1)} %collective-permute-done.12.refs_1_, bf16[144,512]{1,0:T(8,128)(2,1)S(1)} %collective-permute-done.13.refs_2_, ...), custom_call_target="tpu_custom_call" | custom-call | flops 1000 | bytes 1000 | tf_op jit(solution)/shard_map/finish_step/pallas_call | solution.py:479
  (26 shorter events, 0.4 us)
Async XLA Ops:
  0.7 7.6 %copy-start.7 = (bf16[64,8192]{1,0:T(8,128)(2,1)S(1)}, bf16[64,8192]{1,0:T(8,128)(2,1)}, u32[]{:S(2)}) copy-start(bf16[64,8192]{1,0:T(8,128)(2,1)} %param.11) | copy-start | bytes 3145732
  2.1 11.8 %collective-permute-start.3 = (bf16[64,2048]{1,0:T(8,128)(2,1)S(1)}, bf16[64,2048]{1,0:T(8,128)(2,1)S(1)}, u32[]{:S(2)}, u32[]{:S(2)}) collective-permute-start(bf16[64,2048]{1,0:T(8,128)(2,1)S(1)} %get-tuple-element.60), channel_id=1, source_target_pairs={{0,3},{1,0},{2,1},{3,2},{4,7},{5,4},{6,5},{7,6},{8,11},{9,8},{10,9... | collective-permute-start | bytes 786440 | tf_op jit(solution)/shard_map/ppermute | solution.py:433
  7.2 13.3 %collective-permute-start.1 = (bf16[64,2048]{1,0:T(8,128)(2,1)S(1)}, bf16[64,2048]{1,0:T(8,128)(2,1)S(1)}, u32[]{:S(2)}, u32[]{:S(2)}) collective-permute-start(bf16[64,2048]{1,0:T(8,128)(2,1)S(1)} %get-tuple-element.61), channel_id=1, source_target_pairs={{0,1},{1,2},{2,3},{3,0},{4,5},{5,6},{6,7},{7,4},{8,9},{9,10},{10,1... | collective-permute-start | bytes 786440 | tf_op jit(solution)/shard_map/ppermute | solution.py:433
  7.2 31.0 %copy-start = (f32[128,2048]{1,0:T(8,128)S(1)}, f32[128,2048]{1,0:T(8,128)}, u32[]{:S(2)}) copy-start(f32[128,2048]{1,0:T(8,128)} %refs_7_.3) | copy-start | bytes 3145732
  7.2 31.0 %copy-start.1 = (bf16[256,512]{1,0:T(8,128)(2,1)S(1)}, bf16[256,512]{1,0:T(8,128)(2,1)}, u32[]{:S(2)}) copy-start(bf16[256,512]{1,0:T(8,128)(2,1)} %constant.51.clone.refs_8_) | copy-start | bytes 786436
  7.2 31.0 %copy-start.2 = (bf16[144,768]{1,0:T(8,128)(2,1)S(1)}, bf16[144,768]{1,0:T(8,128)(2,1)}, u32[]{:S(2)}) copy-start(bf16[144,768]{1,0:T(8,128)(2,1)} %constant.54.clone.refs_10_) | copy-start | bytes 663556
  7.2 31.0 %copy-start.3 = (bf16[256,384]{1,0:T(8,128)(2,1)S(1)}, bf16[256,384]{1,0:T(8,128)(2,1)}, u32[]{:S(2)}) copy-start(bf16[256,384]{1,0:T(8,128)(2,1)} %constant.52.clone.refs_9_.refs_13_) | copy-start | bytes 589828
  7.2 31.0 %copy-start.4 = (f32[3,2048]{1,0:T(4,128)S(1)}, f32[3,2048]{1,0:T(4,128)}, u32[]{:S(2)}) copy-start(f32[3,2048]{1,0:T(4,128)} %refs_12_.1) | copy-start | bytes 73732
  7.2 22.3 %collective-permute-start.2 = (bf16[64,2048]{1,0:T(8,128)(2,1)S(1)}, bf16[64,2048]{1,0:T(8,128)(2,1)S(1)}, u32[]{:S(2)}, u32[]{:S(2)}) collective-permute-start(bf16[64,2048]{1,0:T(8,128)(2,1)S(1)} %get-tuple-element.63), channel_id=1, source_target_pairs={{0,2},{1,3},{2,0},{3,1},{4,6},{5,7},{6,4},{7,5},{8,10},{9,11},{10,... | collective-permute-start | bytes 786440 | tf_op jit(solution)/shard_map/ppermute | solution.py:433
  29.5 14.8 %collective-permute-start.4 = (bf16[64,2048]{1,0:T(8,128)(2,1)}, bf16[64,2048]{1,0:T(8,128)(2,1)S(1)}, u32[]{:S(2)}, u32[]{:S(2)}) collective-permute-start(bf16[64,2048]{1,0:T(8,128)(2,1)} %get-tuple-element.33), channel_id=1, source_target_pairs={{0,1},{1,2},{2,3},{3,0},{4,5},{5,6},{6,7},{7,4},{8,9},{9,10},{10,1... | collective-permute-start | bytes 786440 | tf_op jit(solution)/shard_map/ppermute | solution.py:433
  29.7 20.5 %collective-permute-start.5 = (bf16[64,2048]{1,0:T(8,128)(2,1)}, bf16[64,2048]{1,0:T(8,128)(2,1)}, u32[]{:S(2)}, u32[]{:S(2)}) collective-permute-start(bf16[64,2048]{1,0:T(8,128)(2,1)} %get-tuple-element.34), channel_id=1, source_target_pairs={{0,2},{1,3},{2,0},{3,1},{4,6},{5,7},{6,4},{7,5},{8,10},{9,11},{10,... | collective-permute-start | bytes 786440 | tf_op jit(solution)/shard_map/ppermute | solution.py:433
  33.0 17.2 %collective-permute-start.6 = (bf16[64,2048]{1,0:T(8,128)(2,1)}, bf16[64,2048]{1,0:T(8,128)(2,1)}, u32[]{:S(2)}, u32[]{:S(2)}) collective-permute-start(bf16[64,2048]{1,0:T(8,128)(2,1)} %get-tuple-element.35), channel_id=1, source_target_pairs={{0,3},{1,0},{2,1},{3,2},{4,7},{5,4},{6,5},{7,6},{8,11},{9,8},{10,9... | collective-permute-start | bytes 786440 | tf_op jit(solution)/shard_map/ppermute | solution.py:433
  34.9 15.3 %copy-start.5 = (f32[3,2048]{1,0:T(4,128)S(1)}, f32[3,2048]{1,0:T(4,128)}, u32[]{:S(2)}) copy-start(f32[3,2048]{1,0:T(4,128)} %refs_11_.1) | copy-start | bytes 73732
  34.9 3.3 %collective-permute-start = (bf16[144,2048]{1,0:T(8,128)(2,1)}, bf16[144,2048]{1,0:T(8,128)(2,1)}, u32[]{:S(2)}, u32[]{:S(2)}) collective-permute-start(bf16[144,2048]{1,0:T(8,128)(2,1)} %param.1), channel_id=1, source_target_pairs={{0,4},{4,8},{8,12},{12,16},{16,20},{20,24},{24,28},{1,5},{5,9},{9,... | collective-permute-start | bytes 1769480 | tf_op jit(solution)/shard_map/cond/branch_1_fun/ppermute | solution.py:440
  38.2 12.0 %copy-start.6 = (bf16[256,768]{1,0:T(8,128)(2,1)S(1)}, bf16[256,768]{1,0:T(8,128)(2,1)}, u32[]{:S(2)}) copy-start(bf16[256,768]{1,0:T(8,128)(2,1)} %constant.53.clone.refs_14_) | copy-start | bytes 1179652
  59.7 8.1 %collective-permute-start.7 = (bf16[144,512]{1,0:T(8,128)(2,1)S(1)}, bf16[144,512]{1,0:T(8,128)(2,1)S(1)}, u32[]{:S(2)}, u32[]{:S(2)}) collective-permute-start(bf16[144,512]{1,0:T(8,128)(2,1)S(1)} %get-tuple-element.47), channel_id=1, source_target_pairs={{0,8},{4,12},{8,0},{12,4},{16,24},{20,28},{24,16},{28,20},{1,9},{5... | collective-permute-start | bytes 442376 | tf_op jit(solution)/shard_map/ppermute | solution.py:449
  63.7 7.7 %collective-permute-start.8 = (bf16[144,512]{1,0:T(8,128)(2,1)S(1)}, bf16[144,512]{1,0:T(8,128)(2,1)S(1)}, u32[]{:S(2)}, u32[]{:S(2)}) collective-permute-start(bf16[144,512]{1,0:T(8,128)(2,1)S(1)} %get-tuple-element.48), channel_id=1, source_target_pairs={{0,16},{4,20},{8,24},{12,28},{16,0},{20,4},{24,8},{28,12},{1,17},{... | collective-permute-start | bytes 442376 | tf_op jit(solution)/shard_map/ppermute | solution.py:449
  65.2 6.2 %collective-permute-start.9 = (bf16[144,512]{1,0:T(8,128)(2,1)S(1)}, bf16[144,512]{1,0:T(8,128)(2,1)S(1)}, u32[]{:S(2)}, u32[]{:S(2)}) collective-permute-start(bf16[144,512]{1,0:T(8,128)(2,1)S(1)} %get-tuple-element.49), channel_id=1, source_target_pairs={{0,24},{4,28},{8,16},{12,20},{16,8},{20,12},{24,0},{28,4},{1,25},{... | collective-permute-start | bytes 442376 | tf_op jit(solution)/shard_map/ppermute | solution.py:449
  66.1 7.1 %collective-permute-start.11 = (bf16[144,2048]{1,0:T(8,128)(2,1)S(1)}, bf16[144,2048]{1,0:T(8,128)(2,1)S(1)}, u32[]{:S(2)}, u32[]{:S(2)}) collective-permute-start(bf16[144,2048]{1,0:T(8,128)(2,1)S(1)} %get-tuple-element.50), channel_id=1, source_target_pairs={{4,0},{8,4},{12,8},{16,12},{20,16},{24,20},{28,24},{5,1},{9,5},{13... | collective-permute-start | bytes 1769480 | tf_op jit(solution)/shard_map/ppermute | solution.py:440
  71.5 1.6 %collective-permute-start.10 = (f32[144,512]{1,0:T(8,128)S(1)}, f32[144,512]{1,0:T(8,128)S(1)}, u32[]{:S(2)}, u32[]{:S(2)}) collective-permute-start(f32[144,512]{1,0:T(8,128)S(1)} %add_add_fusion), channel_id=1, source_target_pairs={{0,4},{4,0},{8,12},{12,8},{16,20},{20,16},{24,28},{28,24},{1,5},{5... | collective-permute-start | bytes 884744 | tf_op jit(solution)/shard_map/ppermute | solution.py:449
  73.2 7.6 %collective-permute-start.14 = (bf16[144,512]{1,0:T(8,128)(2,1)S(1)}, bf16[144,512]{1,0:T(8,128)(2,1)S(1)}, u32[]{:S(2)}, u32[]{:S(2)}) collective-permute-start(bf16[144,512]{1,0:T(8,128)(2,1)S(1)} %add.54.refs_0_), channel_id=1, source_target_pairs={{0,24},{4,28},{8,16},{12,20},{16,8},{20,12},{24,0},{28,4},{1,25},{... | collective-permute-start | bytes 442376 | tf_op jit(solution)/shard_map/ppermute | solution.py:449
  77.4 7.8 %collective-permute-start.13 = (bf16[144,512]{1,0:T(8,128)(2,1)S(1)}, bf16[144,512]{1,0:T(8,128)(2,1)S(1)}, u32[]{:S(2)}, u32[]{:S(2)}) collective-permute-start(bf16[144,512]{1,0:T(8,128)(2,1)S(1)} %add.54.refs_0_), channel_id=1, source_target_pairs={{0,16},{4,20},{8,24},{12,28},{16,0},{20,4},{24,8},{28,12},{1,17},{... | collective-permute-start | bytes 442376 | tf_op jit(solution)/shard_map/ppermute | solution.py:449
  78.0 8.7 %collective-permute-start.12 = (bf16[144,512]{1,0:T(8,128)(2,1)S(1)}, bf16[144,512]{1,0:T(8,128)(2,1)S(1)}, u32[]{:S(2)}, u32[]{:S(2)}) collective-permute-start(bf16[144,512]{1,0:T(8,128)(2,1)S(1)} %add.54.refs_0_), channel_id=1, source_target_pairs={{0,8},{4,12},{8,0},{12,4},{16,24},{20,28},{24,16},{28,20},{1,9},{5... | collective-permute-start | bytes 442376 | tf_op jit(solution)/shard_map/ppermute | solution.py:449

commit v6 on v4

--- a/solution.py
+++ b/solution.py
@@ -513,7 +513,8 @@
     )
     sizes = (extent, taps, taps)
     if shares > 1:
-        terms = [terms[0]] + [partner(terms[k], "ctx", 2 * k).astype(F32) for k in range(1, shares)]
+        for k in range(shares - 1, 0, -1):
+            terms[k] = partner(terms[k], "ctx", 2 * k).astype(F32)
         incoming = shifted(head, "ctx", -1)
         while len(terms) > 1:
             terms = [a + b for a, b in zip(terms[::2], terms[1::2])]

time: 88.6 us -> 88.6 us (level)
  no operation moved by 1% of the time
where the time goes in v6:
time: 88.6 us; the launch traced here: 88.3 us
  waiting for transfers between devices  39.5 us (45%)
  starting transfers between devices  25.5 us (29%)
  Pallas kernels  18.8 us (21%)
  local copies, waits for them, and re-layouts  2.33 us (3%)
  other arithmetic  1.38 us (2%)
    ppermute x6, waiting for transfers between devices, exchange(): lax.ppermute(pieces[k], axis, [(i, (i + k) % count) for i in range(count)])  26.2 us
    pallas_call x2, Pallas kernels, call(): pl.pallas_call(kernel, in_specs=[IN_SMEM] + [ANYWHERE] * n_pieces + [ANYW...  15.6 us
    ppermute x7, waiting for transfers between devices, partner(): return lax.ppermute(x, axis, [(i, i ^ bit) for i in range(count)])  12.2 us
    ppermute x7, starting transfers between devices, partner(): return lax.ppermute(x, axis, [(i, i ^ bit) for i in range(count)])  12.1 us
    ppermute x6, starting transfers between devices, exchange(): lax.ppermute(pieces[k], axis, [(i, (i + k) % count) for i in range(count)])  9.99 us
    ppermute x2, starting transfers between devices, shifted(): return lax.ppermute(x, axis, pairs)  3.43 us
    dynamic_slice x2, local copies, waits for them, and re-layouts, slices(): lax.dynamic_slice_in_dim(x, lax.rem(me + k, count) * width + start, part,...  2.29 us
  transfers between devices with their start and end apart: 15, of which 11 were waited for; matrix products, arithmetic and copies ran while one was open for 3% of the time, Pallas kernels for 9%

profile of v6, /device:TPU:0, one launch (start us, length us, event | category | flops | bytes accessed | tf_op | source)
XLA Modules:
  0.0 88.3 jit_solution(17732905085714703502)
XLA Ops:
  0.7 1.4 %constant_dynamic-slice_fusion.4 = (bf16[64,2048]{1,0:T(8,128)(2,1)S(1)}, bf16[64,2048]{1,0:T(8,128)(2,1)S(1)}, bf16[64,2048]{1,0:T(8,128)(2,1)S(1)}, bf16[64,2048]{1,0:T(8,128)(2,1)S(1)}) fusion(bf16[64,8192]{1,0:T(8,128)(2,1)} %param.12, s32[]{:T(128)S(6)} %select_n.25, s32[]{:T(128)S(6)} %select_n.23, s32[]{:T(128)S(6)} %select_n.22, s32[]{:T(128)S(6)} %select_n.24), kind=kLoop, calls=%fused_computation.7 | loop fusion | bytes 2097168 | tf_op jit(solution)/shard_map/dynamic_slice | solution.py:424
  2.1 5.1 %collective-permute-start.3 = (bf16[64,2048]{1,0:T(8,128)(2,1)S(1)}, bf16[64,2048]{1,0:T(8,128)(2,1)S(1)}, u32[]{:S(2)}, u32[]{:S(2)}) collective-permute-start(bf16[64,2048]{1,0:T(8,128)(2,1)S(1)} %get-tuple-element.60), channel_id=1, source_target_pairs={{0,3},{1,0},{2,1},{3,2},{4,7},{5,4},{6,5},{7,6},{8,11},{9,8},{10,9... | collective-permute-start | bytes 786440 | tf_op jit(solution)/shard_map/ppermute | solution.py:433
  7.2 1.1 %collective-permute-start.2 = (bf16[64,2048]{1,0:T(8,128)(2,1)S(1)}, bf16[64,2048]{1,0:T(8,128)(2,1)S(1)}, u32[]{:S(2)}, u32[]{:S(2)}) collective-permute-start(bf16[64,2048]{1,0:T(8,128)(2,1)S(1)} %get-tuple-element.63), channel_id=1, source_target_pairs={{0,2},{1,3},{2,0},{3,1},{4,6},{5,7},{6,4},{7,5},{8,10},{9,11},{10,... | collective-permute-start | bytes 786440 | tf_op jit(solution)/shard_map/ppermute | solution.py:433
  8.3 0.9 %constant_dynamic-slice_fusion = (bf16[64,2048]{1,0:T(8,128)(2,1)}, bf16[64,2048]{1,0:T(8,128)(2,1)}, bf16[64,2048]{1,0:T(8,128)(2,1)S(1)}, bf16[64,2048]{1,0:T(8,128)(2,1)}) fusion(bf16[64,8192]{1,0:T(8,128)(2,1)S(1)} %copy-done.7, s32[]{:T(128)S(6)} %select_n.25, s32[]{:T(128)S(6)} %select_n.23, s32[]{:T(128)S(6)} %select_n.22, s32[]{:T(128)S(6)} %select_n.24), kind=kLoop, calls=%fused_computation.3 | loop fusion | bytes 2097168 | tf_op jit(solution)/shard_map/dynamic_slice | solution.py:424
  9.2 4.7 %collective-permute-done.3.refs_3_.refs_4_ = bf16[64,2048]{1,0:T(8,128)(2,1)S(1)} collective-permute-done((bf16[64,2048]{1,0:T(8,128)(2,1)S(1)}, bf16[64,2048]{1,0:T(8,128)(2,1)S(1)}, u32[]{:S(2)}, u32[]{:S(2)}) %collective-permute-start.3) | collective-permute-done | bytes 262176 | tf_op jit(solution)/shard_map/ppermute | solution.py:433
  13.9 6.6 %collective-permute-done.1.refs_1_.refs_2_ = bf16[64,2048]{1,0:T(8,128)(2,1)S(1)} collective-permute-done((bf16[64,2048]{1,0:T(8,128)(2,1)S(1)}, bf16[64,2048]{1,0:T(8,128)(2,1)S(1)}, u32[]{:S(2)}, u32[]{:S(2)}) %collective-permute-start.1) | collective-permute-done | bytes 262176 | tf_op jit(solution)/shard_map/ppermute | solution.py:433
  20.5 9.0 %collective-permute-done.2.refs_2_.refs_3_ = bf16[64,2048]{1,0:T(8,128)(2,1)S(1)} collective-permute-done((bf16[64,2048]{1,0:T(8,128)(2,1)S(1)}, bf16[64,2048]{1,0:T(8,128)(2,1)S(1)}, u32[]{:S(2)}, u32[]{:S(2)}) %collective-permute-start.2) | collective-permute-done | bytes 262176 | tf_op jit(solution)/shard_map/ppermute | solution.py:433
  29.5 0.2 collective-permute-start.4
  29.7 3.4 %collective-permute-start.5 = (bf16[64,2048]{1,0:T(8,128)(2,1)}, bf16[64,2048]{1,0:T(8,128)(2,1)}, u32[]{:S(2)}, u32[]{:S(2)}) collective-permute-start(bf16[64,2048]{1,0:T(8,128)(2,1)} %get-tuple-element.34), channel_id=1, source_target_pairs={{0,2},{1,3},{2,0},{3,1},{4,6},{5,7},{6,4},{7,5},{8,10},{9,11},{10,... | collective-permute-start | bytes 786440 | tf_op jit(solution)/shard_map/ppermute | solution.py:433
  33.0 0.3 collective-permute-start.6
  33.4 1.5 %tail_step.1 = bf16[144,2048]{1,0:T(8,128)(2,1)} custom-call(s32[2]{0:T(128)S(1)} %pad_add_fusion.me_ref.refs_0_, bf16[64,2048]{1,0:T(8,128)(2,1)S(1)} %get-tuple-element.36.refs_0_.refs_1_, bf16[64,2048]{1,0:T(8,128)(2,1)S(1)} %collective-permute-done.1.refs_1_.refs_2_, bf16[64,2048]{1,0:T(8,128)(2,1)S(1)} %collective-permute-done.2.refs_2_.refs_3_, ...), custom_call_target="tpu_custom_call" | custom-call | flops 1000 | bytes 1000 | tf_op jit(solution)/shard_map/tail_step/pallas_call | solution.py:346
  34.9 3.3 %conditional.1 = (bf16[144,2048]{1,0:T(8,128)(2,1)}) conditional(s32[]{:T(128)} %convert_element_type.21, () %tuple.17, bf16[144,2048]{1,0:T(8,128)(2,1)} %tail_step.1), branch_computations={%region_0.1_spmd, %region_1.2_spmd} | conditional | bytes 2359344 | solution.py:444
  34.9 2.1 %collective-permute-start = (bf16[144,2048]{1,0:T(8,128)(2,1)}, bf16[144,2048]{1,0:T(8,128)(2,1)}, u32[]{:S(2)}, u32[]{:S(2)}) collective-permute-start(bf16[144,2048]{1,0:T(8,128)(2,1)} %param.1), channel_id=1, source_target_pairs={{0,4},{4,8},{8,12},{12,16},{16,20},{20,24},{24,28},{1,5},{5,9},{9,... | collective-permute-start | bytes 1769480 | tf_op jit(solution)/shard_map/cond/branch_1_fun/ppermute | solution.py:440
  37.0 1.1 %collective-permute-done = bf16[144,2048]{1,0:T(8,128)(2,1)} collective-permute-done((bf16[144,2048]{1,0:T(8,128)(2,1)}, bf16[144,2048]{1,0:T(8,128)(2,1)}, u32[]{:S(2)}, u32[]{:S(2)}) %collective-permute-start) | collective-permute-done | bytes 589856 | tf_op jit(solution)/shard_map/cond/branch_1_fun/ppermute | solution.py:440
  38.2 6.1 %signal_step.1 = (f32[2,256,2048]{2,1,0:T(8,128)S(1)}, f32[256,2048]{1,0:T(8,128)S(1)}, f32[256,2048]{1,0:T(8,128)S(1)}, bf16[256,2048]{1,0:T(8,128)(2,1)S(1)}) custom-call(s32[2]{0:T(128)S(1)} %pad_add_fusion.me_ref.refs_0_, bf16[64,2048]{1,0:T(8,128)(2,1)S(1)} %get-tuple-element.36.refs_0_.refs_1_, ...), custom_call_target="tpu_custom_call" | custom-call | flops 1000 | bytes 1000 | tf_op jit(solution)/shard_map/signal_step/pallas_call | solution.py:308
  44.3 5.9 %collective-permute-done.5.refs_3_ = bf16[64,2048]{1,0:T(8,128)(2,1)} collective-permute-done((bf16[64,2048]{1,0:T(8,128)(2,1)}, bf16[64,2048]{1,0:T(8,128)(2,1)}, u32[]{:S(2)}, u32[]{:S(2)}) %collective-permute-start.5) | collective-permute-done | bytes 262176 | tf_op jit(solution)/shard_map/ppermute | solution.py:433
  50.2 9.5 %gradient_step.1 = (bf16[112,2048]{1,0:T(8,128)(2,1)S(1)}, f32[144,2048]{1,0:T(8,128)S(1)}, bf16[144,2048]{1,0:T(8,128)(2,1)S(1)}, f32[144,512]{1,0:T(8,128)S(1)...) custom-call(s32[2]{0:T(128)S(1)} %pad_add_fusion.me_ref.refs_0_, ...), custom_call_target="tpu_custom_call" | custom-call | flops 20000000000 | bytes 100000000 | tf_op jit(solution)/shard_map/gradient_step/pallas_call | solution.py:308
  59.7 4.0 %collective-permute-start.7 = (bf16[144,512]{1,0:T(8,128)(2,1)S(1)}, bf16[144,512]{1,0:T(8,128)(2,1)S(1)}, u32[]{:S(2)}, u32[]{:S(2)}) collective-permute-start(bf16[144,512]{1,0:T(8,128)(2,1)S(1)} %get-tuple-element.47), channel_id=1, source_target_pairs={{0,8},{4,12},{8,0},{12,4},{16,24},{20,28},{24,16},{28,20},{1,9},{5... | collective-permute-start | bytes 442376 | tf_op jit(solution)/shard_map/ppermute | solution.py:449
  63.7 1.5 %collective-permute-start.8 = (bf16[144,512]{1,0:T(8,128)(2,1)S(1)}, bf16[144,512]{1,0:T(8,128)(2,1)S(1)}, u32[]{:S(2)}, u32[]{:S(2)}) collective-permute-start(bf16[144,512]{1,0:T(8,128)(2,1)S(1)} %get-tuple-element.48), channel_id=1, source_target_pairs={{0,16},{4,20},{8,24},{12,28},{16,0},{20,4},{24,8},{28,12},{1,17},{... | collective-permute-start | bytes 442376 | tf_op jit(solution)/shard_map/ppermute | solution.py:449
  65.2 0.9 collective-permute-start.9
  66.1 1.3 %collective-permute-start.11 = (bf16[144,2048]{1,0:T(8,128)(2,1)S(1)}, bf16[144,2048]{1,0:T(8,128)(2,1)S(1)}, u32[]{:S(2)}, u32[]{:S(2)}) collective-permute-start(bf16[144,2048]{1,0:T(8,128)(2,1)S(1)} %get-tuple-element.50), channel_id=1, source_target_pairs={{4,0},{8,4},{12,8},{16,12},{20,16},{24,20},{28,24},{5,1},{9,5},{13... | collective-permute-start | bytes 1769480 | tf_op jit(solution)/shard_map/ppermute | solution.py:440
  67.4 0.5 collective-permute-done.7
  67.8 3.6 %collective-permute-done.8 = bf16[144,512]{1,0:T(8,128)(2,1)S(1)} collective-permute-done((bf16[144,512]{1,0:T(8,128)(2,1)S(1)}, bf16[144,512]{1,0:T(8,128)(2,1)S(1)}, u32[]{:S(2)}, u32[]{:S(2)}) %collective-permute-start.8) | collective-permute-done | bytes 147488 | tf_op jit(solution)/shard_map/ppermute | solution.py:449
  71.6 1.6 %collective-permute-done.10 = f32[144,512]{1,0:T(8,128)S(1)} collective-permute-done((f32[144,512]{1,0:T(8,128)S(1)}, f32[144,512]{1,0:T(8,128)S(1)}, u32[]{:S(2)}, u32[]{:S(2)}) %collective-permute-start.10) | collective-permute-done | bytes 294944 | tf_op jit(solution)/shard_map/ppermute | solution.py:449
  73.2 4.2 %collective-permute-start.14 = (bf16[144,512]{1,0:T(8,128)(2,1)S(1)}, bf16[144,512]{1,0:T(8,128)(2,1)S(1)}, u32[]{:S(2)}, u32[]{:S(2)}) collective-permute-start(bf16[144,512]{1,0:T(8,128)(2,1)S(1)} %add.54.refs_0_), channel_id=1, source_target_pairs={{0,24},{4,28},{8,16},{12,20},{16,8},{20,12},{24,0},{28,4},{1,25},{... | collective-permute-start | bytes 442376 | tf_op jit(solution)/shard_map/ppermute | solution.py:449
  77.4 0.5 collective-permute-start.13
  78.0 0.9 %collective-permute-start.12 = (bf16[144,512]{1,0:T(8,128)(2,1)S(1)}, bf16[144,512]{1,0:T(8,128)(2,1)S(1)}, u32[]{:S(2)}, u32[]{:S(2)}) collective-permute-start(bf16[144,512]{1,0:T(8,128)(2,1)S(1)} %add.54.refs_0_), channel_id=1, source_target_pairs={{0,8},{4,12},{8,0},{12,4},{16,24},{20,28},{24,16},{28,20},{1,9},{5... | collective-permute-start | bytes 442376 | tf_op jit(solution)/shard_map/ppermute | solution.py:449
  79.0 1.1 %pad_maximum_fusion = bf16[256,2048]{1,0:T(8,128)(2,1)} fusion(bf16[144,2048]{1,0:T(8,128)(2,1)S(1)} %add_convert_fusion, bf16[112,2048]{1,0:T(8,128)(2,1)S(1)} %get-tuple-element.44), kind=kLoop, calls=%fused_computation.1 | loop fusion | flops 2097152 | bytes 2097152 | tf_op jit(solution)/shard_map/concatenate | solution.py:532
  80.1 0.8 collective-permute-done.14.refs_3_
  80.8 4.5 %collective-permute-done.13.refs_2_ = bf16[144,512]{1,0:T(8,128)(2,1)S(1)} collective-permute-done((bf16[144,512]{1,0:T(8,128)(2,1)S(1)}, bf16[144,512]{1,0:T(8,128)(2,1)S(1)}, u32[]{:S(2)}, u32[]{:S(2)}) %collective-permute-start.13) | collective-permute-done | bytes 147488 | tf_op jit(solution)/shard_map/ppermute | solution.py:449
  85.3 1.4 %collective-permute-done.12.refs_1_ = bf16[144,512]{1,0:T(8,128)(2,1)S(1)} collective-permute-done((bf16[144,512]{1,0:T(8,128)(2,1)S(1)}, bf16[144,512]{1,0:T(8,128)(2,1)S(1)}, u32[]{:S(2)}, u32[]{:S(2)}) %collective-permute-start.12) | collective-permute-done | bytes 147488 | tf_op jit(solution)/shard_map/ppermute | solution.py:449
  86.7 1.7 %finish_step.1 = (f32[128,2048]{1,0:T(8,128)}, f32[3,2048]{1,0:T(4,128)}, f32[3,2048]{1,0:T(4,128)}) custom-call(s32[2]{0:T(128)S(1)} %pad_add_fusion.me_ref.refs_0_, bf16[144,512]{1,0:T(8,128)(2,1)S(1)} %add.54.refs_0_, bf16[144,512]{1,0:T(8,128)(2,1)S(1)} %collective-permute-done.12.refs_1_, bf16[144,512]{1,0:T(8,128)(2,1)S(1)} %collective-permute-done.13.refs_2_, ...), custom_call_target="tpu_custom_call" | custom-call | flops 1000 | bytes 1000 | tf_op jit(solution)/shard_map/finish_step/pallas_call | solution.py:479
  (26 shorter events, 0.4 us)
Async XLA Ops:
  0.7 7.6 %copy-start.7 = (bf16[64,8192]{1,0:T(8,128)(2,1)S(1)}, bf16[64,8192]{1,0:T(8,128)(2,1)}, u32[]{:S(2)}) copy-start(bf16[64,8192]{1,0:T(8,128)(2,1)} %param.11) | copy-start | bytes 3145732
  2.1 11.8 %collective-permute-start.3 = (bf16[64,2048]{1,0:T(8,128)(2,1)S(1)}, bf16[64,2048]{1,0:T(8,128)(2,1)S(1)}, u32[]{:S(2)}, u32[]{:S(2)}) collective-permute-start(bf16[64,2048]{1,0:T(8,128)(2,1)S(1)} %get-tuple-element.60), channel_id=1, source_target_pairs={{0,3},{1,0},{2,1},{3,2},{4,7},{5,4},{6,5},{7,6},{8,11},{9,8},{10,9... | collective-permute-start | bytes 786440 | tf_op jit(solution)/shard_map/ppermute | solution.py:433
  7.2 13.3 %collective-permute-start.1 = (bf16[64,2048]{1,0:T(8,128)(2,1)S(1)}, bf16[64,2048]{1,0:T(8,128)(2,1)S(1)}, u32[]{:S(2)}, u32[]{:S(2)}) collective-permute-start(bf16[64,2048]{1,0:T(8,128)(2,1)S(1)} %get-tuple-element.61), channel_id=1, source_target_pairs={{0,1},{1,2},{2,3},{3,0},{4,5},{5,6},{6,7},{7,4},{8,9},{9,10},{10,1... | collective-permute-start | bytes 786440 | tf_op jit(solution)/shard_map/ppermute | solution.py:433
  7.2 31.0 %copy-start = (f32[128,2048]{1,0:T(8,128)S(1)}, f32[128,2048]{1,0:T(8,128)}, u32[]{:S(2)}) copy-start(f32[128,2048]{1,0:T(8,128)} %refs_7_.3) | copy-start | bytes 3145732
  7.2 31.0 %copy-start.1 = (bf16[256,512]{1,0:T(8,128)(2,1)S(1)}, bf16[256,512]{1,0:T(8,128)(2,1)}, u32[]{:S(2)}) copy-start(bf16[256,512]{1,0:T(8,128)(2,1)} %constant.51.clone.refs_8_) | copy-start | bytes 786436
  7.2 31.0 %copy-start.2 = (bf16[144,768]{1,0:T(8,128)(2,1)S(1)}, bf16[144,768]{1,0:T(8,128)(2,1)}, u32[]{:S(2)}) copy-start(bf16[144,768]{1,0:T(8,128)(2,1)} %constant.54.clone.refs_10_) | copy-start | bytes 663556
  7.2 31.0 %copy-start.3 = (bf16[256,384]{1,0:T(8,128)(2,1)S(1)}, bf16[256,384]{1,0:T(8,128)(2,1)}, u32[]{:S(2)}) copy-start(bf16[256,384]{1,0:T(8,128)(2,1)} %constant.52.clone.refs_9_.refs_13_) | copy-start | bytes 589828
  7.2 31.0 %copy-start.4 = (f32[3,2048]{1,0:T(4,128)S(1)}, f32[3,2048]{1,0:T(4,128)}, u32[]{:S(2)}) copy-start(f32[3,2048]{1,0:T(4,128)} %refs_12_.1) | copy-start | bytes 73732
  7.2 22.3 %collective-permute-start.2 = (bf16[64,2048]{1,0:T(8,128)(2,1)S(1)}, bf16[64,2048]{1,0:T(8,128)(2,1)S(1)}, u32[]{:S(2)}, u32[]{:S(2)}) collective-permute-start(bf16[64,2048]{1,0:T(8,128)(2,1)S(1)} %get-tuple-element.63), channel_id=1, source_target_pairs={{0,2},{1,3},{2,0},{3,1},{4,6},{5,7},{6,4},{7,5},{8,10},{9,11},{10,... | collective-permute-start | bytes 786440 | tf_op jit(solution)/shard_map/ppermute | solution.py:433
  29.5 14.8 %collective-permute-start.4 = (bf16[64,2048]{1,0:T(8,128)(2,1)}, bf16[64,2048]{1,0:T(8,128)(2,1)S(1)}, u32[]{:S(2)}, u32[]{:S(2)}) collective-permute-start(bf16[64,2048]{1,0:T(8,128)(2,1)} %get-tuple-element.33), channel_id=1, source_target_pairs={{0,1},{1,2},{2,3},{3,0},{4,5},{5,6},{6,7},{7,4},{8,9},{9,10},{10,1... | collective-permute-start | bytes 786440 | tf_op jit(solution)/shard_map/ppermute | solution.py:433
  29.7 20.5 %collective-permute-start.5 = (bf16[64,2048]{1,0:T(8,128)(2,1)}, bf16[64,2048]{1,0:T(8,128)(2,1)}, u32[]{:S(2)}, u32[]{:S(2)}) collective-permute-start(bf16[64,2048]{1,0:T(8,128)(2,1)} %get-tuple-element.34), channel_id=1, source_target_pairs={{0,2},{1,3},{2,0},{3,1},{4,6},{5,7},{6,4},{7,5},{8,10},{9,11},{10,... | collective-permute-start | bytes 786440 | tf_op jit(solution)/shard_map/ppermute | solution.py:433
  33.0 17.2 %collective-permute-start.6 = (bf16[64,2048]{1,0:T(8,128)(2,1)}, bf16[64,2048]{1,0:T(8,128)(2,1)}, u32[]{:S(2)}, u32[]{:S(2)}) collective-permute-start(bf16[64,2048]{1,0:T(8,128)(2,1)} %get-tuple-element.35), channel_id=1, source_target_pairs={{0,3},{1,0},{2,1},{3,2},{4,7},{5,4},{6,5},{7,6},{8,11},{9,8},{10,9... | collective-permute-start | bytes 786440 | tf_op jit(solution)/shard_map/ppermute | solution.py:433
  34.9 15.3 %copy-start.5 = (f32[3,2048]{1,0:T(4,128)S(1)}, f32[3,2048]{1,0:T(4,128)}, u32[]{:S(2)}) copy-start(f32[3,2048]{1,0:T(4,128)} %refs_11_.1) | copy-start | bytes 73732
  34.9 3.3 %collective-permute-start = (bf16[144,2048]{1,0:T(8,128)(2,1)}, bf16[144,2048]{1,0:T(8,128)(2,1)}, u32[]{:S(2)}, u32[]{:S(2)}) collective-permute-start(bf16[144,2048]{1,0:T(8,128)(2,1)} %param.1), channel_id=1, source_target_pairs={{0,4},{4,8},{8,12},{12,16},{16,20},{20,24},{24,28},{1,5},{5,9},{9,... | collective-permute-start | bytes 1769480 | tf_op jit(solution)/shard_map/cond/branch_1_fun/ppermute | solution.py:440
  38.2 12.0 %copy-start.6 = (bf16[256,768]{1,0:T(8,128)(2,1)S(1)}, bf16[256,768]{1,0:T(8,128)(2,1)}, u32[]{:S(2)}) copy-start(bf16[256,768]{1,0:T(8,128)(2,1)} %constant.53.clone.refs_14_) | copy-start | bytes 1179652
  59.7 8.1 %collective-permute-start.7 = (bf16[144,512]{1,0:T(8,128)(2,1)S(1)}, bf16[144,512]{1,0:T(8,128)(2,1)S(1)}, u32[]{:S(2)}, u32[]{:S(2)}) collective-permute-start(bf16[144,512]{1,0:T(8,128)(2,1)S(1)} %get-tuple-element.47), channel_id=1, source_target_pairs={{0,8},{4,12},{8,0},{12,4},{16,24},{20,28},{24,16},{28,20},{1,9},{5... | collective-permute-start | bytes 442376 | tf_op jit(solution)/shard_map/ppermute | solution.py:449
  63.7 7.7 %collective-permute-start.8 = (bf16[144,512]{1,0:T(8,128)(2,1)S(1)}, bf16[144,512]{1,0:T(8,128)(2,1)S(1)}, u32[]{:S(2)}, u32[]{:S(2)}) collective-permute-start(bf16[144,512]{1,0:T(8,128)(2,1)S(1)} %get-tuple-element.48), channel_id=1, source_target_pairs={{0,16},{4,20},{8,24},{12,28},{16,0},{20,4},{24,8},{28,12},{1,17},{... | collective-permute-start | bytes 442376 | tf_op jit(solution)/shard_map/ppermute | solution.py:449
  65.2 6.2 %collective-permute-start.9 = (bf16[144,512]{1,0:T(8,128)(2,1)S(1)}, bf16[144,512]{1,0:T(8,128)(2,1)S(1)}, u32[]{:S(2)}, u32[]{:S(2)}) collective-permute-start(bf16[144,512]{1,0:T(8,128)(2,1)S(1)} %get-tuple-element.49), channel_id=1, source_target_pairs={{0,24},{4,28},{8,16},{12,20},{16,8},{20,12},{24,0},{28,4},{1,25},{... | collective-permute-start | bytes 442376 | tf_op jit(solution)/shard_map/ppermute | solution.py:449
  66.1 7.1 %collective-permute-start.11 = (bf16[144,2048]{1,0:T(8,128)(2,1)S(1)}, bf16[144,2048]{1,0:T(8,128)(2,1)S(1)}, u32[]{:S(2)}, u32[]{:S(2)}) collective-permute-start(bf16[144,2048]{1,0:T(8,128)(2,1)S(1)} %get-tuple-element.50), channel_id=1, source_target_pairs={{4,0},{8,4},{12,8},{16,12},{20,16},{24,20},{28,24},{5,1},{9,5},{13... | collective-permute-start | bytes 1769480 | tf_op jit(solution)/shard_map/ppermute | solution.py:440
  71.5 1.6 %collective-permute-start.10 = (f32[144,512]{1,0:T(8,128)S(1)}, f32[144,512]{1,0:T(8,128)S(1)}, u32[]{:S(2)}, u32[]{:S(2)}) collective-permute-start(f32[144,512]{1,0:T(8,128)S(1)} %add_add_fusion), channel_id=1, source_target_pairs={{0,4},{4,0},{8,12},{12,8},{16,20},{20,16},{24,28},{28,24},{1,5},{5... | collective-permute-start | bytes 884744 | tf_op jit(solution)/shard_map/ppermute | solution.py:449
  73.2 7.6 %collective-permute-start.14 = (bf16[144,512]{1,0:T(8,128)(2,1)S(1)}, bf16[144,512]{1,0:T(8,128)(2,1)S(1)}, u32[]{:S(2)}, u32[]{:S(2)}) collective-permute-start(bf16[144,512]{1,0:T(8,128)(2,1)S(1)} %add.54.refs_0_), channel_id=1, source_target_pairs={{0,24},{4,28},{8,16},{12,20},{16,8},{20,12},{24,0},{28,4},{1,25},{... | collective-permute-start | bytes 442376 | tf_op jit(solution)/shard_map/ppermute | solution.py:449
  77.4 7.8 %collective-permute-start.13 = (bf16[144,512]{1,0:T(8,128)(2,1)S(1)}, bf16[144,512]{1,0:T(8,128)(2,1)S(1)}, u32[]{:S(2)}, u32[]{:S(2)}) collective-permute-start(bf16[144,512]{1,0:T(8,128)(2,1)S(1)} %add.54.refs_0_), channel_id=1, source_target_pairs={{0,16},{4,20},{8,24},{12,28},{16,0},{20,4},{24,8},{28,12},{1,17},{... | collective-permute-start | bytes 442376 | tf_op jit(solution)/shard_map/ppermute | solution.py:449
  78.0 8.7 %collective-permute-start.12 = (bf16[144,512]{1,0:T(8,128)(2,1)S(1)}, bf16[144,512]{1,0:T(8,128)(2,1)S(1)}, u32[]{:S(2)}, u32[]{:S(2)}) collective-permute-start(bf16[144,512]{1,0:T(8,128)(2,1)S(1)} %add.54.refs_0_), channel_id=1, source_target_pairs={{0,8},{4,12},{8,0},{12,4},{16,24},{20,28},{24,16},{28,20},{1,9},{5... | collective-permute-start | bytes 442376 | tf_op jit(solution)/shard_map/ppermute | solution.py:449
